TPU v7x, 32 devices: a whole 2x2x4 slice. The times are simulated.
32 devices in a mesh: dp: 8 (over y, x, core), mp: 4 (over z).
Axes of the slice: x: 2, y: 2, z: 4, core: 2. Of those that a mesh axis runs over, the one named last changes fastest.
Arguments:
- tokens: bfloat16 [6144, 768], P(('dp', 'mp')), may hold values from -6 to 6
- cotangent: bfloat16 [6144, 768], P(('dp', 'mp')), may hold values from -6 to 6
- lengths: int32 [8, 4], P('dp'), may hold values from 1 to 512, 768 in all within a row
- routes: int32 [6144], P(('dp', 'mp')), may hold values from 0 to 7, as said below
- slot_place: int32 [6144], P(('dp', 'mp')), may hold values from 0 to 29, as said below
- norm_in: float32 [2, 768], replicated, may hold values from 0.5 to 1.5
- w_in: bfloat16 [2, 2, 768, 1536], P(None, None, None, 'mp'), may hold values from -0.21875 to 0.21875
- conv_w: float32 [2, 4, 1536], P(None, None, 'mp'), may hold values from -3 to 3
- conv_b: float32 [2, 1536], P(None, 'mp'), may hold values from -3 to 3
- x_proj: bfloat16 [2, 1536, 80], P(None, 'mp'), may hold values from -0.15625 to 0.15625
- dt_proj: bfloat16 [2, 48, 1536], P(None, None, 'mp'), may hold values from -0.875 to 0.875
- dt_bias: float32 [2, 1536], P(None, 'mp'), may hold values from -4 to 2
- a_log: float32 [2, 16, 1536], P(None, None, 'mp'), may hold values from 0 to 2.77
- d_skip: float32 [2, 1536], P(None, 'mp'), may hold values from 0.5 to 1.5
- w_out: bfloat16 [2, 1536, 768], P(None, 'mp'), may hold values from -0.3125 to 0.3125
- norm_moe: float32 [2, 768], replicated, may hold values from 0.5 to 1.5
- router: float32 [2, 768, 8], replicated, may hold values from -0.15625 to 0.15625
- w_up: bfloat16 [2, 8, 768, 3072], P(None, 'dp', None, 'mp'), may hold values from -0.21875 to 0.21875
- w_down: bfloat16 [2, 8, 3072, 768], P(None, 'dp', 'mp'), may hold values from -0.875 to 0.875
Outputs:
- result: float32 [6144, 768], P(('dp', 'mp'))
- d_tokens: float32 [6144, 768], P(('dp', 'mp'))
- d_norm_in: float32 [2, 768], replicated
- d_w_in: float32 [2, 2, 768, 1536], P(None, None, None, 'mp')
- d_conv_w: float32 [2, 4, 1536], P(None, None, 'mp')
- d_conv_b: float32 [2, 1536], P(None, 'mp')
- d_x_proj: float32 [2, 1536, 80], P(None, 'mp')
- d_dt_proj: float32 [2, 48, 1536], P(None, None, 'mp')
- d_dt_bias: float32 [2, 1536], P(None, 'mp')
- d_a_log: float32 [2, 16, 1536], P(None, None, 'mp')
- d_d_skip: float32 [2, 1536], P(None, 'mp')
- d_w_out: float32 [2, 1536, 768], P(None, 'mp')
- d_norm_moe: float32 [2, 768], replicated
- d_router: float32 [2, 768, 8], replicated
- d_w_up: float32 [2, 8, 768, 3072], P(None, 'dp', None, 'mp')
- d_w_down: float32 [2, 8, 3072, 768], P(None, 'dp', 'mp')
Inputs may be any that keep to these rules, and one draw needn't show every extreme that they name: `routes`: in each aligned block of 192 rows (the rows of one device) no expert is named more than 30 times, and one expert, the same in every block, exactly 30 times. `slot_place`: among the tokens of one block of 192 rows with one expert, the slots are 0, 1, 2, ... each once. `lengths`: each row sums to 768.
All inputs are finite; a program needn't handle non-finite values.
Results may differ from a plain program's by a relative error of at most 0.03.
Values may be sent and summed in bfloat16 or wider, within the bound.
A program may use at most 192 MiB of HBM per device.

v0:
```python
import jax
import jax.numpy as jnp
from jax import lax
from jax.sharding import PartitionSpec as P

STATE = 16
DT_RANK = 48
CONV = 4
SCAN_LEN = 64


highest = lax.Precision.HIGHEST
epsilon = 1e-05
dt_most = 0.05


def rms_scale(values, gain):
    return values * lax.rsqrt(jnp.mean(values * values, axis=-1, keepdims=True) + epsilon) * gain


def row_layout(seq_lengths, row_total):
    seq_ends = jnp.cumsum(seq_lengths)
    seq_starts = seq_ends - seq_lengths
    position = jnp.arange(row_total, dtype=jnp.int32)
    segment = jnp.sum((position[:, None] >= seq_ends[None, :]).astype(jnp.int32), axis=1)
    restart = jnp.any(position[:, None] == seq_starts[None, :], axis=1)
    return (segment, restart)


def causal_conv(conv_in, taps, bias, segment):
    summed_taps = bias[None, :] + taps[CONV - 1][None, :] * conv_in
    for offset in range(1, CONV):
        shifted = jnp.concatenate(
            [jnp.zeros((offset, conv_in.shape[1]), conv_in.dtype), conv_in[:-offset]], axis=0
        )
        seg_shift = jnp.concatenate([jnp.full((offset,), -1, jnp.int32), segment[:-offset]])
        usable = (seg_shift == segment).astype(conv_in.dtype)
        summed_taps = summed_taps + taps[CONV - 1 - offset][None, :] * shifted * usable[:, None]
    return jax.nn.silu(summed_taps)


def front_piece(conv_in, taps, bias, weight_proj, segment):
    conv_out = causal_conv(conv_in, taps, bias, segment)
    return (conv_out, jnp.dot(conv_out, weight_proj, precision=highest))


def scan_block(carried, block_in, decay_rate):
    step_size, drive_in, in_mat, out_mat, restart, skipped = block_in
    block_len = step_size.shape[0]
    lower = (
        jnp.arange(block_len, dtype=jnp.int32)[:, None]
        >= jnp.arange(block_len, dtype=jnp.int32)[None, :]
    ).astype(step_size.dtype)
    cum_step = jnp.dot(lower, step_size, precision=highest)
    log_decay = decay_rate[None] * cum_step[:, None, :]
    count_reset = jnp.dot(lower, restart, precision=highest)
    joined = lower * (count_reset[:, None] == count_reset[None, :]).astype(step_size.dtype)
    drive = drive_in[:, None, :] * in_mat[:, :, None]
    weighted = jnp.dot(
        joined, (jnp.exp(-log_decay) * drive).reshape(block_len, -1), precision=highest
    ).reshape(log_decay.shape)
    fresh = (count_reset == 0).astype(step_size.dtype)
    states = jnp.exp(log_decay) * (weighted + fresh[:, None, None] * carried[None])
    outputs = jnp.einsum("cn,cne->ce", out_mat, states, precision=highest) + skipped
    return (states[-1], outputs)


def selective(conv_out, gate_in, projected, dt_weight, dt_shift, log_rate, skip, restart):
    row_total, channels = conv_out.shape
    dt_low = projected[:, :DT_RANK]
    in_mat = projected[:, DT_RANK : DT_RANK + STATE]
    out_mat = projected[:, DT_RANK + STATE :]
    step_size = dt_most * jax.nn.sigmoid(jnp.dot(dt_low, dt_weight, precision=highest) + dt_shift)
    decay_rate = -jnp.exp(log_rate)
    blocks = row_total // SCAN_LEN

    def into_blocks(values):
        return values.reshape((blocks, SCAN_LEN) + values.shape[1:])

    def block_step(carried, block_in):
        return scan_block(carried, block_in, decay_rate)

    _, outputs = lax.scan(
        jax.checkpoint(block_step),
        jnp.zeros((STATE, channels), conv_out.dtype),
        (
            into_blocks(step_size),
            into_blocks(step_size * conv_out),
            into_blocks(in_mat),
            into_blocks(out_mat),
            into_blocks(restart),
            into_blocks(skip[None, :] * conv_out),
        ),
    )
    return outputs.reshape(row_total, channels) * jax.nn.silu(gate_in)


def gather_rows(values):
    return lax.all_gather(values, "mp", axis=0, tiled=True)


def scatter_rows(term_fn, row_count):
    return lax.psum_scatter(
        term_fn(jnp.int32(0), row_count * lax.axis_size("mp")).astype(jnp.bfloat16),
        "mp",
        scatter_dimension=0,
        tiled=True,
    ).astype(jnp.float32)


def sum_over_channels(values):
    return lax.psum(values.astype(jnp.bfloat16), "mp").astype(jnp.float32)


def to_experts(buffer):
    capacity = buffer.shape[1]
    model_width = buffer.shape[2]
    mp_lanes = lax.axis_size("mp")
    copies = jnp.broadcast_to(
        buffer[:, None], (buffer.shape[0], mp_lanes, capacity, model_width)
    ).reshape(-1, capacity, model_width)
    arrived = lax.all_to_all(copies, ("dp", "mp"), split_axis=0, concat_axis=0, tiled=True)
    return arrived.reshape(-1, mp_lanes * capacity, model_width)


def from_experts(partial_out, mp_lanes):
    model_width = partial_out.shape[2]
    capacity = partial_out.shape[1] // mp_lanes
    arrived = lax.all_to_all(
        partial_out.reshape(-1, capacity, model_width).astype(jnp.bfloat16),
        ("dp", "mp"),
        split_axis=0,
        concat_axis=0,
        tiled=True,
    ).astype(jnp.float32)
    return jnp.sum(arrived.reshape(-1, mp_lanes, capacity, model_width), axis=1).astype(
        jnp.bfloat16
    )


def on_device(
    tokens,
    cotangent,
    lengths,
    routes,
    slot_place,
    norm_in,
    w_in,
    conv_w,
    conv_b,
    x_proj,
    dt_proj,
    dt_bias,
    a_log,
    d_skip,
    w_out,
    norm_moe,
    router,
    w_up,
    w_down,
):
    layers = norm_in.shape[0]
    rows_here, model_width = tokens.shape
    mp_lanes = lax.axis_size("mp")
    row_total = rows_here * mp_lanes
    experts = router.shape[2]
    capacity = max(2, (5 * rows_here + 4 * experts - 1) // (4 * experts))
    segment, restart_flag = row_layout(lengths[0], row_total)
    restart = restart_flag.astype(jnp.float32)
    choose = (routes[:, None] == jnp.arange(experts, dtype=jnp.int32)[None, :]).astype(jnp.float32)
    activation = tokens.astype(jnp.float32)
    stored = []
    for layer_index in range(layers):
        normed, norm_pull = jax.vjp(rms_scale, activation, norm_in[layer_index])
        whole = gather_rows(normed.astype(jnp.bfloat16))
        paired = jnp.einsum(
            "td,kde->kte", whole, w_in[layer_index], preferred_element_type=jnp.float32
        )

        def front_local(conv_in, taps, bias, weight_proj):
            return front_piece(conv_in, taps, bias, weight_proj, segment)

        (conv_out, proj_part), front_pull = jax.vjp(
            front_local,
            paired[0],
            conv_w[layer_index],
            conv_b[layer_index],
            x_proj[layer_index].astype(jnp.float32),
        )
        projected = sum_over_channels(proj_part)

        def back_local(conv_in, gate_in, proj_in, dt_weight, dt_shift, log_rate, skip):
            return selective(
                conv_in, gate_in, proj_in, dt_weight, dt_shift, log_rate, skip, restart
            )

        gated, back_pull = jax.vjp(
            back_local,
            conv_out,
            paired[1],
            projected,
            dt_proj[layer_index].astype(jnp.float32),
            dt_bias[layer_index],
            a_log[layer_index],
            d_skip[layer_index],
        )
        gated_low = gated.astype(jnp.bfloat16)
        weight_out = w_out[layer_index]

        def out_term(start, count):
            return jnp.dot(gated_low, weight_out, preferred_element_type=jnp.float32)

        mixed = scatter_rows(out_term, rows_here)
        middle = activation + mixed

        def route_piece(values, gain, table):
            normed_moe = rms_scale(values, gain)
            chance = jax.nn.softmax(jnp.dot(normed_moe, table, precision=highest), axis=-1)
            return (normed_moe, jnp.sum(chance * choose, axis=1))

        (normed_moe, gate_value), route_pull = jax.vjp(
            route_piece, middle, norm_moe[layer_index], router[layer_index]
        )
        buffer = (
            jnp.zeros((experts, capacity, model_width), jnp.bfloat16)
            .at[routes, slot_place]
            .set(normed_moe.astype(jnp.bfloat16))
        )
        arrived = to_experts(buffer)
        flat_in = arrived.reshape(-1, model_width)
        hidden = jnp.dot(flat_in, w_up[layer_index, 0], preferred_element_type=jnp.float32)
        active = jax.nn.gelu(hidden).astype(jnp.bfloat16)
        partial_out = jnp.dot(
            active, w_down[layer_index, 0], preferred_element_type=jnp.float32
        ).reshape(arrived.shape)
        returned = from_experts(partial_out, mp_lanes)
        picked = returned[routes, slot_place].astype(jnp.float32)
        stored.append(
            (
                norm_pull,
                whole,
                front_pull,
                back_pull,
                gated_low,
                route_pull,
                arrived,
                hidden,
                active,
                picked,
                gate_value,
            )
        )
        activation = middle + gate_value[:, None] * picked
    upstream = cotangent.astype(jnp.float32)
    collected = []
    for layer_index in reversed(range(layers)):
        (
            norm_pull,
            whole,
            front_pull,
            back_pull,
            gated_low,
            route_pull,
            arrived,
            hidden,
            active,
            picked,
            gate_value,
        ) = stored[layer_index]
        slot_grad = (
            jnp.zeros((experts, capacity, model_width), jnp.bfloat16)
            .at[routes, slot_place]
            .set((gate_value[:, None] * upstream).astype(jnp.bfloat16))
        )
        grad_arrived = to_experts(slot_grad).reshape(-1, model_width)
        flat_in = arrived.reshape(-1, model_width)
        grad_down = jnp.einsum(
            "rf,rd->fd", active, grad_arrived, preferred_element_type=jnp.float32
        )
        grad_active = jnp.einsum(
            "rd,fd->rf", grad_arrived, w_down[layer_index, 0], preferred_element_type=jnp.float32
        )
        _, gelu_pull = jax.vjp(jax.nn.gelu, hidden)
        grad_hidden = gelu_pull(grad_active)[0].astype(jnp.bfloat16)
        grad_up = jnp.einsum("rd,rf->df", flat_in, grad_hidden, preferred_element_type=jnp.float32)
        grad_part = jnp.einsum(
            "rf,df->rd", grad_hidden, w_up[layer_index, 0], preferred_element_type=jnp.float32
        ).reshape(arrived.shape)
        grad_slots = from_experts(grad_part, mp_lanes)
        grad_normed_moe = grad_slots[routes, slot_place].astype(jnp.float32)
        grad_gate = jnp.sum(upstream * picked, axis=1)
        grad_middle, grad_norm_moe, grad_router = route_pull((grad_normed_moe, grad_gate))
        grad_middle = grad_middle + upstream
        grad_whole = gather_rows(grad_middle.astype(jnp.bfloat16))
        grad_w_out = jnp.einsum(
            "te,td->ed", gated_low, grad_whole, preferred_element_type=jnp.float32
        )
        grad_gated = jnp.einsum(
            "td,ed->te", grad_whole, w_out[layer_index], preferred_element_type=jnp.float32
        )
        (
            grad_conv,
            grad_gate_in,
            grad_proj_part,
            grad_dt_weight,
            grad_dt_shift,
            grad_log_rate,
            grad_skip,
        ) = back_pull(grad_gated)
        grad_projected = sum_over_channels(grad_proj_part)
        grad_conv_in, grad_taps, grad_bias, grad_weight_proj = front_pull(
            (grad_conv, grad_projected)
        )
        grad_paired = jnp.stack([grad_conv_in, grad_gate_in]).astype(jnp.bfloat16)
        grad_w_in = jnp.einsum(
            "td,kte->kde", whole, grad_paired, preferred_element_type=jnp.float32
        )
        weight_in = w_in[layer_index]

        def in_term(start, count):
            return jnp.einsum(
                "kte,kde->td", grad_paired, weight_in, preferred_element_type=jnp.float32
            )

        grad_normed = scatter_rows(in_term, rows_here)
        grad_activation, grad_norm_in = norm_pull(grad_normed)
        upstream = grad_activation + grad_middle
        summed = (
            lax.psum(grad_w_in.astype(jnp.bfloat16), "dp").astype(jnp.float32),
            lax.psum(grad_taps.astype(jnp.bfloat16), "dp").astype(jnp.float32),
            lax.psum(grad_bias.astype(jnp.bfloat16), "dp").astype(jnp.float32),
            lax.psum(grad_weight_proj.astype(jnp.bfloat16), "dp").astype(jnp.float32),
            lax.psum(grad_dt_weight.astype(jnp.bfloat16), "dp").astype(jnp.float32),
            lax.psum(grad_dt_shift.astype(jnp.bfloat16), "dp").astype(jnp.float32),
            lax.psum(grad_log_rate.astype(jnp.bfloat16), "dp").astype(jnp.float32),
            lax.psum(grad_skip.astype(jnp.bfloat16), "dp").astype(jnp.float32),
            lax.psum(grad_w_out.astype(jnp.bfloat16), "dp").astype(jnp.float32),
        )
        shared = lax.psum((grad_norm_in, grad_norm_moe, grad_router), ("dp", "mp"))
        collected.append((summed, shared, grad_up, grad_down))
    collected = collected[::-1]

    def stacked(first, second):
        return jnp.stack([entry[first][second] for entry in collected])

    d_w_up = jnp.stack([entry[2][None] for entry in collected])
    d_w_down = jnp.stack([entry[3][None] for entry in collected])
    return (
        activation,
        upstream,
        stacked(1, 0),
        stacked(0, 0),
        stacked(0, 1),
        stacked(0, 2),
        stacked(0, 3),
        stacked(0, 4),
        stacked(0, 5),
        stacked(0, 6),
        stacked(0, 7),
        stacked(0, 8),
        stacked(1, 1),
        stacked(1, 2),
        d_w_up,
        d_w_down,
    )


def solution(mesh):
    return jax.shard_map(
        on_device,
        mesh=mesh,
        in_specs=(
            P(("dp", "mp"), None),
            P(("dp", "mp"), None),
            P("dp", None),
            P(("dp", "mp")),
            P(("dp", "mp")),
            P(),
            P(None, None, None, "mp"),
            P(None, None, "mp"),
            P(None, "mp"),
            P(None, "mp", None),
            P(None, None, "mp"),
            P(None, "mp"),
            P(None, None, "mp"),
            P(None, "mp"),
            P(None, "mp", None),
            P(),
            P(),
            P(None, "dp", None, "mp"),
            P(None, "dp", "mp", None),
        ),
        out_specs=(
            P(("dp", "mp"), None),
            P(("dp", "mp"), None),
            P(),
            P(None, None, None, "mp"),
            P(None, None, "mp"),
            P(None, "mp"),
            P(None, "mp", None),
            P(None, None, "mp"),
            P(None, "mp"),
            P(None, None, "mp"),
            P(None, "mp"),
            P(None, "mp", None),
            P(),
            P(),
            P(None, "dp", None, "mp"),
            P(None, "dp", "mp", None),
        ),
        check_vma=False,
    )
```

profile of v0, /device:TPU:0, one launch (start us, length us, event | category | flops | bytes accessed | tf_op | source)
XLA Modules:
  0.0 1920.4 jit_solution(12066129660462896150)
XLA Ops:
  14.5 30.4 %all-gather.5.cloned.1.call-done = bf16[768,768]{1,0:T(8,128)(2,1)} async-done(((bf16[192,768]{1,0:T(8,128)(2,1)}), bf16[768,768]{1,0:T(8,128)(2,1)}) %all-gather.5.cloned.1.call-update) | async-done | bytes 1179664 | tf_op jit(solution)/shard_map/all_gather | solution.py:99
  60.0 26.5 %all-reduce.40.cloned.1.call-done = bf16[768,80]{0,1:T(8,128)(2,1)} async-done(((bf16[768,80]{0,1:T(8,128)(2,1)}), bf16[768,80]{0,1:T(8,128)(2,1)}) %all-reduce.40.cloned.1.call-update) | async-done | bytes 122896 | tf_op jit(solution)/shard_map/psum | solution.py:112
  93.4 135.3 %while.90 = (s32[]{:T(128)}, f32[16,384]{1,0:T(8,128)S(1)}, f32[12,64,384]{2,1,0:T(8,128)}, f32[12,16,384]{2,1,0:T(8,128)S(1)}, f32[1,16,384]{2,1,0:T(8,128)S(1)...) while((s32[]{:T(128)}, f32[16,384]{1,0:T(8,128)S(1)}, ...), condition=%wide.wide.region_6.7_spmd.clone.clone, body=%wide.wide.region_5.6_spmd.clone.clone.sunk | while | flops 328835200 | bytes 20221068 | solution.py:83
  233.0 28.6 %reduce-scatter.5.cloned.1.call-done = bf16[192,768]{1,0:T(8,128)(2,1)} async-done(((bf16[768,768]{1,0:T(8,128)(2,1)}), bf16[192,768]{1,0:T(8,128)(2,1)}) %reduce-scatter.5.cloned.1.call-update) | async-done | bytes 294928 | tf_op jit(solution)/shard_map/reduce_scatter | solution.py:103
  263.9 11.3 scatter_fusion
  275.5 40.2 %all_to_all.40 = bf16[32,30,768]{2,1,0:T(8,128)(2,1)S(1)} all-to-all(bf16[32,30,768]{2,1,0:T(8,128)(2,1)S(1)} %bitcast.895), channel_id=1, replica_groups=mesh['dp'=8,'mp'=4] {'dp','mp'}, dimensions={0} | all-to-all | bytes 2949120 | tf_op jit(solution)/shard_map/all_to_all | solution.py:122
  317.1 5.4 multiply_convert_fusion.1
  330.0 4.1 all-to-all-start.1
  334.9 35.1 %all-to-all-done.1 = bf16[32,30,768]{2,1,0:T(8,128)(2,1)S(1)} async-done(((bf16[32,30,768]{2,1,0:T(8,128)(2,1)}), bf16[32,30,768]{2,1,0:T(8,128)(2,1)S(1)}, u32[]{:S(2)}, u32[]{:S(2)}) %all-to-all-start.1) | async-done | bytes 1474592 | tf_op jit(solution)/shard_map/all_to_all | solution.py:129
  374.8 30.5 %all-gather.7.cloned.1.call-done = bf16[768,768]{1,0:T(8,128)(2,1)} async-done(((bf16[192,768]{1,0:T(8,128)(2,1)}), bf16[768,768]{1,0:T(8,128)(2,1)}) %all-gather.7.cloned.1.call-update) | async-done | bytes 1179664 | tf_op jit(solution)/shard_map/all_gather | solution.py:99
  415.2 32.8 %all-reduce.42.cloned.1.call-done = bf16[768,80]{0,1:T(8,128)(2,1)} async-done(((bf16[768,80]{0,1:T(8,128)(2,1)}), bf16[768,80]{0,1:T(8,128)(2,1)}) %all-reduce.42.cloned.1.call-update) | async-done | bytes 122896 | tf_op jit(solution)/shard_map/psum | solution.py:112
  449.6 3.9 fusion.328
  454.7 126.8 %while.91 = (s32[]{:T(128)}, f32[16,384]{1,0:T(8,128)S(1)}, f32[12,64,384]{2,1,0:T(8,128)}, f32[12,16,384]{2,1,0:T(8,128)S(1)}, f32[1,16,384]{2,1,0:T(8,128)S(1)...) while((s32[]{:T(128)}, f32[16,384]{1,0:T(8,128)S(1)}, ...), condition=%wide.wide.region_17.18_spmd.clone.clone, body=%wide.wide.region_16.17_spmd.clone.clone.sunk | while | flops 328835200 | bytes 20221068 | solution.py:83
  585.1 29.3 %reduce-scatter.7.cloned.1.call-done = bf16[192,768]{1,0:T(8,128)(2,1)} async-done(((bf16[768,768]{1,0:T(8,128)(2,1)}), bf16[192,768]{1,0:T(8,128)(2,1)}) %reduce-scatter.7.cloned.1.call-update) | async-done | bytes 294928 | tf_op jit(solution)/shard_map/reduce_scatter | solution.py:103
  615.8 11.3 scatter_fusion.1
  627.4 40.2 %all_to_all.41 = bf16[32,30,768]{2,1,0:T(8,128)(2,1)S(1)} all-to-all(bf16[32,30,768]{2,1,0:T(8,128)(2,1)S(1)} %bitcast.896), channel_id=1, replica_groups=mesh['dp'=8,'mp'=4] {'dp','mp'}, dimensions={0} | all-to-all | bytes 2949120 | tf_op jit(solution)/shard_map/all_to_all | solution.py:122
  668.9 5.4 multiply_convert_fusion
  681.9 4.1 all-to-all-start.3
  686.7 35.2 %all-to-all-done.3 = bf16[32,30,768]{2,1,0:T(8,128)(2,1)S(1)} async-done(((bf16[32,30,768]{2,1,0:T(8,128)(2,1)}), bf16[32,30,768]{2,1,0:T(8,128)(2,1)S(1)}, u32[]{:S(2)}, u32[]{:S(2)}) %all-to-all-start.3) | async-done | bytes 1474592 | tf_op jit(solution)/shard_map/all_to_all | solution.py:129
  725.7 11.3 scatter_fusion.2
  737.3 41.5 %all_to_all.42 = bf16[32,30,768]{2,1,0:T(8,128)(2,1)S(1)} all-to-all(bf16[32,30,768]{2,1,0:T(8,128)(2,1)S(1)} %bitcast.897), channel_id=1, replica_groups=mesh['dp'=8,'mp'=4] {'dp','mp'}, dimensions={0} | all-to-all | bytes 2949120 | tf_op jit(solution)/shard_map/all_to_all | solution.py:122
  780.1 6.5 fusion.131
  794.1 4.1 all-to-all-start.5
  798.2 35.9 %all-to-all-done.5 = bf16[32,30,768]{2,1,0:T(8,128)(2,1)S(1)} async-done(((bf16[32,30,768]{2,1,0:T(8,128)(2,1)}), bf16[32,30,768]{2,1,0:T(8,128)(2,1)S(1)}, u32[]{:S(2)}, u32[]{:S(2)}) %all-to-all-start.5) | async-done | bytes 1474592 | tf_op jit(solution)/shard_map/all_to_all | solution.py:129
  834.6 3.9 gather_fusion.2
  843.9 29.5 %all-gather.9.cloned.1.call-done = bf16[768,768]{1,0:T(8,128)(2,1)} async-done(((bf16[192,768]{1,0:T(8,128)(2,1)}), bf16[768,768]{1,0:T(8,128)(2,1)}) %all-gather.9.cloned.1.call-update) | async-done | bytes 1179664 | tf_op jit(solution)/shard_map/all_gather | solution.py:99
  873.4 4.3 fusion.171
  882.5 267.4 %while.88 = (s32[]{:T(128)}, f32[16,384]{1,0:T(8,128)S(1)}, f32[16,384]{1,0:T(8,128)S(1)}, f32[12,64,384]{2,1,0:T(8,128)}, f32[12,64,384]{2,1,0:T(8,128)}, /*ind...) while((s32[]{:T(128)}, f32[16,384]{1,0:T(8,128)S(1)}, ...), condition=%wide.region_36.37_spmd.clone, body=%wide.region_30.36_spmd.clone.sunk | while | flops 661433472 | bytes 30051904 | solution.py:83
  1149.9 4.4 fusion.338
  1156.3 33.1 %all-reduce.44.cloned.1.call-done = bf16[768,80]{0,1:T(8,128)(2,1)} async-done(((bf16[768,80]{0,1:T(8,128)(2,1)}), bf16[768,80]{0,1:T(8,128)(2,1)}) %all-reduce.44.cloned.1.call-update) | async-done | bytes 122896 | tf_op jit(solution)/shard_map/psum | solution.py:112
  1200.3 29.3 %reduce-scatter.9.cloned.1.call-done = bf16[192,768]{1,0:T(8,128)(2,1)} async-done(((bf16[768,768]{1,0:T(8,128)(2,1)}), bf16[192,768]{1,0:T(8,128)(2,1)}) %reduce-scatter.9.cloned.1.call-update) | async-done | bytes 294928 | tf_op jit(solution)/shard_map/reduce_scatter | solution.py:103
  1234.4 11.3 scatter_fusion.3
  1245.9 40.1 %all_to_all.43 = bf16[32,30,768]{2,1,0:T(8,128)(2,1)} all-to-all(bf16[32,30,768]{2,1,0:T(8,128)(2,1)S(1)} %bitcast.898), channel_id=1, replica_groups=mesh['dp'=8,'mp'=4] {'dp','mp'}, dimensions={0} | all-to-all | bytes 2949120 | tf_op jit(solution)/shard_map/all_to_all | solution.py:122
  1289.4 6.4 fusion.124
  1299.1 3.7 convolution_convert_fusion
  1304.7 4.2 all-to-all-start.7
  1309.3 35.6 %all-to-all-done.7 = bf16[32,30,768]{2,1,0:T(8,128)(2,1)} async-done(((bf16[32,30,768]{2,1,0:T(8,128)(2,1)}), bf16[32,30,768]{2,1,0:T(8,128)(2,1)}, u32[]{:S(2)}, u32[]{:S(2)}) %all-to-all-start.7) | async-done | bytes 1474592 | tf_op jit(solution)/shard_map/all_to_all | solution.py:129
  1363.5 20.3 %all-gather.11.cloned.1.call-done = bf16[768,768]{1,0:T(8,128)(2,1)} async-done(((bf16[192,768]{1,0:T(8,128)(2,1)}), bf16[768,768]{1,0:T(8,128)(2,1)}) %all-gather.11.cloned.1.call-update) | async-done | bytes 1179664 | tf_op jit(solution)/shard_map/all_gather | solution.py:99
  1383.8 3.9 fusion.164
  1392.6 259.9 %while.89 = (s32[]{:T(128)}, f32[16,384]{1,0:T(8,128)S(1)}, f32[16,384]{1,0:T(8,128)S(1)}, f32[12,64,384]{2,1,0:T(8,128)}, f32[12,64,384]{2,1,0:T(8,128)}, /*ind...) while((s32[]{:T(128)}, f32[16,384]{1,0:T(8,128)S(1)}, ...), condition=%wide.region_51.52_spmd.clone, body=%wide.region_45.51_spmd.clone.sunk | while | flops 661433472 | bytes 30035492 | solution.py:83
  1652.5 4.4 fusion.336
  1664.7 27.4 %all-reduce.46.cloned.1.call-done = bf16[768,80]{0,1:T(8,128)(2,1)} async-done(((bf16[768,80]{0,1:T(8,128)(2,1)}), bf16[768,80]{0,1:T(8,128)(2,1)}) %all-reduce.46.cloned.1.call-update) | async-done | bytes 122896 | tf_op jit(solution)/shard_map/psum | solution.py:112
  1726.2 31.6 %all-reduce.48.cloned.1.call-done = (bf16[1,4,384]{2,1,0:T(4,128)(2,1)}, bf16[1,4,384]{2,1,0:T(4,128)(2,1)}, bf16[1,384]{1,0:T(2,128)(2,1)}, bf16[1,384]{1,0:T(2...) async-done(((bf16[1,4,384]{2,1,0:T(4,128)(2,1)}, ...) | async-done | bytes 231952 | tf_op jit(solution)/shard_map/psum | solution.py:330
  1767.2 69.6 %all-reduce.50.cloned.1.call-done = (bf16[1,2,768,384]{2,3,1,0:T(8,128)(2,1)}, bf16[1,2,768,384]{2,3,1,0:T(8,128)(2,1)}, bf16[1,384,768]{2,1,0:T(8,128)(2,1)}, bf16[1,384,768]{2,1,0:T(8,128)(2,1)}) async-done(((bf16[1,2,768,384]{2,3,1,0:T(8,128)(2,1)}, bf16[1,2,768,384]{2,3,1,0:T(8,128)(2,1)}, bf16[1,384,768]{2,1,0:T(8,128)(2,1)}, bf16[1,384,768]{2,1,0:T(8,128)(2,1)}), (bf16[1,2,768,384]{2,3,1,0:T(8,128)(2,1)}, ...) | async-done | bytes 3538960 | tf_op jit(solution)/shard_map/psum | solution.py:329
  1836.8 4.1 maximum_convert_fusion
  1840.9 6.2 copy.243
  1848.7 19.7 %reduce-scatter.11.cloned.1.call-done = bf16[192,768]{1,0:T(8,128)(2,1)} async-done(((bf16[768,768]{1,0:T(8,128)(2,1)}), bf16[192,768]{1,0:T(8,128)(2,1)}) %reduce-scatter.11.cloned.1.call-update) | async-done | bytes 294928 | tf_op jit(solution)/shard_map/reduce_scatter | solution.py:103
  1869.7 40.0 %all-reduce.30 = (f32[1,768]{1,0:T(1,128)S(1)}, f32[1,768]{1,0:T(1,128)S(1)}, f32[1,768]{1,0:T(1,128)S(1)}, f32[1,768]{1,0:T(1,128)S(1)}, f32[1,768,8]{1,2,0:T(8,128)S(1)}, /*index=5*/f32[1,768,8]{1,2,0:T(8,128)S(1)}) all-reduce(f32[1,768]{1,0:T(1,128)S(1)} %stack.190, ...), channel_id=1, replica_groups=mesh['dp'=8,'mp'=4] {'dp','mp'}, use_global_device_ids=true, to_apply=%region_58.59 | all-reduce | flops 15360 | bytes 122880 | tf_op jit(solution)/shard_map/psum | solution.py:339
  (1800 shorter events, 992.0 us)
Async XLA Ops:
  7.2 37.7 %all-gather.5.cloned.1.call-start = ((), (), s32[]{:S(2)}) async-start(), calls=%async_computation.12 | async-start | bytes 1474560 | tf_op jit(solution)/shard_map/all_gather | solution.py:99
  8.1 365.7 %copy-start.106 = (f32[768]{0:T(1024)}, f32[768]{0:T(1024)S(1)}, u32[]{:S(2)}) copy-start(f32[768]{0:T(1024)S(1)} %get-tuple-element.1436) | copy-start | bytes 9220
  11.6 74.9 %all-reduce.40.cloned.1.call-start = ((), (), s32[]{:S(2)}) async-start(), calls=%async_computation.13 | async-start | bytes 245760 | tf_op jit(solution)/shard_map/psum | solution.py:112
  13.8 394.6 %copy-start.85 = (f32[768]{0:T(1024)}, f32[768]{0:T(1024)S(1)}, u32[]{:S(2)}) copy-start(f32[768]{0:T(1024)S(1)} %get-tuple-element.1653) | copy-start | bytes 9220
  13.8 394.6 %copy-start.88 = (f32[768]{0:T(1024)}, f32[768]{0:T(1024)S(1)}, u32[]{:S(2)}) copy-start(f32[768]{0:T(1024)S(1)} %get-tuple-element.1654) | copy-start | bytes 9220
  13.8 394.6 %copy-start.91 = (f32[768]{0:T(1024)}, f32[768]{0:T(1024)S(1)}, u32[]{:S(2)}) copy-start(f32[768]{0:T(1024)S(1)} %get-tuple-element.1655) | copy-start | bytes 9220
  51.5 37.3 %copy-start.15 = (f32[768,384]{1,0:T(8,128)}, f32[768,384]{1,0:T(8,128)S(1)}, u32[]{:S(2)}) copy-start(f32[768,384]{1,0:T(8,128)S(1)} %get-tuple-element.1601) | copy-start | bytes 3538948
  53.1 208.5 %reduce-scatter.5.cloned.1.call-start = ((), (), s32[]{:S(2)}) async-start(), calls=%async_computation.14 | async-start | bytes 1474560 | tf_op jit(solution)/shard_map/reduce_scatter | solution.py:103
  93.4 135.3 %slice-start = ((f32[2,768,384]{2,1,0:T(8,128)}), f32[1,768,384]{2,1,0:T(8,128)S(1)}, s32[]{:S(2)}) async-start(f32[2,768,384]{2,1,0:T(8,128)} %copy-done.3), calls=%async_computation.26 | async-start | bytes 2359296 | tf_op jit(solution)/shard_map/slice | solution.py:200
  233.0 101.2 %copy-start.103 = (f32[768]{0:T(1024)}, f32[768]{0:T(1024)S(1)}, u32[]{:S(2)}) copy-start(f32[768]{0:T(1024)S(1)} %get-tuple-element.1435) | copy-start | bytes 9220
  233.0 608.1 %copy-start.77 = (f32[768]{0:T(1024)}, f32[768]{0:T(1024)S(1)}, u32[]{:S(2)}) copy-start(f32[768]{0:T(1024)S(1)} %get-tuple-element.1434) | copy-start | bytes 9220
  262.8 71.4 %copy-start.142 = (f32[192]{0:T(256)}, f32[192]{0:T(256)S(1)}, u32[]{:S(2)}) copy-start(f32[192]{0:T(256)S(1)} %fusion.314) | copy-start | bytes 2308
  330.0 40.0 %all-to-all-start.1 = ((bf16[32,30,768]{2,1,0:T(8,128)(2,1)}), bf16[32,30,768]{2,1,0:T(8,128)(2,1)S(1)}, u32[]{:S(2)}, u32[]{:S(2)}) async-start(bf16[32,30,768]{2,1,0:T(8,128)(2,1)} %copy.217), calls=%async_computation.2 | async-start | bytes 3145728 | tf_op jit(solution)/shard_map/all_to_all | solution.py:129
  334.1 71.2 %all-gather.7.cloned.1.call-start = ((), (), s32[]{:S(2)}) async-start(), calls=%async_computation.15 | async-start | bytes 1474560 | tf_op jit(solution)/shard_map/all_gather | solution.py:99
  334.8 35.2 %copy-start.162 = (f32[192]{0:T(256)}, f32[192]{0:T(256)S(1)}, u32[]{:S(2)}) copy-start(f32[192]{0:T(256)S(1)} %get-tuple-element.1661) | copy-start | bytes 2308
  334.8 35.6 %copy-start.98 = (f32[192,8]{0,1:T(8,128)}, f32[192,8]{0,1:T(8,128)S(1)}, u32[]{:S(2)}) copy-start(f32[192,8]{0,1:T(8,128)S(1)} %get-tuple-element.1662) | copy-start | bytes 18436
  334.9 35.6 %copy-start.159 = (f32[192]{0:T(256)}, f32[192]{0:T(256)S(1)}, u32[]{:S(2)}) copy-start(f32[192]{0:T(256)S(1)} %fusion.305) | copy-start | bytes 2308
  334.9 38.6 %copy-start.168 = (f32[192]{0:T(256)}, f32[192]{0:T(256)S(1)}, u32[]{:S(2)}) copy-start(f32[192]{0:T(256)S(1)} %select_reduce_fusion.1) | copy-start | bytes 2308
  374.7 73.2 %all-reduce.42.cloned.1.call-start = ((), (), s32[]{:S(2)}) async-start(), calls=%async_computation.16 | async-start | bytes 245760 | tf_op jit(solution)/shard_map/psum | solution.py:112
  414.6 199.9 %reduce-scatter.7.cloned.1.call-start = ((), (), s32[]{:S(2)}) async-start(), calls=%async_computation.17 | async-start | bytes 1474560 | tf_op jit(solution)/shard_map/reduce_scatter | solution.py:103
  454.7 126.8 %slice-start.1 = ((f32[2,768,384]{2,1,0:T(8,128)}), f32[1,768,384]{2,1,0:T(8,128)S(1)}, s32[]{:S(2)}) async-start(f32[2,768,384]{2,1,0:T(8,128)} %copy-done.6), calls=%async_computation.27 | async-start | bytes 2359296 | tf_op jit(solution)/shard_map/slice | solution.py:200
  615.6 225.5 %copy-start = (f32[192,768]{1,0:T(8,128)}, f32[192,768]{1,0:T(8,128)S(1)}, u32[]{:S(2)}) copy-start(f32[192,768]{1,0:T(8,128)S(1)} %get-tuple-element.1595) | copy-start | bytes 1769476
  615.6 225.5 %copy-start.108 = (f32[192]{0:T(256)}, f32[192]{0:T(256)S(1)}, u32[]{:S(2)}) copy-start(f32[192]{0:T(256)S(1)} %fusion.316) | copy-start | bytes 2308
  681.9 40.0 %all-to-all-start.3 = ((bf16[32,30,768]{2,1,0:T(8,128)(2,1)}), bf16[32,30,768]{2,1,0:T(8,128)(2,1)S(1)}, u32[]{:S(2)}, u32[]{:S(2)}) async-start(bf16[32,30,768]{2,1,0:T(8,128)(2,1)} %copy.223), calls=%async_computation.5 | async-start | bytes 3145728 | tf_op jit(solution)/shard_map/all_to_all | solution.py:129
  686.6 151.8 %copy-start.75 = (f32[192,8]{0,1:T(8,128)}, f32[192,8]{0,1:T(8,128)S(1)}, u32[]{:S(2)}) copy-start(f32[192,8]{0,1:T(8,128)S(1)} %get-tuple-element.1665) | copy-start | bytes 18436
  686.6 151.8 %copy-start.117 = (f32[192]{0:T(256)}, f32[192]{0:T(256)S(1)}, u32[]{:S(2)}) copy-start(f32[192]{0:T(256)S(1)} %get-tuple-element.1664) | copy-start | bytes 2308
  686.7 151.8 %copy-start.118 = (f32[192]{0:T(256)}, f32[192]{0:T(256)S(1)}, u32[]{:S(2)}) copy-start(f32[192]{0:T(256)S(1)} %fusion.306) | copy-start | bytes 2308
  725.5 112.9 %copy-start.147 = (f32[192]{0:T(256)}, f32[192]{0:T(256)S(1)}, u32[]{:S(2)}) copy-start(f32[192]{0:T(256)S(1)} %fusion.228) | copy-start | bytes 2308
  794.1 40.0 %all-to-all-start.5 = ((bf16[32,30,768]{2,1,0:T(8,128)(2,1)}), bf16[32,30,768]{2,1,0:T(8,128)(2,1)S(1)}, u32[]{:S(2)}, u32[]{:S(2)}) async-start(bf16[32,30,768]{2,1,0:T(8,128)(2,1)} %copy.227), calls=%async_computation.7 | async-start | bytes 3145728 | tf_op jit(solution)/shard_map/all_to_all | solution.py:129
  798.1 75.3 %all-gather.9.cloned.1.call-start = ((), (), s32[]{:S(2)}) async-start(), calls=%async_computation.18 | async-start | bytes 1474560 | tf_op jit(solution)/shard_map/all_gather | solution.py:99
  798.2 40.2 %copy-start.165 = (f32[192]{0:T(256)}, f32[192]{0:T(256)S(1)}, u32[]{:S(2)}) copy-start(f32[192]{0:T(256)S(1)} %neg.125) | copy-start | bytes 2308
  841.1 36.7 %copy-start.151 = (f32[192]{0:T(256)}, f32[192]{0:T(256)S(1)}, u32[]{:S(2)}) copy-start(f32[192]{0:T(256)S(1)} %multiply_multiply_fusion.15) | copy-start | bytes 2308
  842.8 346.6 %all-reduce.44.cloned.1.call-start = ((), (), s32[]{:S(2)}) async-start(), calls=%async_computation.19 | async-start | bytes 245760 | tf_op jit(solution)/shard_map/psum | solution.py:112
  1154.4 35.0 %copy-start.18 = (f32[768,384]{1,0:T(8,128)S(1)}, f32[768,384]{1,0:T(8,128)}, u32[]{:S(2)}) copy-start(f32[768,384]{1,0:T(8,128)} %copy-done.17) | copy-start | bytes 3538948
  1154.4 35.0 %copy-start.84 = (bf16[2,384,80]{1,2,0:T(8,128)(2,1)S(1)}, bf16[2,384,80]{1,2,0:T(8,128)(2,1)}, u32[]{:S(2)}) copy-start(bf16[2,384,80]{1,2,0:T(8,128)(2,1)} %param.36) | copy-start | bytes 368644
  1156.1 73.6 %reduce-scatter.9.cloned.1.call-start = ((), (), s32[]{:S(2)}) async-start(), calls=%async_computation.20 | async-start | bytes 1474560 | tf_op jit(solution)/shard_map/reduce_scatter | solution.py:103
  1234.2 115.6 %copy-start.173 = (f32[192]{0:T(256)}, f32[192]{0:T(256)S(1)}, u32[]{:S(2)}) copy-start(f32[192]{0:T(256)S(1)} %get-tuple-element.1592) | copy-start | bytes 2308
  1234.2 117.2 %copy-start.27 = (f32[192,768]{1,0:T(8,128)}, f32[192,768]{1,0:T(8,128)S(1)}, u32[]{:S(2)}) copy-start(f32[192,768]{1,0:T(8,128)S(1)} %get-tuple-element.1593) | copy-start | bytes 1769476
  1304.7 40.1 %all-to-all-start.7 = ((bf16[32,30,768]{2,1,0:T(8,128)(2,1)}), bf16[32,30,768]{2,1,0:T(8,128)(2,1)}, u32[]{:S(2)}, u32[]{:S(2)}) async-start(bf16[32,30,768]{2,1,0:T(8,128)(2,1)} %copy.235), calls=%async_computation.10 | async-start | bytes 3145728 | tf_op jit(solution)/shard_map/all_to_all | solution.py:129
  1308.9 74.8 %all-gather.11.cloned.1.call-start = ((), (), s32[]{:S(2)}) async-start(), calls=%async_computation.21 | async-start | bytes 1474560 | tf_op jit(solution)/shard_map/all_gather | solution.py:99
  1309.3 40.5 %copy-start.180 = (f32[192]{0:T(256)}, f32[192]{0:T(256)S(1)}, u32[]{:S(2)}) copy-start(f32[192]{0:T(256)S(1)} %neg.128) | copy-start | bytes 2308
  1353.2 338.8 %all-reduce.46.cloned.1.call-start = ((), (), s32[]{:S(2)}) async-start(), calls=%async_computation.22 | async-start | bytes 245760 | tf_op jit(solution)/shard_map/psum | solution.py:112
  1658.7 99.1 %all-reduce.48.cloned.1.call-start = ((), (), s32[]{:S(2)}) async-start(), calls=%async_computation.24 | async-start | bytes 473088 | tf_op jit(solution)/shard_map/psum | solution.py:330
  1701.4 135.4 %all-reduce.50.cloned.1.call-start = ((), (), s32[]{:S(2)}) async-start(), calls=%async_computation.25 | async-start | bytes 7077888 | tf_op jit(solution)/shard_map/psum | solution.py:329
  1704.8 163.6 %reduce-scatter.11.cloned.1.call-start = ((), (), s32[]{:S(2)}) async-start(), calls=%async_computation.23 | async-start | bytes 1474560 | tf_op jit(solution)/shard_map/reduce_scatter | solution.py:103
  1847.1 64.4 %copy-start.40 = (f32[192,768]{1,0:T(8,128)S(1)}, f32[192,768]{1,0:T(8,128)}, u32[]{:S(2)}) copy-start(f32[192,768]{1,0:T(8,128)} %copy-done.39) | copy-start | bytes 1769476
  1847.1 64.4 %copy-start.150 = (f32[192]{0:T(256)S(1)}, f32[192]{0:T(256)}, u32[]{:S(2)}) copy-start(f32[192]{0:T(256)} %copy-done.149) | copy-start | bytes 2308
  1848.7 62.8 %copy-start.28 = (f32[192,768]{1,0:T(8,128)S(1)}, f32[192,768]{1,0:T(8,128)}, u32[]{:S(2)}) copy-start(f32[192,768]{1,0:T(8,128)} %copy-done.27) | copy-start | bytes 1769476
  (223 other events, 1372.5 us)
Sparse Core Ops, SparseCore 0:
  11.7 33.1 all-gather.4
  53.2 33.1 all-reduce.39
  232.4 29.1 reduce-scatter.4
  374.8 30.4 all-gather.6
  414.7 33.1 all-reduce.41
  585.3 29.1 reduce-scatter.6
  843.0 30.4 all-gather.8
  1156.2 33.1 all-reduce.43
  1200.4 29.1 reduce-scatter.8
  1353.3 30.4 all-gather.10
  1658.8 33.1 all-reduce.45
  1701.5 56.1 all-reduce.47
  1761.9 74.8 all-reduce.49
  1839.1 29.2 reduce-scatter.10
where the time goes:
time: 1940 us; the launch traced here: 1920 us
  waiting for transfers between devices  580 us (30%)
  local copies, waits for them, and re-layouts  494 us (25%)
  matrix products  447 us (23%)
  blocking collectives  202 us (10%)
  other arithmetic  157 us (8%)
    squeeze x216, local copies, waits for them, and re-layouts, selective(): lax.scan(jax.checkpoint(block_step), jnp.zeros((STATE, channels), conv_ou...  186 us
    all_to_all x4, blocking collectives, to_experts(): lax.all_to_all(copies, ('dp', 'mp'), split_axis=0, concat_axis=0, tiled=T...  162 us
    dot_general x72, matrix products, scan_block(): jnp.dot(joined, (jnp.exp(-log_decay) * drive).reshape(block_len, -1), pre...  143 us
    all_to_all x4, waiting for transfers between devices, from_experts(): lax.all_to_all(partial_out.reshape(-1, capacity, model_width).astype(jnp....  142 us
    psum x4, waiting for transfers between devices, sum_over_channels(): return lax.psum(values.astype(jnp.bfloat16), 'mp').astype(jnp.float32)  120 us
    dot_general x48, matrix products, scan_block(): jnp.einsum('cn,cne->ce', out_mat, states, precision=highest) + skipped  117 us
    all_gather x4, waiting for transfers between devices, gather_rows(): return lax.all_gather(values, 'mp', axis=0, tiled=True)  111 us
    reduce_scatter x4, waiting for transfers between devices, scatter_rows(): lax.psum_scatter(term_fn(jnp.int32(0), row_count * lax.axis_size('mp')).a...  107 us
  transfers between devices with their start and end apart: 18, of which 18 were waited for; matrix products, arithmetic and copies ran while one was open for 4% of the time, Pallas kernels for 0%

commit v1 on v0

v1 whole, which is shorter than its diff:
```python
import functools
import jax
import jax.numpy as jnp
from jax import lax
from jax.experimental import pallas as pl
from jax.experimental.pallas import tpu as pltpu
from jax.sharding import PartitionSpec as P

STATE = 16
DT_RANK = 48
LANES = 128
CHUNK = 128
LOG2E = 1.4426950408889634
RESET = 1.0e6
CONV = 4
dt_most = 0.05
epsilon = 1e-05
highest = lax.Precision.HIGHEST
F32, BF16 = jnp.float32, jnp.bfloat16


def sigmoid(v):
    return 1.0 / (1.0 + jnp.exp(-v))


def dot(a, b):
    return jnp.dot(a, b, preferred_element_type=F32)


def dot_nt(a, b):
    return lax.dot_general(a, b, (((1,), (1,)), ((), ())), preferred_element_type=F32)


def dot_tn(a, b):
    return lax.dot_general(a, b, (((0,), (0,)), ((), ())), preferred_element_type=F32)


def spread_matrix(first):
    rows = lax.broadcasted_iota(jnp.int32, (LANES, STATE * LANES), 0)
    cols = lax.broadcasted_iota(jnp.int32, (LANES, STATE * LANES), 1)
    return (rows == first + cols // LANES).astype(BF16)


def put(ref, value):
    for j in range(ref.shape[0]):
        ref[j] = value[:, j * LANES : (j + 1) * LANES]


def spread_rows(proj, spread, out_ref):
    wide = dot(proj, spread)
    for n in range(STATE):
        out_ref[pl.ds(n, CHUNK, stride=STATE), :] = wide[:, n * LANES : (n + 1) * LANES]


def scan_fwd_kernel(xs_ref, zg_ref, proj_ref, rst_ref, dtw_ref, dtb_ref, alog_ref, skip_ref, sb_ref, sc_ref,
                    gated_ref, ys_ref, hck_ref,
                    h_ref, dm_ref, dx_ref, bx_ref, cx_ref, yq_ref):
    groups = xs_ref.shape[1] // LANES

    @pl.when(pl.program_id(0) == 0)
    def _():
        h_ref[...] = jnp.zeros_like(h_ref)

    hck_ref[0] = h_ref[...]
    proj = proj_ref[...]
    xs = xs_ref[...]
    delta = dt_most * sigmoid(dot(proj, dtw_ref[...]) + dtb_ref[...])
    put(dm_ref, delta + RESET * rst_ref[...])
    put(dx_ref, delta * xs)
    spread_rows(proj, sb_ref[...], bx_ref)
    spread_rows(proj, sc_ref[...], cx_ref)
    rate = -LOG2E * jnp.exp(alog_ref[...])
    rates = [rate[:, j * LANES : (j + 1) * LANES] for j in range(groups)]

    def step(g, hs):
        hs = list(hs)
        t0 = pl.multiple_of(g * 8, 8)
        for i in range(8):
            t = t0 + i
            r0 = pl.multiple_of(t * STATE, STATE)
            b = bx_ref[pl.ds(r0, STATE), :]
            c = cx_ref[pl.ds(r0, STATE), :]
            q0 = pl.multiple_of(t * 8, 8)
            for j in range(groups):
                lanes = slice(j * LANES, (j + 1) * LANES)
                dec = jnp.exp2(dm_ref[j, pl.ds(t, 1), :] * rates[j])
                hs[j] = dec * hs[j] + dx_ref[j, pl.ds(t, 1), :] * b
                q = c * hs[j]
                yq_ref[j, pl.ds(q0, 8), :] = q[:8] + q[8:]
        return tuple(hs)

    hs = lax.fori_loop(0, CHUNK // 8, step, tuple(h_ref[:, j * LANES : (j + 1) * LANES] for j in range(groups)))
    for j in range(groups):
        h_ref[:, j * LANES : (j + 1) * LANES] = hs[j]
    zg = zg_ref[...]
    for j in range(groups):
        lanes = slice(j * LANES, (j + 1) * LANES)
        y = skip_ref[:, lanes] * xs[:, lanes]
        for k in range(8):
            y = y + yq_ref[j, pl.ds(k, CHUNK, stride=8), :]
        ys_ref[:, lanes] = y
        z = zg[:, lanes]
        gated_ref[:, lanes] = (y * z * sigmoid(z)).astype(BF16)


def scan_fwd(xs, zg, proj, restart, dtw, dtb, alog, skip, sb, sc):
    rows, ch = xs.shape
    steps = rows // CHUNK
    row = lambda w: pl.BlockSpec((CHUNK, w), lambda i: (i, 0))
    full = lambda s: pl.BlockSpec(s, lambda i: (0,) * len(s))
    return pl.pallas_call(
        scan_fwd_kernel,
        grid=(steps,),
        out_shape=[
            jax.ShapeDtypeStruct((rows, ch), BF16),
            jax.ShapeDtypeStruct((rows, ch), F32),
            jax.ShapeDtypeStruct((steps, STATE, ch), F32),
        ],
        in_specs=[row(ch), row(ch), row(LANES), row(1), full((LANES, ch)), full((1, ch)), full((STATE, ch)), full((1, ch)),
                  full((LANES, STATE * LANES)), full((LANES, STATE * LANES))],
        out_specs=[row(ch), row(ch), pl.BlockSpec((1, STATE, ch), lambda i: (i, 0, 0))],
        scratch_shapes=[
            pltpu.VMEM((STATE, ch), F32),
            pltpu.VMEM((ch // LANES, CHUNK, LANES), F32),
            pltpu.VMEM((ch // LANES, CHUNK, LANES), F32),
            pltpu.VMEM((CHUNK * STATE, LANES), F32),
            pltpu.VMEM((CHUNK * STATE, LANES), F32),
            pltpu.VMEM((ch // LANES, CHUNK * 8, LANES), F32),
        ],
        compiler_params=pltpu.CompilerParams(vmem_limit_bytes=48 << 20),
        name="scan_fwd",
    )(xs, zg, proj, restart, dtw, dtb, alog, skip, sb, sc)


def scan_bwd_kernel(xs_ref, zg_ref, proj_ref, rst_ref, ys_ref, gg_ref, hck_ref, dtw_ref, dtb_ref, alog_ref, skip_ref,
                    sb_ref, sc_ref,
                    gxs_ref, gzg_ref, gproj_ref, gdtw_ref, gdtb_ref, galog_ref, gskip_ref,
                    a_ref, dm_ref, dx_ref, dl_ref, gy_ref, bx_ref, cx_ref, h_ref, dec_ref, pq_ref, gq_ref, gb_ref, gc_ref):
    groups = xs_ref.shape[1] // LANES
    cols = [slice(j * LANES, (j + 1) * LANES) for j in range(groups)]

    @pl.when(pl.program_id(0) == 0)
    def _():
        a_ref[...] = jnp.zeros_like(a_ref)
        gdtw_ref[...] = jnp.zeros_like(gdtw_ref)
        gdtb_ref[...] = jnp.zeros_like(gdtb_ref)
        galog_ref[...] = jnp.zeros_like(galog_ref)
        gskip_ref[...] = jnp.zeros_like(gskip_ref)

    proj = proj_ref[...]
    xs = xs_ref[...]
    delta = dt_most * sigmoid(dot(proj, dtw_ref[...]) + dtb_ref[...])
    put(dl_ref, delta)
    put(dm_ref, delta + RESET * rst_ref[...])
    put(dx_ref, delta * xs)
    zg = zg_ref[...]
    sz = sigmoid(zg)
    gg = gg_ref[...]
    gy = gg * (zg * sz)
    put(gy_ref, gy)
    gzg_ref[...] = gg * ys_ref[...] * (sz * (1.0 + zg * (1.0 - sz)))
    gskip_ref[...] += jnp.sum(gy * xs, axis=0, keepdims=True)
    spread_rows(proj, sb_ref[...], bx_ref)
    spread_rows(proj, sc_ref[...], cx_ref)
    rate = -jnp.exp(alog_ref[...])
    rates2 = [LOG2E * rate[:, c] for c in cols]
    rates = [rate[:, c] for c in cols]

    for j in range(groups):
        h_ref[j, :STATE, :] = hck_ref[0][:, cols[j]]

    def again(g, hs):
        hs = list(hs)
        t0 = pl.multiple_of(g * 8, 8)
        for i in range(8):
            t = t0 + i
            r0 = pl.multiple_of(t * STATE, STATE)
            r1 = pl.multiple_of(t * STATE + STATE, STATE)
            b = bx_ref[pl.ds(r0, STATE), :]
            for j in range(groups):
                dec = jnp.exp2(dm_ref[j, pl.ds(t, 1), :] * rates2[j])
                hs[j] = dec * hs[j] + dx_ref[j, pl.ds(t, 1), :] * b
                dec_ref[j, pl.ds(r0, STATE), :] = dec
                h_ref[j, pl.ds(r1, STATE), :] = hs[j]
        return tuple(hs)

    last = lax.fori_loop(0, CHUNK // 8, again, tuple(hck_ref[0][:, c] for c in cols))

    def back(g, carry):
        carry = [list(c) for c in carry]
        aa, hs, acc = carry
        t0 = pl.multiple_of(CHUNK - 8 - g * 8, 8)
        for i in reversed(range(8)):
            t = t0 + i
            r0 = pl.multiple_of(t * STATE, STATE)
            q0 = pl.multiple_of(t * 8, 8)
            b = bx_ref[pl.ds(r0, STATE), :]
            c = cx_ref[pl.ds(r0, STATE), :]
            gb, gc = None, None
            for j in range(groups):
                gyj = gy_ref[j, pl.ds(t, 1), :]
                a = c * gyj + aa[j]
                dec = dec_ref[j, pl.ds(r0, STATE), :]
                before = h_ref[j, pl.ds(r0, STATE), :]
                carry_a = dec * a
                p = carry_a * before * rates[j]
                ab = a * b
                pq_ref[j, pl.ds(q0, 8), :] = p[:8] + p[8:]
                gq_ref[j, pl.ds(q0, 8), :] = ab[:8] + ab[8:]
                acc[j] = acc[j] + p * dl_ref[j, pl.ds(t, 1), :]
                gbj = a * dx_ref[j, pl.ds(t, 1), :]
                gcj = gyj * hs[j]
                gb = gbj if gb is None else gb + gbj
                gc = gcj if gc is None else gc + gcj
                aa[j] = carry_a
                hs[j] = before
            gb_ref[pl.ds(r0, STATE), :] = gb
            gc_ref[pl.ds(r0, STATE), :] = gc
        return tuple(tuple(c) for c in carry)

    aa, _, acc = lax.fori_loop(
        0, CHUNK // 8, back,
        (tuple(a_ref[:, c] for c in cols), last, tuple(jnp.zeros((STATE, LANES), F32) for _ in cols)))
    for j in range(groups):
        a_ref[:, cols[j]] = aa[j]
        galog_ref[:, cols[j]] += acc[j]

    skip = skip_ref[...]
    gdts = []
    for j in range(groups):
        psum = pq_ref[j, pl.ds(0, CHUNK, stride=8), :]
        gsum = gq_ref[j, pl.ds(0, CHUNK, stride=8), :]
        for k in range(1, 8):
            psum = psum + pq_ref[j, pl.ds(k, CHUNK, stride=8), :]
            gsum = gsum + gq_ref[j, pl.ds(k, CHUNK, stride=8), :]
        dl = delta[:, cols[j]]
        gdelta = psum + xs[:, cols[j]] * gsum
        gxs_ref[:, cols[j]] = dl * gsum + skip[:, cols[j]] * gy[:, cols[j]]
        gdts.append(gdelta * dl * (1.0 - dl * (1.0 / dt_most)))
    gdt = jnp.concatenate(gdts, axis=1)
    gdtb_ref[...] += jnp.sum(gdt, axis=0, keepdims=True)
    gdt_low = gdt.astype(BF16)
    gdtw_ref[...] += dot_tn(proj, gdt_low)
    gp = dot_nt(gdt_low, dtw_ref[...])
    wide_b = jnp.concatenate([gb_ref[pl.ds(n, CHUNK, stride=STATE), :].astype(BF16) for n in range(STATE)], axis=1)
    gp = gp + dot_nt(wide_b, sb_ref[...])
    wide_c = jnp.concatenate([gc_ref[pl.ds(n, CHUNK, stride=STATE), :].astype(BF16) for n in range(STATE)], axis=1)
    gproj_ref[...] = gp + dot_nt(wide_c, sc_ref[...])


def scan_bwd(xs, zg, proj, restart, ys, gg, hck, dtw, dtb, alog, skip, sb, sc):
    rows, ch = xs.shape
    steps = rows // CHUNK
    row = lambda w: pl.BlockSpec((CHUNK, w), lambda i: (steps - 1 - i, 0))
    full = lambda s: pl.BlockSpec(s, lambda i: (0,) * len(s))
    big = lambda: pltpu.VMEM((CHUNK * STATE, LANES), F32)
    g = ch // LANES
    return pl.pallas_call(
        scan_bwd_kernel,
        grid=(steps,),
        out_shape=[
            jax.ShapeDtypeStruct((rows, ch), F32),
            jax.ShapeDtypeStruct((rows, ch), F32),
            jax.ShapeDtypeStruct((rows, LANES), F32),
            jax.ShapeDtypeStruct((LANES, ch), F32),
            jax.ShapeDtypeStruct((1, ch), F32),
            jax.ShapeDtypeStruct((STATE, ch), F32),
            jax.ShapeDtypeStruct((1, ch), F32),
        ],
        in_specs=[row(ch), row(ch), row(LANES), row(1), row(ch), row(ch),
                  pl.BlockSpec((1, STATE, ch), lambda i: (steps - 1 - i, 0, 0)),
                  full((LANES, ch)), full((1, ch)), full((STATE, ch)), full((1, ch)),
                  full((LANES, STATE * LANES)), full((LANES, STATE * LANES))],
        out_specs=[row(ch), row(ch), row(LANES), full((LANES, ch)), full((1, ch)), full((STATE, ch)), full((1, ch))],
        scratch_shapes=[
            pltpu.VMEM((STATE, ch), F32),
            pltpu.VMEM((ch // LANES, CHUNK, LANES), F32),
            pltpu.VMEM((ch // LANES, CHUNK, LANES), F32),
            pltpu.VMEM((ch // LANES, CHUNK, LANES), F32),
            pltpu.VMEM((ch // LANES, CHUNK, LANES), F32),
            big(), big(),
            pltpu.VMEM((g, CHUNK * STATE + STATE, LANES), F32),
            pltpu.VMEM((g, CHUNK * STATE, LANES), F32),
            pltpu.VMEM((g, CHUNK * 8, LANES), F32),
            pltpu.VMEM((g, CHUNK * 8, LANES), F32),
            big(), big(),
        ],
        compiler_params=pltpu.CompilerParams(vmem_limit_bytes=48 << 20),
        name="scan_bwd",
    )(xs, zg, proj, restart, ys, gg, hck, dtw, dtb, alog, skip, sb, sc)


def rms_inverse(values):
    return lax.rsqrt(jnp.mean(values * values, axis=-1, keepdims=True) + epsilon)


def norm_back(values, inverse, gain, grad):
    scaled = grad * gain
    pulled = inverse * scaled - values * (inverse**3) * jnp.mean(scaled * values, axis=-1, keepdims=True)
    return pulled, jnp.sum(grad * values * inverse, axis=0)


def row_layout(seq_lengths, row_total):
    seq_ends = jnp.cumsum(seq_lengths)
    seq_starts = seq_ends - seq_lengths
    position = jnp.arange(row_total, dtype=jnp.int32)
    segment = jnp.sum((position[:, None] >= seq_ends[None, :]).astype(jnp.int32), axis=1)
    restart = jnp.any(position[:, None] == seq_starts[None, :], axis=1)
    return (segment, restart)


def causal_conv(conv_in, taps, bias, segment):
    summed_taps = bias[None, :] + taps[CONV - 1][None, :] * conv_in
    for offset in range(1, CONV):
        shifted = jnp.concatenate(
            [jnp.zeros((offset, conv_in.shape[1]), conv_in.dtype), conv_in[:-offset]], axis=0
        )
        seg_shift = jnp.concatenate([jnp.full((offset,), -1, jnp.int32), segment[:-offset]])
        usable = (seg_shift == segment).astype(conv_in.dtype)
        summed_taps = summed_taps + taps[CONV - 1 - offset][None, :] * shifted * usable[:, None]
    return jax.nn.silu(summed_taps)


def gather_rows(values):
    return lax.all_gather(values, "mp", axis=0, tiled=True)


def scatter_rows(values):
    return lax.psum_scatter(values.astype(BF16), "mp", scatter_dimension=0, tiled=True).astype(F32)


def sum_over_channels(values):
    return lax.psum(values.astype(BF16), "mp")


def to_experts(buffer, lanes):
    experts_slots, width = buffer.shape
    capacity = experts_slots // lax.axis_size("dp")
    copies = jnp.broadcast_to(
        buffer.reshape(-1, 1, capacity, width), (lax.axis_size("dp"), lanes, capacity, width)
    ).reshape(-1, capacity, width)
    arrived = lax.all_to_all(copies, ("dp", "mp"), split_axis=0, concat_axis=0, tiled=True)
    return arrived.reshape(-1, width)


def from_experts(partial_out, lanes):
    rows, width = partial_out.shape
    capacity = rows // (lanes * lax.axis_size("dp"))
    arrived = lax.all_to_all(
        partial_out.reshape(-1, capacity, width).astype(BF16),
        ("dp", "mp"),
        split_axis=0,
        concat_axis=0,
        tiled=True,
    ).astype(F32)
    return jnp.sum(arrived.reshape(-1, lanes, capacity, width), axis=1).astype(BF16).reshape(-1, width)


def on_device(
    tokens, cotangent, lengths, routes, slot_place, norm_in, w_in, conv_w, conv_b, x_proj, dt_proj, dt_bias,
    a_log, d_skip, w_out, norm_moe, router, w_up, w_down,
):
    layers = norm_in.shape[0]
    rows_here, width = tokens.shape
    lanes = lax.axis_size("mp")
    row_total = rows_here * lanes
    experts = router.shape[2]
    capacity = max(2, (5 * rows_here + 4 * experts - 1) // (4 * experts))
    padded = (capacity + 15) // 16 * 16
    segment, restart_flag = row_layout(lengths[0], row_total)
    restart = restart_flag.astype(F32)[:, None]
    chosen = routes[:, None] == jnp.arange(experts, dtype=jnp.int32)[None, :]
    choose = chosen.astype(F32)
    place = routes * padded + slot_place
    pick = (place[:, None] == jnp.arange(experts * padded, dtype=jnp.int32)[None, :]).astype(BF16)
    spread_b, spread_c = spread_matrix(DT_RANK), spread_matrix(DT_RANK + STATE)
    proj_pad = ((0, 0), (0, 0), (0, LANES - x_proj.shape[2]))
    x_proj = jnp.pad(x_proj, proj_pad)
    dt_proj = jnp.pad(dt_proj, ((0, 0), (0, LANES - DT_RANK), (0, 0)))

    activation = tokens.astype(F32)
    stored = []
    for l in range(layers):
        inv_in = rms_inverse(activation)
        whole = gather_rows((activation * inv_in * norm_in[l]).astype(BF16))
        conv_in = dot(whole, w_in[l, 0])
        gate_in = dot(whole, w_in[l, 1])
        conv_out, conv_pull = jax.vjp(
            lambda v, taps, bias: causal_conv(v, taps, bias, segment), conv_in, conv_w[l], conv_b[l]
        )
        conv_low = conv_out.astype(BF16)
        proj = sum_over_channels(dot(conv_low, x_proj[l]))
        gated, ys, marks = scan_fwd(
            conv_out, gate_in, proj, restart, dt_proj[l], dt_bias[l : l + 1], a_log[l], d_skip[l : l + 1], spread_b, spread_c
        )
        middle = activation + scatter_rows(dot(gated, w_out[l]))
        inv_moe = rms_inverse(middle)
        normed = middle * inv_moe * norm_moe[l]
        chance = jax.nn.softmax(jnp.dot(normed, router[l], precision=highest), axis=-1)
        gate = jnp.sum(chance * choose, axis=1, keepdims=True)
        arrived = to_experts(dot_tn(pick, normed.astype(BF16)).astype(BF16), lanes)
        hidden = dot(arrived, w_up[l, 0])
        active = jax.nn.gelu(hidden).astype(BF16)
        picked = dot(pick, from_experts(dot(active, w_down[l, 0]), lanes))
        stored.append((activation, inv_in, whole, gate_in, conv_out, conv_low, conv_pull, proj, gated, ys, marks,
                       middle, inv_moe, normed, chance, gate, arrived, hidden, active, picked))
        activation = middle + gate * picked
    upstream = cotangent.astype(F32)
    collected = []
    for l in reversed(range(layers)):
        (before, inv_in, whole, gate_in, conv_out, conv_low, conv_pull, proj, gated, ys, marks,
         middle, inv_moe, normed, chance, gate, arrived, hidden, active, picked) = stored[l]
        slot_grad = to_experts(dot_tn(pick, (gate * upstream).astype(BF16)).astype(BF16), lanes)
        grad_down = dot_tn(active, slot_grad)
        grad_active = dot_nt(slot_grad, w_down[l, 0])
        _, gelu_pull = jax.vjp(jax.nn.gelu, hidden)
        grad_hidden = gelu_pull(grad_active)[0].astype(BF16)
        grad_up = dot_tn(arrived, grad_hidden)
        grad_normed = dot(pick, from_experts(dot_nt(grad_hidden, w_up[l, 0]), lanes))
        grad_gate = jnp.sum(upstream * picked, axis=1, keepdims=True)
        grad_logit = gate * grad_gate * (choose - chance)
        grad_router = lax.dot_general(normed, grad_logit, (((0,), (0,)), ((), ())), precision=highest)
        grad_normed = grad_normed + lax.dot_general(
            grad_logit, router[l], (((1,), (1,)), ((), ())), precision=highest
        )
        pulled, grad_norm_moe = norm_back(middle, inv_moe, norm_moe[l], grad_normed)
        grad_middle = upstream + pulled
        grad_whole = gather_rows(grad_middle.astype(BF16))
        grad_w_out = dot_tn(gated, grad_whole)
        grad_gated = dot_nt(grad_whole, w_out[l])
        grad_conv, grad_gate_in, grad_proj_part, grad_dtw, grad_dtb, grad_alog, grad_skip = scan_bwd(
            conv_out, gate_in, proj, restart, ys, grad_gated, marks, dt_proj[l], dt_bias[l : l + 1], a_log[l],
            d_skip[l : l + 1], spread_b, spread_c
        )
        grad_proj = sum_over_channels(grad_proj_part)
        grad_x_proj = dot_tn(conv_low, grad_proj)
        grad_conv_in, grad_taps, grad_bias = conv_pull(grad_conv + dot_nt(grad_proj, x_proj[l]))
        grad_xi, grad_zg = grad_conv_in.astype(BF16), grad_gate_in.astype(BF16)
        grad_w_in = jnp.stack([dot_tn(whole, grad_xi), dot_tn(whole, grad_zg)])
        grad_u = scatter_rows(dot_nt(grad_xi, w_in[l, 0]) + dot_nt(grad_zg, w_in[l, 1]))
        pulled, grad_norm_in = norm_back(before, inv_in, norm_in[l], grad_u)
        upstream = grad_middle + pulled
        summed = [
            lax.psum(value.astype(BF16), "dp").astype(F32)
            for value in (grad_w_in, grad_taps, grad_bias, grad_x_proj[:, : DT_RANK + 2 * STATE], grad_dtw[:DT_RANK],
                          grad_dtb[0], grad_alog, grad_skip[0], grad_w_out)
        ]
        shared = lax.psum((grad_norm_in, grad_norm_moe, grad_router), ("dp", "mp"))
        collected.append((summed, shared, grad_up, grad_down))
    collected = collected[::-1]

    def stacked(first, second):
        return jnp.stack([entry[first][second] for entry in collected])

    return (
        activation,
        upstream,
        stacked(1, 0),
        *(stacked(0, i) for i in range(9)),
        stacked(1, 1),
        stacked(1, 2),
        jnp.stack([entry[2][None] for entry in collected]),
        jnp.stack([entry[3][None] for entry in collected]),
    )


def solution(mesh):
    return jax.shard_map(
        on_device,
        mesh=mesh,
        in_specs=(
            P(("dp", "mp"), None),
            P(("dp", "mp"), None),
            P("dp", None),
            P(("dp", "mp")),
            P(("dp", "mp")),
            P(),
            P(None, None, None, "mp"),
            P(None, None, "mp"),
            P(None, "mp"),
            P(None, "mp", None),
            P(None, None, "mp"),
            P(None, "mp"),
            P(None, None, "mp"),
            P(None, "mp"),
            P(None, "mp", None),
            P(),
            P(),
            P(None, "dp", None, "mp"),
            P(None, "dp", "mp", None),
        ),
        out_specs=(
            P(("dp", "mp"), None),
            P(("dp", "mp"), None),
            P(),
            P(None, None, None, "mp"),
            P(None, None, "mp"),
            P(None, "mp"),
            P(None, "mp", None),
            P(None, None, "mp"),
            P(None, "mp"),
            P(None, None, "mp"),
            P(None, "mp"),
            P(None, "mp", None),
            P(),
            P(),
            P(None, "dp", None, "mp"),
            P(None, "dp", "mp", None),
        ),
        check_vma=False,
    )
```

time: 1940 us -> 1100 us (0.57)
  local copies, waits for them, and re-layouts: 494 us -> 51.8 us
  matrix products: 447 us -> 106 us
  other arithmetic: 157 us -> 65.9 us
  blocking collectives: 202 us -> 120 us
  Pallas kernels: 0 us -> 81.2 us
  waiting for transfers between devices: 580 us -> 624 us
    dot_general x282 -> x50, matrix products: 447 us -> 106 us  [the longest x12 34.7 us: dot_nt(): lax.dot_general(a, b, (((1,), (1,)), ((), ())), preferred_element_type=F32)]
    squeeze x216 -> x2, local copies, waits for them, and re-layouts: 186 us -> 0.66 us  [the longest x1 0.65 us: on_device(): dt_proj[l]]
    dynamic_update_slice x96 -> x0, local copies, waits for them, and re-layouts: 89.4 us -> none  [selective(): lax.scan(jax.checkpoint(block_step), jnp.zeros((STATE, channels), conv_ou...]
    all_to_all x4 -> x2, blocking collectives: 162 us -> 79.9 us  [to_experts(): lax.all_to_all(copies, ('dp', 'mp'), split_axis=0, concat_axis=0, tiled=T...]
    pallas_call x0 -> x4, Pallas kernels: none -> 81.2 us  [the longest x2 56.1 us: scan_bwd(): pl.pallas_call(scan_bwd_kernel, grid=(steps,), out_shape=[jax.ShapeDtypeS...]
    scatter x8 -> x0, local copies, waits for them, and re-layouts: 45.6 us -> none  [the longest x4 22.8 us: on_device(): buffer = jnp.zeros((experts, capacity, model_width), jnp.bfloat16).at[rou...]
    while x216 -> x0, local copies, waits for them, and re-layouts: 42.7 us -> none
    mul x170 -> x0, local copies, waits for them, and re-layouts: 41.1 us -> none  [the longest x96 34.8 us: scan_block(): drive = drive_in[:, None, :] * in_mat[:, :, None]]
  transfers between devices with their start and end apart: 18 -> 20, of which waited for: 18 -> 20; matrix products, arithmetic and copies ran while one was open for 4% -> 9% of each run, Pallas kernels for 0% -> 0%
where the time goes in v1:
time: 1100 us; the launch traced here: 1090 us
  waiting for transfers between devices  624 us (57%)
  blocking collectives  120 us (11%)
  matrix products  106 us (10%)
  Pallas kernels  81.2 us (7%)
  other arithmetic  65.9 us (6%)
  local copies, waits for them, and re-layouts  51.8 us (5%)
  starting transfers between devices  27.4 us (2%)
  between operations  16.3 us (1%)
    psum x4, waiting for transfers between devices, sum_over_channels(): return lax.psum(values.astype(BF16), 'mp')  125 us
    all_to_all x4, waiting for transfers between devices, from_experts(): lax.all_to_all(partial_out.reshape(-1, capacity, width).astype(BF16), ('d...  125 us
    reduce_scatter x4, waiting for transfers between devices, scatter_rows(): lax.psum_scatter(values.astype(BF16), 'mp', scatter_dimension=0, tiled=True)  112 us
    all_gather x4, waiting for transfers between devices, gather_rows(): return lax.all_gather(values, 'mp', axis=0, tiled=True)  107 us
    psum x2, waiting for transfers between devices, on_device(): lax.psum(value.astype(BF16), 'dp').astype(F32)  98.6 us
    all_to_all x2, blocking collectives, to_experts(): lax.all_to_all(copies, ('dp', 'mp'), split_axis=0, concat_axis=0, tiled=T...  79.9 us
    all_to_all x2, waiting for transfers between devices, to_experts(): lax.all_to_all(copies, ('dp', 'mp'), split_axis=0, concat_axis=0, tiled=T...  56.5 us
    pallas_call x2, Pallas kernels, scan_bwd(): pl.pallas_call(scan_bwd_kernel, grid=(steps,), out_shape=[jax.ShapeDtypeS...  56.1 us
  transfers between devices with their start and end apart: 20, of which 20 were waited for; matrix products, arithmetic and copies ran while one was open for 9% of the time, Pallas kernels for 0%

profile of v1, /device:TPU:0, one launch (start us, length us, event | category | flops | bytes accessed | tf_op | source)
XLA Modules:
  0.0 1092.9 jit_solution(4649038172577978455)
XLA Ops:
  17.6 28.5 %all-gather.5.cloned.1.call-done = bf16[768,768]{1,0:T(8,128)(2,1)} async-done(((bf16[192,768]{1,0:T(8,128)(2,1)}), bf16[768,768]{1,0:T(8,128)(2,1)}) %all-gather.5.cloned.1.call-update) | async-done | bytes 1179664 | tf_op jit(solution)/shard_map/all_gather | solution.py:325
  53.7 31.8 %all-reduce.34.cloned.1.call-done.proj_ref = bf16[768,128]{1,0:T(8,128)(2,1)} async-done(((bf16[768,128]{1,0:T(8,128)(2,1)}), bf16[768,128]{1,0:T(8,128)(2,1)}) %all-reduce.34.cloned.1.call-update) | async-done | bytes 196624 | tf_op jit(solution)/shard_map/psum | solution.py:333
  88.8 12.5 %scan_fwd.2 = (bf16[768,384]{1,0:T(8,128)(2,1)S(1)}, f32[768,384]{1,0:T(8,128)S(1)}, f32[6,16,384]{2,1,0:T(8,128)S(1)}) custom-call(f32[768,384]{1,0:T(8,128)S(1)} %get-tuple-element.130.xs_ref, f32[768,384]{1,0:T(8,128)S(1)} %fusion.87.zg_ref, bf16[768,128]{1,0:T(8,128)(2,1)S(1)} %copy-done.18, f32[768,1]{1,0:T(8,128)S(1)} %copy-done.2, ...), custom_call_target="tpu_custom_call" | custom-call | tf_op jit(solution)/shard_map/scan_fwd/pallas_call | solution.py:111
  107.0 27.7 %reduce-scatter.5.cloned.1.call-done = bf16[192,768]{1,0:T(8,128)(2,1)} async-done(((bf16[768,768]{1,0:T(8,128)(2,1)}), bf16[192,768]{1,0:T(8,128)(2,1)}) %reduce-scatter.5.cloned.1.call-update) | async-done | bytes 294928 | tf_op jit(solution)/shard_map/reduce_scatter | solution.py:329
  138.0 40.0 %all_to_all.40 = bf16[32,32,768]{2,1,0:T(8,128)(2,1)S(1)} all-to-all(bf16[32,32,768]{2,1,0:T(8,128)(2,1)S(1)} %bitcast.247), channel_id=1, replica_groups=mesh['dp'=8,'mp'=4] {'dp','mp'}, dimensions={0} | all-to-all | bytes 3145728 | tf_op jit(solution)/shard_map/all_to_all | solution.py:342
  178.0 3.4 multiply_convert_fusion.1
  185.1 4.2 all-to-all-start.1
  190.7 34.5 %all-to-all-done.1 = bf16[32,32,768]{2,1,0:T(8,128)(2,1)} async-done(((bf16[32,32,768]{2,1,0:T(8,128)(2,1)}), bf16[32,32,768]{2,1,0:T(8,128)(2,1)}, u32[]{:S(2)}, u32[]{:S(2)}) %all-to-all-start.1) | async-done | bytes 1572896 | tf_op jit(solution)/shard_map/all_to_all | solution.py:349
  230.2 30.5 %all-gather.7.cloned.1.call-done = bf16[768,768]{1,0:T(8,128)(2,1)} async-done(((bf16[192,768]{1,0:T(8,128)(2,1)}), bf16[768,768]{1,0:T(8,128)(2,1)}) %all-gather.7.cloned.1.call-update) | async-done | bytes 1179664 | tf_op jit(solution)/shard_map/all_gather | solution.py:325
  263.0 3.1 fusion.40
  267.6 3.2 fusion.77.zg_ref
  270.8 30.4 %all-reduce.36.cloned.1.call-done.proj_ref = bf16[768,128]{1,0:T(8,128)(2,1)} async-done(((bf16[768,128]{1,0:T(8,128)(2,1)}), bf16[768,128]{1,0:T(8,128)(2,1)}) %all-reduce.36.cloned.1.call-update) | async-done | bytes 196624 | tf_op jit(solution)/shard_map/psum | solution.py:333
  306.6 12.5 %scan_fwd.3 = (bf16[768,384]{1,0:T(8,128)(2,1)S(1)}, f32[768,384]{1,0:T(8,128)S(1)}, f32[6,16,384]{2,1,0:T(8,128)S(1)}) custom-call(f32[768,384]{1,0:T(8,128)S(1)} %get-tuple-element.126.xs_ref, f32[768,384]{1,0:T(8,128)S(1)} %copy-done.1, bf16[768,128]{1,0:T(8,128)(2,1)S(1)} %copy-done.20, f32[768,1]{1,0:T(8,128)S(1)} %copy-done.3, ...), custom_call_target="tpu_custom_call" | custom-call | tf_op jit(solution)/shard_map/scan_fwd/pallas_call | solution.py:111
  323.5 29.1 %reduce-scatter.7.cloned.1.call-done = bf16[192,768]{1,0:T(8,128)(2,1)} async-done(((bf16[768,768]{1,0:T(8,128)(2,1)}), bf16[192,768]{1,0:T(8,128)(2,1)}) %reduce-scatter.7.cloned.1.call-update) | async-done | bytes 294928 | tf_op jit(solution)/shard_map/reduce_scatter | solution.py:329
  356.5 3.4 all-to-all-start.2
  366.3 29.6 %all-to-all-done.2 = bf16[32,32,768]{2,1,0:T(8,128)(2,1)} async-done(((bf16[32,32,768]{2,1,0:T(8,128)(2,1)}), bf16[32,32,768]{2,1,0:T(8,128)(2,1)}, u32[]{:S(2)}, u32[]{:S(2)}) %all-to-all-start.2) | async-done | bytes 1572896 | tf_op jit(solution)/shard_map/all_to_all | solution.py:342
  398.2 4.7 all-to-all-start.4
  402.9 5.3 multiply_convert_fusion
  411.9 26.9 %all-to-all-done.4 = bf16[32,32,768]{2,1,0:T(8,128)(2,1)} async-done(((bf16[32,32,768]{2,1,0:T(8,128)(2,1)}), bf16[32,32,768]{2,1,0:T(8,128)(2,1)}, u32[]{:S(2)}, u32[]{:S(2)}) %all-to-all-start.4) | async-done | bytes 1572896 | tf_op jit(solution)/shard_map/all_to_all | solution.py:342
  438.8 4.7 all-to-all-start.3
  443.5 5.7 fusion.13
  452.9 26.5 %all-to-all-done.3 = bf16[32,32,768]{2,1,0:T(8,128)(2,1)} async-done(((bf16[32,32,768]{2,1,0:T(8,128)(2,1)}), bf16[32,32,768]{2,1,0:T(8,128)(2,1)}, u32[]{:S(2)}, u32[]{:S(2)}) %all-to-all-start.3) | async-done | bytes 1572896 | tf_op jit(solution)/shard_map/all_to_all | solution.py:349
  479.5 4.7 all-to-all-start.5
  489.4 30.7 %all-to-all-done.5 = bf16[32,32,768]{2,1,0:T(8,128)(2,1)} async-done(((bf16[32,32,768]{2,1,0:T(8,128)(2,1)}), bf16[32,32,768]{2,1,0:T(8,128)(2,1)}, u32[]{:S(2)}, u32[]{:S(2)}) %all-to-all-start.5) | async-done | bytes 1572896 | tf_op jit(solution)/shard_map/all_to_all | solution.py:349
  524.4 30.5 %all-gather.9.cloned.1.call-done = bf16[768,768]{1,0:T(8,128)(2,1)} async-done(((bf16[192,768]{1,0:T(8,128)(2,1)}), bf16[768,768]{1,0:T(8,128)(2,1)}) %all-gather.9.cloned.1.call-update) | async-done | bytes 1179664 | tf_op jit(solution)/shard_map/all_gather | solution.py:325
  555.0 3.3 fusion.73.gg_ref
  558.3 28.0 %scan_bwd.2 = (f32[768,384]{1,0:T(8,128)S(1)}, f32[768,384]{1,0:T(8,128)S(1)}, f32[768,128]{1,0:T(8,128)S(1)}, f32[128,384]{1,0:T(8,128)S(1)}, f32[1,384]{1,0:T(...) custom-call(f32[768,384]{1,0:T(8,128)S(1)} %get-tuple-element.126.xs_ref, f32[768,384]{1,0:T(8,128)} %fusion.77.zg_ref, ...), custom_call_target="tpu_custom_call" | custom-call | tf_op jit(solution)/shard_map/scan_bwd/pallas_call | solution.py:258
  591.6 34.0 %all-reduce.38.cloned.1.call-done = bf16[768,128]{1,0:T(8,128)(2,1)} async-done(((bf16[768,128]{1,0:T(8,128)(2,1)}), bf16[768,128]{1,0:T(8,128)(2,1)}) %all-reduce.38.cloned.1.call-update) | async-done | bytes 196624 | tf_op jit(solution)/shard_map/psum | solution.py:333
  625.6 4.7 multiply_reduce_fusion.3
  637.7 29.0 %reduce-scatter.9.cloned.1.call-done = bf16[192,768]{1,0:T(8,128)(2,1)} async-done(((bf16[768,768]{1,0:T(8,128)(2,1)}), bf16[192,768]{1,0:T(8,128)(2,1)}) %reduce-scatter.9.cloned.1.call-update) | async-done | bytes 294928 | tf_op jit(solution)/shard_map/reduce_scatter | solution.py:329
  671.4 40.0 %all_to_all.41 = bf16[32,32,768]{2,1,0:T(8,128)(2,1)S(1)} all-to-all(bf16[32,32,768]{2,1,0:T(8,128)(2,1)S(1)} %bitcast.248), channel_id=1, replica_groups=mesh['dp'=8,'mp'=4] {'dp','mp'}, dimensions={0} | all-to-all | bytes 3145728 | tf_op jit(solution)/shard_map/all_to_all | solution.py:342
  711.4 3.5 fusion.6
  718.6 4.2 all-to-all-start.7
  725.7 33.0 %all-to-all-done.7 = bf16[32,32,768]{2,1,0:T(8,128)(2,1)} async-done(((bf16[32,32,768]{2,1,0:T(8,128)(2,1)}), bf16[32,32,768]{2,1,0:T(8,128)(2,1)}, u32[]{:S(2)}, u32[]{:S(2)}) %all-to-all-start.7) | async-done | bytes 1572896 | tf_op jit(solution)/shard_map/all_to_all | solution.py:349
  767.4 3.1 fusion.19
  775.6 17.8 %all-gather.11.cloned.1.call-done = bf16[768,768]{1,0:T(8,128)(2,1)} async-done(((bf16[192,768]{1,0:T(8,128)(2,1)}), bf16[768,768]{1,0:T(8,128)(2,1)}) %all-gather.11.cloned.1.call-update) | async-done | bytes 1179664 | tf_op jit(solution)/shard_map/all_gather | solution.py:325
  793.4 3.2 fusion.83.gg_ref
  796.7 28.1 %scan_bwd.3 = (f32[768,384]{1,0:T(8,128)S(1)}, f32[768,384]{1,0:T(8,128)S(1)}, f32[768,128]{1,0:T(8,128)S(1)}, f32[128,384]{1,0:T(8,128)S(1)}, f32[1,384]{1,0:T(...) custom-call(f32[768,384]{1,0:T(8,128)S(1)} %get-tuple-element.130.xs_ref, f32[768,384]{1,0:T(8,128)} %copy-done, ...), custom_call_target="tpu_custom_call" | custom-call | tf_op jit(solution)/shard_map/scan_bwd/pallas_call | solution.py:258
  830.0 3.1 fusion.18
  835.3 28.7 %all-reduce.40.cloned.1.call-done = bf16[768,128]{1,0:T(8,128)(2,1)} async-done(((bf16[768,128]{1,0:T(8,128)(2,1)}), bf16[768,128]{1,0:T(8,128)(2,1)}) %all-reduce.40.cloned.1.call-update) | async-done | bytes 196624 | tf_op jit(solution)/shard_map/psum | solution.py:333
  866.0 4.0 multiply_reduce_fusion.7
  876.9 4.8 convolution_bitcast_fusion
  881.9 4.4 convolution_bitcast_fusion.2
  890.2 3.5 convolution_bitcast_fusion.1
  901.3 29.0 %all-reduce.42.cloned.1.call-done = (bf16[1,4,384]{2,1,0:T(4,128)(2,1)}, bf16[1,4,384]{2,1,0:T(4,128)(2,1)}, bf16[1,384]{1,0:T(2,128)(2,1)}, bf16[1,384]{1,0:T(2...) async-done(((bf16[1,4,384]{2,1,0:T(4,128)(2,1)}, ...) | async-done | bytes 231952 | tf_op jit(solution)/shard_map/psum | solution.py:444
  939.8 69.6 %all-reduce.44.cloned.1.call-done = (bf16[1,2,768,384]{3,2,1,0:T(8,128)(2,1)}, bf16[1,2,768,384]{3,2,1,0:T(8,128)(2,1)}, bf16[1,384,768]{2,1,0:T(8,128)(2,1)}, bf16[1,384,768]{2,1,0:T(8,128)(2,1)}) async-done(((bf16[1,2,768,384]{3,2,1,0:T(8,128)(2,1)}, bf16[1,2,768,384]{3,2,1,0:T(8,128)(2,1)}, bf16[1,384,768]{2,1,0:T(8,128)(2,1)}, bf16[1,384,768]{2,1,0:T(8,128)(2,1)}), (bf16[1,2,768,384]{3,2,1,0:T(8,128)(2,1)}, ...) | async-done | bytes 3538960 | tf_op jit(solution)/shard_map/psum | solution.py:444
  1014.8 26.1 %reduce-scatter.11.cloned.1.call-done = bf16[192,768]{1,0:T(8,128)(2,1)} async-done(((bf16[768,768]{1,0:T(8,128)(2,1)}), bf16[192,768]{1,0:T(8,128)(2,1)}) %reduce-scatter.11.cloned.1.call-update) | async-done | bytes 294928 | tf_op jit(solution)/shard_map/reduce_scatter | solution.py:329
  1042.1 40.0 %all-reduce.24 = (f32[1,768]{1,0:T(1,128)S(1)}, f32[1,768]{1,0:T(1,128)S(1)}, f32[1,768]{1,0:T(1,128)S(1)}, f32[1,768]{1,0:T(1,128)S(1)}, f32[1,768,8]{1,2,0:T(8,128)S(1)}, /*index=5*/f32[1,768,8]{1,2,0:T(8,128)S(1)}) all-reduce(f32[1,768]{1,0:T(1,128)S(1)} %stack.184, ...), channel_id=1, replica_groups=mesh['dp'=8,'mp'=4] {'dp','mp'}, use_global_device_ids=true, to_apply=%region_34.35 | all-reduce | flops 15360 | bytes 122880 | tf_op jit(solution)/shard_map/psum | solution.py:448
  (566 shorter events, 167.6 us)
Async XLA Ops:
  7.3 38.9 %all-gather.5.cloned.1.call-start = ((), (), s32[]{:S(2)}) async-start(), calls=%async_computation.12 | async-start | bytes 1474560 | tf_op jit(solution)/shard_map/all_gather | solution.py:325
  12.8 72.7 %all-reduce.34.cloned.1.call-start = ((), (), s32[]{:S(2)}) async-start(), calls=%async_computation.13 | async-start | bytes 393216 | tf_op jit(solution)/shard_map/psum | solution.py:333
  51.4 83.3 %reduce-scatter.5.cloned.1.call-start = ((), (), s32[]{:S(2)}) async-start(), calls=%async_computation.14 | async-start | bytes 1474560 | tf_op jit(solution)/shard_map/reduce_scatter | solution.py:329
  53.7 47.7 %copy-start = (f32[768,384]{1,0:T(8,128)}, f32[768,384]{1,0:T(8,128)S(1)}, u32[]{:S(2)}) copy-start(f32[768,384]{1,0:T(8,128)S(1)} %fusion.87.zg_ref) | copy-start | bytes 3538948
  105.7 29.1 %copy-start.50 = (bf16[192,768]{1,0:T(8,128)(2,1)S(1)}, bf16[192,768]{1,0:T(8,128)(2,1)}, u32[]{:S(2)}) copy-start(bf16[192,768]{1,0:T(8,128)(2,1)} %param.19) | copy-start | bytes 884740
  107.0 82.4 %copy-start.116 = (f32[768]{0:T(1024)}, f32[768]{0:T(1024)S(1)}, u32[]{:S(2)}) copy-start(f32[768]{0:T(1024)S(1)} %get-tuple-element.77) | copy-start | bytes 9220
  107.0 31.1 %copy-start.110 = (s32[192]{0:T(256)}, s32[192]{0:T(256)S(1)}, u32[]{:S(2)}) copy-start(s32[192]{0:T(256)S(1)} %multiply_add_fusion.4) | copy-start | bytes 2308
  136.5 52.9 %copy-start.158 = (f32[192]{0:T(256)}, f32[192]{0:T(256)S(1)}, u32[]{:S(2)}) copy-start(f32[192]{0:T(256)S(1)} %get-tuple-element.159) | copy-start | bytes 2308
  138.0 40.0 %copy-start.188 = (bf16[2,1,768,768]{3,2,1,0:T(8,128)(2,1)S(1)}, bf16[2,1,768,768]{3,2,1,0:T(8,128)(2,1)}, u32[]{:S(2)}) copy-start(bf16[2,1,768,768]{3,2,1,0:T(8,128)(2,1)} %param.36) | copy-start | bytes 7077892
  185.1 40.1 %all-to-all-start.1 = ((bf16[32,32,768]{2,1,0:T(8,128)(2,1)}), bf16[32,32,768]{2,1,0:T(8,128)(2,1)}, u32[]{:S(2)}, u32[]{:S(2)}) async-start(bf16[32,32,768]{2,1,0:T(8,128)(2,1)} %convolution_convert_fusion.3), calls=%async_computation.2 | async-start | bytes 3145728 | tf_op jit(solution)/shard_map/all_to_all | solution.py:349
  189.3 71.5 %all-gather.7.cloned.1.call-start = ((), (), s32[]{:S(2)}) async-start(), calls=%async_computation.15 | async-start | bytes 1474560 | tf_op jit(solution)/shard_map/all_gather | solution.py:325
  190.1 36.8 %copy-start.102 = (f32[192,8]{0,1:T(8,128)}, f32[192,8]{0,1:T(8,128)S(1)}, u32[]{:S(2)}) copy-start(f32[192,8]{0,1:T(8,128)S(1)} %get-tuple-element.167) | copy-start | bytes 18436
  190.1 36.8 %copy-start.164 = (f32[192]{0:T(256)}, f32[192]{0:T(256)S(1)}, u32[]{:S(2)}) copy-start(f32[192]{0:T(256)S(1)} %get-tuple-element.166) | copy-start | bytes 2308
  190.1 36.8 %copy-start.166 = (f32[192]{0:T(256)}, f32[192]{0:T(256)S(1)}, u32[]{:S(2)}) copy-start(f32[192]{0:T(256)S(1)} %fusion.175) | copy-start | bytes 2308
  228.7 34.3 %copy-start.53 = (f32[192,768]{1,0:T(8,128)}, f32[192,768]{1,0:T(8,128)S(1)}, u32[]{:S(2)}) copy-start(f32[192,768]{1,0:T(8,128)S(1)} %get-tuple-element.129) | copy-start | bytes 1769476
  229.3 33.6 %copy-start.153 = (f32[192]{0:T(256)}, f32[192]{0:T(256)S(1)}, u32[]{:S(2)}) copy-start(f32[192]{0:T(256)S(1)} %get-tuple-element.161) | copy-start | bytes 2308
  230.2 71.0 %all-reduce.36.cloned.1.call-start = ((), (), s32[]{:S(2)}) async-start(), calls=%async_computation.16 | async-start | bytes 393216 | tf_op jit(solution)/shard_map/psum | solution.py:333
  267.1 85.5 %reduce-scatter.7.cloned.1.call-start = ((), (), s32[]{:S(2)}) async-start(), calls=%async_computation.17 | async-start | bytes 1474560 | tf_op jit(solution)/shard_map/reduce_scatter | solution.py:329
  356.5 39.4 %all-to-all-start.2 = ((bf16[32,32,768]{2,1,0:T(8,128)(2,1)}), bf16[32,32,768]{2,1,0:T(8,128)(2,1)}, u32[]{:S(2)}, u32[]{:S(2)}) async-start(bf16[32,32,768]{2,1,0:T(8,128)(2,1)} %bitcast.245), calls=%async_computation.4 | async-start | bytes 3145728 | tf_op jit(solution)/shard_map/all_to_all | solution.py:342
  398.2 40.6 %all-to-all-start.4 = ((bf16[32,32,768]{2,1,0:T(8,128)(2,1)}), bf16[32,32,768]{2,1,0:T(8,128)(2,1)}, u32[]{:S(2)}, u32[]{:S(2)}) async-start(bf16[32,32,768]{2,1,0:T(8,128)(2,1)} %bitcast.246), calls=%async_computation.6 | async-start | bytes 3145728 | tf_op jit(solution)/shard_map/all_to_all | solution.py:342
  438.8 40.7 %all-to-all-start.3 = ((bf16[32,32,768]{2,1,0:T(8,128)(2,1)}), bf16[32,32,768]{2,1,0:T(8,128)(2,1)}, u32[]{:S(2)}, u32[]{:S(2)}) async-start(bf16[32,32,768]{2,1,0:T(8,128)(2,1)} %convolution_convert_fusion.2), calls=%async_computation.5 | async-start | bytes 3145728 | tf_op jit(solution)/shard_map/all_to_all | solution.py:349
  479.5 40.6 %all-to-all-start.5 = ((bf16[32,32,768]{2,1,0:T(8,128)(2,1)}), bf16[32,32,768]{2,1,0:T(8,128)(2,1)}, u32[]{:S(2)}, u32[]{:S(2)}) async-start(bf16[32,32,768]{2,1,0:T(8,128)(2,1)} %convolution_convert_fusion.1), calls=%async_computation.7 | async-start | bytes 3145728 | tf_op jit(solution)/shard_map/all_to_all | solution.py:349
  484.1 70.8 %all-gather.9.cloned.1.call-start = ((), (), s32[]{:S(2)}) async-start(), calls=%async_computation.18 | async-start | bytes 1474560 | tf_op jit(solution)/shard_map/all_gather | solution.py:325
  524.4 101.2 %all-reduce.38.cloned.1.call-start = ((), (), s32[]{:S(2)}) async-start(), calls=%async_computation.19 | async-start | bytes 393216 | tf_op jit(solution)/shard_map/psum | solution.py:333
  591.5 75.2 %reduce-scatter.9.cloned.1.call-start = ((), (), s32[]{:S(2)}) async-start(), calls=%async_computation.20 | async-start | bytes 1474560 | tf_op jit(solution)/shard_map/reduce_scatter | solution.py:329
  637.7 29.1 %copy-start.109 = (f32[768]{0:T(1024)S(1)}, f32[768]{0:T(1024)}, u32[]{:S(2)}) copy-start(f32[768]{0:T(1024)} %get-tuple-element.78) | copy-start | bytes 9220
  637.7 29.1 %copy-start.154 = (f32[192]{0:T(256)S(1)}, f32[192]{0:T(256)}, u32[]{:S(2)}) copy-start(f32[192]{0:T(256)} %copy-done.153) | copy-start | bytes 2308
  637.7 31.0 %copy-start.176 = (f32[192]{0:T(256)S(1)}, f32[192]{0:T(256)}, u32[]{:S(2)}) copy-start(f32[192]{0:T(256)} %get-tuple-element.160) | copy-start | bytes 2308
  670.5 41.0 %copy-start.198 = (f32[1024,768]{1,0:T(8,128)S(1)}, f32[1024,768]{1,0:T(8,128)}, u32[]{:S(2)}) copy-start(f32[1024,768]{1,0:T(8,128)} %get-tuple-element.165) | copy-start | bytes 9437188
  671.4 40.0 %copy-start.187 = (bf16[2,1,768,768]{3,2,1,0:T(8,128)(2,1)S(1)}, bf16[2,1,768,768]{3,2,1,0:T(8,128)(2,1)}, u32[]{:S(2)}) copy-start(bf16[2,1,768,768]{3,2,1,0:T(8,128)(2,1)} %param.37) | copy-start | bytes 7077892
  718.6 40.1 %all-to-all-start.7 = ((bf16[32,32,768]{2,1,0:T(8,128)(2,1)}), bf16[32,32,768]{2,1,0:T(8,128)(2,1)}, u32[]{:S(2)}, u32[]{:S(2)}) async-start(bf16[32,32,768]{2,1,0:T(8,128)(2,1)} %convolution_convert_fusion), calls=%async_computation.10 | async-start | bytes 3145728 | tf_op jit(solution)/shard_map/all_to_all | solution.py:349
  722.8 70.6 %all-gather.11.cloned.1.call-start = ((), (), s32[]{:S(2)}) async-start(), calls=%async_computation.21 | async-start | bytes 1474560 | tf_op jit(solution)/shard_map/all_gather | solution.py:325
  723.5 37.0 %copy-start.117 = (f32[768]{0:T(1024)S(1)}, f32[768]{0:T(1024)}, u32[]{:S(2)}) copy-start(f32[768]{0:T(1024)} %copy-done.116) | copy-start | bytes 9220
  723.5 37.1 %copy-start.159 = (f32[192]{0:T(256)S(1)}, f32[192]{0:T(256)}, u32[]{:S(2)}) copy-start(f32[192]{0:T(256)} %copy-done.158) | copy-start | bytes 2308
  762.9 101.2 %all-reduce.40.cloned.1.call-start = ((), (), s32[]{:S(2)}) async-start(), calls=%async_computation.22 | async-start | bytes 393216 | tf_op jit(solution)/shard_map/psum | solution.py:333
  775.6 21.1 %copy-start.31 = (f32[1,384]{1,0:T(1,128)S(1)}, f32[1,384]{1,0:T(1,128)}, u32[]{:S(2)}) copy-start(f32[1,384]{1,0:T(1,128)} %get-tuple-element.153.skip_ref) | copy-start | bytes 4612
  775.6 21.1 %copy-start.33 = (f32[1,384]{1,0:T(1,128)S(1)}, f32[1,384]{1,0:T(1,128)}, u32[]{:S(2)}) copy-start(f32[1,384]{1,0:T(1,128)} %get-tuple-element.181.dtb_ref) | copy-start | bytes 4612
  829.9 100.4 %all-reduce.42.cloned.1.call-start = ((), (), s32[]{:S(2)}) async-start(), calls=%async_computation.24 | async-start | bytes 473088 | tf_op jit(solution)/shard_map/psum | solution.py:444
  834.7 31.3 %copy-start.12 = (f32[768,384]{1,0:T(8,128)S(1)}, f32[768,384]{1,0:T(8,128)}, u32[]{:S(2)}) copy-start(f32[768,384]{1,0:T(8,128)} %copy-done.11) | copy-start | bytes 3538948
  834.7 31.3 %copy-start.97 = (f32[768]{0:T(1024)S(1)}, f32[768]{0:T(1024)}, u32[]{:S(2)}) copy-start(f32[768]{0:T(1024)} %get-tuple-element.149) | copy-start | bytes 9220
  834.7 31.3 %copy-start.99 = (f32[768]{0:T(1024)S(1)}, f32[768]{0:T(1024)}, u32[]{:S(2)}) copy-start(f32[768]{0:T(1024)} %get-tuple-element.150) | copy-start | bytes 9220
  834.7 31.3 %copy-start.101 = (f32[768]{0:T(1024)S(1)}, f32[768]{0:T(1024)}, u32[]{:S(2)}) copy-start(f32[768]{0:T(1024)} %get-tuple-element.151) | copy-start | bytes 9220
  874.2 135.1 %all-reduce.44.cloned.1.call-start = ((), (), s32[]{:S(2)}) async-start(), calls=%async_computation.25 | async-start | bytes 7077888 | tf_op jit(solution)/shard_map/psum | solution.py:444
  876.5 164.4 %reduce-scatter.11.cloned.1.call-start = ((), (), s32[]{:S(2)}) async-start(), calls=%async_computation.23 | async-start | bytes 1474560 | tf_op jit(solution)/shard_map/reduce_scatter | solution.py:329
  1012.3 28.6 %copy-start.107 = (f32[768]{0:T(1024)S(1)}, f32[768]{0:T(1024)}, u32[]{:S(2)}) copy-start(f32[768]{0:T(1024)} %copy-done.106) | copy-start | bytes 9220
  1012.3 28.6 %copy-start.143 = (f32[192]{0:T(256)S(1)}, f32[192]{0:T(256)}, u32[]{:S(2)}) copy-start(f32[192]{0:T(256)} %copy-done.142) | copy-start | bytes 2308
  1012.3 71.6 %copy-start.174 = (f32[192]{0:T(256)S(1)}, f32[192]{0:T(256)}, u32[]{:S(2)}) copy-start(f32[192]{0:T(256)} %get-tuple-element.156) | copy-start | bytes 2308
  1014.8 69.1 %copy-start.74 = (f32[192,768]{1,0:T(8,128)S(1)}, f32[192,768]{1,0:T(8,128)}, u32[]{:S(2)}) copy-start(f32[192,768]{1,0:T(8,128)} %get-tuple-element.119) | copy-start | bytes 1769476
  (171 other events, 512.7 us)
Sparse Core Ops, SparseCore 0:
  12.9 33.1 all-gather.4
  51.5 33.9 all-reduce.33
  105.8 28.8 reduce-scatter.4
  230.3 30.4 all-gather.6
  267.2 33.9 all-reduce.35
  323.6 28.8 reduce-scatter.6
  524.5 30.4 all-gather.8
  591.7 33.9 all-reduce.37
  637.9 28.8 reduce-scatter.8
  763.0 30.3 all-gather.10
  830.0 33.9 all-reduce.39
  874.4 55.9 all-reduce.41
  934.5 74.8 all-reduce.43
  1011.6 29.2 reduce-scatter.10

commit v2 on v1

v2 whole, which is shorter than its diff:
```python
import functools
import jax
import jax.numpy as jnp
from jax import lax
from jax.experimental import pallas as pl
from jax.experimental.pallas import tpu as pltpu
from jax.sharding import PartitionSpec as P

STATE = 16
DT_RANK = 48
LANES = 128
CHUNK = 128
LOG2E = 1.4426950408889634
RESET = 1.0e6
PROJ = DT_RANK + 2 * STATE
CONV = 4
dt_most = 0.05
epsilon = 1e-05
highest = lax.Precision.HIGHEST
MESH = pl.DeviceIdType.MESH
F32, BF16 = jnp.float32, jnp.bfloat16


def sigmoid(v):
    return 1.0 / (1.0 + jnp.exp(-v))


def dot(a, b):
    return jnp.dot(a, b, preferred_element_type=F32)


def dot_nt(a, b):
    return lax.dot_general(a, b, (((1,), (1,)), ((), ())), preferred_element_type=F32)


def dot_tn(a, b):
    return lax.dot_general(a, b, (((0,), (0,)), ((), ())), preferred_element_type=F32)


def spread_matrix():
    rows = lax.broadcasted_iota(jnp.int32, (STATE, STATE * LANES), 0)
    cols = lax.broadcasted_iota(jnp.int32, (STATE, STATE * LANES), 1)
    return (rows == cols // LANES).astype(BF16)


def put(ref, value):
    for j in range(ref.shape[0]):
        ref[j] = value[:, j * LANES : (j + 1) * LANES]


def spread_rows(proj, spread, out_ref):
    wide = dot_tn(proj, spread)
    for n in range(STATE):
        out_ref[pl.ds(n, CHUNK, stride=STATE), :] = wide[:, n * LANES : (n + 1) * LANES]


def scan_fwd_kernel(l, xs_ref, zg_ref, proj_ref, since_ref, dtw_ref, dtb_ref, alog_ref, skip_ref, spread_ref,
                    gated_ref, ys_ref, hck_ref,
                    h_ref, dm_ref, dx_ref, bx_ref, cx_ref, yq_ref):
    groups = xs_ref.shape[1] // LANES

    @pl.when(pl.program_id(0) == 0)
    def _():
        h_ref[...] = jnp.zeros_like(h_ref)

    hck_ref[0] = h_ref[...]
    proj = proj_ref[...]
    xs = xs_ref[...]
    delta = dt_most * sigmoid(dot_tn(proj[:DT_RANK], dtw_ref[l]) + dtb_ref[l : l + 1, :])
    put(dm_ref, delta + RESET * (since_ref[...] == 0).astype(F32))
    put(dx_ref, delta * xs)
    spread_rows(proj[DT_RANK : DT_RANK + STATE], spread_ref[...], bx_ref)
    spread_rows(proj[DT_RANK + STATE :], spread_ref[...], cx_ref)
    rate = -LOG2E * jnp.exp(alog_ref[l])
    rates = [rate[:, j * LANES : (j + 1) * LANES] for j in range(groups)]

    def step(g, hs):
        hs = list(hs)
        t0 = pl.multiple_of(g * 8, 8)
        for i in range(8):
            t = t0 + i
            r0 = pl.multiple_of(t * STATE, STATE)
            b = bx_ref[pl.ds(r0, STATE), :]
            c = cx_ref[pl.ds(r0, STATE), :]
            q0 = pl.multiple_of(t * 8, 8)
            for j in range(groups):
                lanes = slice(j * LANES, (j + 1) * LANES)
                dec = jnp.exp2(dm_ref[j, pl.ds(t, 1), :] * rates[j])
                hs[j] = dec * hs[j] + dx_ref[j, pl.ds(t, 1), :] * b
                q = c * hs[j]
                yq_ref[j, pl.ds(q0, 8), :] = q[:8] + q[8:]
        return tuple(hs)

    hs = lax.fori_loop(0, CHUNK // 8, step, tuple(h_ref[:, j * LANES : (j + 1) * LANES] for j in range(groups)))
    for j in range(groups):
        h_ref[:, j * LANES : (j + 1) * LANES] = hs[j]
    zg = zg_ref[...]
    for j in range(groups):
        lanes = slice(j * LANES, (j + 1) * LANES)
        y = skip_ref[l : l + 1, lanes] * xs[:, lanes]
        for k in range(8):
            y = y + yq_ref[j, pl.ds(k, CHUNK, stride=8), :]
        ys_ref[:, lanes] = y
        z = zg[:, lanes]
        gated_ref[:, lanes] = (y * z * sigmoid(z)).astype(BF16)


def scan_fwd(l, xs, zg, proj, since, dtw, dtb, alog, skip, spread):
    rows, ch = xs.shape
    steps = rows // CHUNK
    row = lambda w: pl.BlockSpec((CHUNK, w), lambda i: (i, 0))
    full = lambda s: pl.BlockSpec(s, lambda i: (0,) * len(s))
    return pl.pallas_call(
        functools.partial(scan_fwd_kernel, l),
        grid=(steps,),
        out_shape=[
            jax.ShapeDtypeStruct((rows, ch), BF16),
            jax.ShapeDtypeStruct((rows, ch), F32),
            jax.ShapeDtypeStruct((steps, STATE, ch), F32),
        ],
        in_specs=[row(ch), row(ch), pl.BlockSpec((PROJ, CHUNK), lambda i: (0, i)), row(1)]
        + [full(v.shape) for v in (dtw, dtb, alog, skip, spread)],
        out_specs=[row(ch), row(ch), pl.BlockSpec((1, STATE, ch), lambda i: (i, 0, 0))],
        scratch_shapes=[
            pltpu.VMEM((STATE, ch), F32),
            pltpu.VMEM((ch // LANES, CHUNK, LANES), F32),
            pltpu.VMEM((ch // LANES, CHUNK, LANES), F32),
            pltpu.VMEM((CHUNK * STATE, LANES), F32),
            pltpu.VMEM((CHUNK * STATE, LANES), F32),
            pltpu.VMEM((ch // LANES, CHUNK * 8, LANES), F32),
        ],
        compiler_params=pltpu.CompilerParams(vmem_limit_bytes=48 << 20),
        name="scan_fwd",
    )(xs, zg, proj, since, dtw, dtb, alog, skip, spread)


def scan_bwd_kernel(l, xs_ref, zg_ref, proj_ref, since_ref, ys_ref, gg_ref, hck_ref, dtw_ref, dtb_ref, alog_ref, skip_ref, spread_ref,
                    gxs_ref, gzg_ref, gproj_ref, gdtw_ref, gdtb_ref, galog_ref, gskip_ref,
                    a_ref, dm_ref, dx_ref, dl_ref, gy_ref, bx_ref, cx_ref, h_ref, dec_ref, pq_ref, gq_ref, gb_ref, gc_ref):
    groups = xs_ref.shape[1] // LANES
    cols = [slice(j * LANES, (j + 1) * LANES) for j in range(groups)]

    @pl.when(pl.program_id(0) == 0)
    def _():
        a_ref[...] = jnp.zeros_like(a_ref)
        gdtw_ref[...] = jnp.zeros_like(gdtw_ref)
        gdtb_ref[...] = jnp.zeros_like(gdtb_ref)
        galog_ref[...] = jnp.zeros_like(galog_ref)
        gskip_ref[...] = jnp.zeros_like(gskip_ref)

    proj = proj_ref[...]
    xs = xs_ref[...]
    delta = dt_most * sigmoid(dot_tn(proj[:DT_RANK], dtw_ref[l]) + dtb_ref[l : l + 1, :])
    put(dl_ref, delta)
    put(dm_ref, delta + RESET * (since_ref[...] == 0).astype(F32))
    put(dx_ref, delta * xs)
    zg = zg_ref[...]
    sz = sigmoid(zg)
    gg = gg_ref[...]
    gy = gg * (zg * sz)
    put(gy_ref, gy)
    gzg_ref[...] = (gg * ys_ref[...] * (sz * (1.0 + zg * (1.0 - sz)))).astype(BF16)
    gskip_ref[...] += jnp.sum(gy * xs, axis=0, keepdims=True)
    spread_rows(proj[DT_RANK : DT_RANK + STATE], spread_ref[...], bx_ref)
    spread_rows(proj[DT_RANK + STATE :], spread_ref[...], cx_ref)
    rate = -jnp.exp(alog_ref[l])
    rates2 = [LOG2E * rate[:, c] for c in cols]
    rates = [rate[:, c] for c in cols]

    for j in range(groups):
        h_ref[j, :STATE, :] = hck_ref[0][:, cols[j]]

    def again(g, hs):
        hs = list(hs)
        t0 = pl.multiple_of(g * 8, 8)
        for i in range(8):
            t = t0 + i
            r0 = pl.multiple_of(t * STATE, STATE)
            r1 = pl.multiple_of(t * STATE + STATE, STATE)
            b = bx_ref[pl.ds(r0, STATE), :]
            for j in range(groups):
                dec = jnp.exp2(dm_ref[j, pl.ds(t, 1), :] * rates2[j])
                hs[j] = dec * hs[j] + dx_ref[j, pl.ds(t, 1), :] * b
                dec_ref[j, pl.ds(r0, STATE), :] = dec
                h_ref[j, pl.ds(r1, STATE), :] = hs[j]
        return tuple(hs)

    last = lax.fori_loop(0, CHUNK // 8, again, tuple(hck_ref[0][:, c] for c in cols))

    def back(g, carry):
        carry = [list(c) for c in carry]
        aa, hs, acc = carry
        t0 = pl.multiple_of(CHUNK - 8 - g * 8, 8)
        for i in reversed(range(8)):
            t = t0 + i
            r0 = pl.multiple_of(t * STATE, STATE)
            q0 = pl.multiple_of(t * 8, 8)
            b = bx_ref[pl.ds(r0, STATE), :]
            c = cx_ref[pl.ds(r0, STATE), :]
            gb, gc = None, None
            for j in range(groups):
                gyj = gy_ref[j, pl.ds(t, 1), :]
                a = c * gyj + aa[j]
                dec = dec_ref[j, pl.ds(r0, STATE), :]
                before = h_ref[j, pl.ds(r0, STATE), :]
                carry_a = dec * a
                p = carry_a * before * rates[j]
                ab = a * b
                pq_ref[j, pl.ds(q0, 8), :] = p[:8] + p[8:]
                gq_ref[j, pl.ds(q0, 8), :] = ab[:8] + ab[8:]
                acc[j] = acc[j] + p * dl_ref[j, pl.ds(t, 1), :]
                gbj = a * dx_ref[j, pl.ds(t, 1), :]
                gcj = gyj * hs[j]
                gb = gbj if gb is None else gb + gbj
                gc = gcj if gc is None else gc + gcj
                aa[j] = carry_a
                hs[j] = before
            gb_ref[pl.ds(r0, STATE), :] = gb
            gc_ref[pl.ds(r0, STATE), :] = gc
        return tuple(tuple(c) for c in carry)

    aa, _, acc = lax.fori_loop(
        0, CHUNK // 8, back,
        (tuple(a_ref[:, c] for c in cols), last, tuple(jnp.zeros((STATE, LANES), F32) for _ in cols)))
    for j in range(groups):
        a_ref[:, cols[j]] = aa[j]
        galog_ref[:, cols[j]] += acc[j]

    skip = skip_ref[l : l + 1, :]
    gdts = []
    for j in range(groups):
        psum = pq_ref[j, pl.ds(0, CHUNK, stride=8), :]
        gsum = gq_ref[j, pl.ds(0, CHUNK, stride=8), :]
        for k in range(1, 8):
            psum = psum + pq_ref[j, pl.ds(k, CHUNK, stride=8), :]
            gsum = gsum + gq_ref[j, pl.ds(k, CHUNK, stride=8), :]
        dl = delta[:, cols[j]]
        gdelta = psum + xs[:, cols[j]] * gsum
        gxs_ref[:, cols[j]] = dl * gsum + skip[:, cols[j]] * gy[:, cols[j]]
        gdts.append(gdelta * dl * (1.0 - dl * (1.0 / dt_most)))
    gdt = jnp.concatenate(gdts, axis=1)
    gdtb_ref[...] += jnp.sum(gdt, axis=0, keepdims=True)
    gdt_low = gdt.astype(BF16)
    gdtw_ref[...] += dot(proj[:DT_RANK], gdt_low)
    gproj_ref[:DT_RANK, :] = dot_nt(dtw_ref[l], gdt_low)
    wide_b = jnp.concatenate([gb_ref[pl.ds(n, CHUNK, stride=STATE), :].astype(BF16) for n in range(STATE)], axis=1)
    gproj_ref[DT_RANK : DT_RANK + STATE, :] = dot_nt(spread_ref[...], wide_b)
    wide_c = jnp.concatenate([gc_ref[pl.ds(n, CHUNK, stride=STATE), :].astype(BF16) for n in range(STATE)], axis=1)
    gproj_ref[DT_RANK + STATE :, :] = dot_nt(spread_ref[...], wide_c)


def scan_bwd(l, xs, zg, proj, since, ys, gg, hck, dtw, dtb, alog, skip, spread):
    rows, ch = xs.shape
    steps = rows // CHUNK
    row = lambda w: pl.BlockSpec((CHUNK, w), lambda i: (steps - 1 - i, 0))
    full = lambda s: pl.BlockSpec(s, lambda i: (0,) * len(s))
    big = lambda: pltpu.VMEM((CHUNK * STATE, LANES), F32)
    g = ch // LANES
    return pl.pallas_call(
        functools.partial(scan_bwd_kernel, l),
        grid=(steps,),
        out_shape=[
            jax.ShapeDtypeStruct((rows, ch), F32),
            jax.ShapeDtypeStruct((rows, ch), BF16),
            jax.ShapeDtypeStruct((PROJ, rows), F32),
            jax.ShapeDtypeStruct((DT_RANK, ch), F32),
            jax.ShapeDtypeStruct((1, ch), F32),
            jax.ShapeDtypeStruct((STATE, ch), F32),
            jax.ShapeDtypeStruct((1, ch), F32),
        ],
        in_specs=[row(ch), row(ch), pl.BlockSpec((PROJ, CHUNK), lambda i: (0, steps - 1 - i)), row(1), row(ch), row(ch),
                  pl.BlockSpec((1, STATE, ch), lambda i: (steps - 1 - i, 0, 0))]
        + [full(v.shape) for v in (dtw, dtb, alog, skip, spread)],
        out_specs=[row(ch), row(ch), pl.BlockSpec((PROJ, CHUNK), lambda i: (0, steps - 1 - i)), full((DT_RANK, ch)), full((1, ch)), full((STATE, ch)), full((1, ch))],
        scratch_shapes=[
            pltpu.VMEM((STATE, ch), F32),
            pltpu.VMEM((ch // LANES, CHUNK, LANES), F32),
            pltpu.VMEM((ch // LANES, CHUNK, LANES), F32),
            pltpu.VMEM((ch // LANES, CHUNK, LANES), F32),
            pltpu.VMEM((ch // LANES, CHUNK, LANES), F32),
            big(), big(),
            pltpu.VMEM((g, CHUNK * STATE + STATE, LANES), F32),
            pltpu.VMEM((g, CHUNK * STATE, LANES), F32),
            pltpu.VMEM((g, CHUNK * 8, LANES), F32),
            pltpu.VMEM((g, CHUNK * 8, LANES), F32),
            big(), big(),
        ],
        compiler_params=pltpu.CompilerParams(vmem_limit_bytes=48 << 20),
        name="scan_bwd",
    )(xs, zg, proj, since, ys, gg, hck, dtw, dtb, alog, skip, spread)


def rms_inverse(values):
    return lax.rsqrt(jnp.mean(values * values, axis=-1, keepdims=True) + epsilon)


def norm_back(values, inverse, gain, grad):
    scaled = grad * gain
    pulled = inverse * scaled - values * (inverse * inverse * inverse) * jnp.mean(scaled * values, axis=-1, keepdims=True)
    return pulled, jnp.sum(grad * values * inverse, axis=0, keepdims=True)


GELU_A, GELU_B = 0.7978845608028654, 0.044715


def gelu(v):
    return 0.5 * v * (1.0 + jnp.tanh(GELU_A * (v + GELU_B * v * v * v)))


def gelu_slope(v):
    square = v * v
    t = jnp.tanh(GELU_A * v * (1.0 + GELU_B * square))
    return 0.5 * (1.0 + t) + 0.5 * v * (1.0 - t * t) * GELU_A * (1.0 + 3.0 * GELU_B * square)


def by_lane(m, values):
    picked = jnp.int32(values[0])
    for k in range(1, len(values)):
        picked = jnp.where(m == k, jnp.int32(values[k]), picked)
    return picked


def nearest_first(m, lanes):
    orders = [sorted((s for s in range(lanes) if s != k), key=lambda s: (abs(s - k), s)) for k in range(lanes)]
    return [by_lane(m, [order[i] for order in orders]) for i in range(lanes - 1)]


def chain_order(m, lanes):
    def due(k, s):
        return (lanes - 1 - s) + k if s > k else s + (lanes - 1 - k)

    orders = [sorted((s for s in range(lanes) if s != k), key=lambda s: (due(k, s), s)) for k in range(lanes)]
    return [by_lane(m, [order[i] for order in orders]) for i in range(lanes - 1)]


def greet(d, m, lanes, peers, across):
    barrier = pltpu.get_barrier_semaphore()
    if across:
        for k in range(1, lanes):
            pl.semaphore_signal(barrier, inc=1, device_id=(d, lax.rem(m + k, lanes)), device_id_type=MESH)
        for k in range(1, peers):
            pl.semaphore_signal(barrier, inc=1, device_id=(lax.rem(d + k, peers), m), device_id_type=MESH)
        pl.semaphore_wait(barrier, lanes + peers - 2)
    else:

        @pl.when(m > 0)
        def _():
            pl.semaphore_signal(barrier, inc=1, device_id=(d, m - 1), device_id_type=MESH)

        @pl.when(m < lanes - 1)
        def _():
            pl.semaphore_signal(barrier, inc=1, device_id=(d, m + 1), device_id_type=MESH)

        pl.semaphore_wait(barrier, jnp.where(m > 0, 1, 0) + jnp.where(m < lanes - 1, 1, 0))


class LineGather:
    def __init__(self, buf, send, recv, d, m, lanes):
        self.buf, self.send, self.recv, self.d, self.m, self.lanes = buf, send, recv, d, m, lanes
        self.order = nearest_first(m, lanes)

    def copy(self, s, up):
        return pltpu.make_async_remote_copy(
            src_ref=self.buf.at[s], dst_ref=self.buf.at[s], send_sem=self.send.at[0 if up else 1, s],
            recv_sem=self.recv.at[s], device_id=(self.d, self.m + 1 if up else self.m - 1), device_id_type=MESH,
        )

    def start(self):
        @pl.when(self.m < self.lanes - 1)
        def _():
            self.copy(self.m, True).start()

        @pl.when(self.m > 0)
        def _():
            self.copy(self.m, False).start()

    def arrive(self, i):
        s, m = self.order[i], self.m
        self.copy(s, True).wait_recv()

        @pl.when((s < m) & (m < self.lanes - 1))
        def _():
            self.copy(s, True).start()

        @pl.when((s > m) & (m > 0))
        def _():
            self.copy(s, False).start()

        return s

    def finish(self):
        for s in range(self.lanes):

            @pl.when((s <= self.m) & (self.m < self.lanes - 1))
            def _():
                self.copy(s, True).wait_send()

            @pl.when((s >= self.m) & (self.m > 0))
            def _():
                self.copy(s, False).wait_send()


class LineReduce:
    def __init__(self, stage, inbox, send, recv, d, m, lanes):
        self.stage, self.inbox, self.send, self.recv = stage, inbox, send, recv
        self.d, self.m, self.lanes = d, m, lanes
        self.order = chain_order(m, lanes)

    def copy(self, s):
        up = s > self.m
        side = jnp.where(up, 0, 1)
        return pltpu.make_async_remote_copy(
            src_ref=self.stage.at[s], dst_ref=self.inbox.at[side, s], send_sem=self.send.at[s],
            recv_sem=self.recv.at[side, s], device_id=(self.d, jnp.where(up, self.m + 1, self.m - 1)), device_id_type=MESH,
        )

    def push(self, s, term):
        up = s > self.m
        side = jnp.where(up, 0, 1)
        has_more = jnp.where(up, self.m, self.lanes - 1 - self.m) > 0

        @pl.when(has_more)
        def _():
            self.copy(s).wait_recv()
            self.stage[s] = (term + self.inbox[side, s].astype(F32)).astype(BF16)

        @pl.when(jnp.logical_not(has_more))
        def _():
            self.stage[s] = term.astype(BF16)

        self.copy(s).start()

    def total(self, own_ref):
        m = self.m

        def wait(side):
            pltpu.make_async_remote_copy(
                src_ref=self.stage.at[m], dst_ref=self.inbox.at[side, m], send_sem=self.send.at[m],
                recv_sem=self.recv.at[side, m], device_id=(self.d, m), device_id_type=MESH,
            ).wait_recv()

        @pl.when(m > 0)
        def _():
            wait(0)
            own_ref[...] += self.inbox[0, m].astype(F32)

        @pl.when(m < self.lanes - 1)
        def _():
            wait(1)
            own_ref[...] += self.inbox[1, m].astype(F32)

    def finish(self):
        for s in self.order:
            self.copy(s).wait_send()


PARTS = 2


def line_sum(part, stage, inbox, send, recv, out, d, m, lanes, between=lambda: None):
    width = part.shape[1] // PARTS

    def copy(side, b):
        return pltpu.make_async_remote_copy(
            src_ref=stage.at[side, b], dst_ref=inbox.at[side, b], send_sem=send.at[side, b], recv_sem=recv.at[side, b],
            device_id=(d, m + 1 if side == 0 else m - 1), device_id_type=MESH,
        )

    def step(side, b):
        has_source = m > 0 if side == 0 else m < lanes - 1
        has_target = m < lanes - 1 if side == 0 else m > 0
        cols = slice(b * width, (b + 1) * width)

        @pl.when(has_source)
        def _():
            copy(side, b).wait_recv()

        @pl.when(jnp.logical_not(has_source))
        def _():
            inbox[side, b] = jnp.zeros(inbox.shape[2:], BF16)

        @pl.when(has_target)
        def _():
            stage[side, b] = (part[:, cols] + inbox[side, b].astype(F32)).astype(BF16)
            copy(side, b).start()

    low = 2 * m < lanes

    def both(first):
        def run(side):
            for b in range(PARTS):
                step(side, b)

        @pl.when(low)
        def _():
            run(0 if first else 1)

        @pl.when(jnp.logical_not(low))
        def _():
            run(1 if first else 0)

    both(True)
    between()
    both(False)
    for b in range(PARTS):
        cols = slice(b * width, (b + 1) * width)
        out[:, cols] = (part[:, cols] + inbox[0, b].astype(F32) + inbox[1, b].astype(F32)).astype(BF16)

    def finish():
        for b in range(PARTS):

            @pl.when(m < lanes - 1)
            def _():
                copy(0, b).wait_send()

            @pl.when(m > 0)
            def _():
                copy(1, b).wait_send()

    return finish


def vmem(count):
    return [pl.BlockSpec(memory_space=pltpu.VMEM)] * count


def f32(*shape):
    return jax.ShapeDtypeStruct(shape, F32)


def bf16(*shape):
    return jax.ShapeDtypeStruct(shape, BF16)


def dma(*shape):
    return pltpu.SemaphoreType.DMA(shape)


def hbm(count):
    return [pl.BlockSpec(memory_space=pl.ANY)] * count


def fetch(pairs, sem):
    copies = [pltpu.make_async_copy(src, dst, sem.at[i]) for i, (src, dst) in enumerate(pairs)]
    for copy in copies:
        copy.start()
    return copies


def params(cid):
    return pltpu.CompilerParams(collective_id=cid, has_side_effects=True, vmem_limit_bytes=56 << 20)


CONV_ROWS = 128
HEAD = 8


def conv_window(padded_ref, since_ref, taps, bias, base):
    window = padded_ref[pl.ds(base, CONV_ROWS + HEAD), :]
    since = since_ref[pl.ds(base, CONV_ROWS), :]
    shifted = [window[HEAD:]]
    for j in range(1, CONV):
        shifted.append(window[HEAD - j : HEAD - j + CONV_ROWS] * (since >= j).astype(F32))
    pre = bias
    for j in range(CONV):
        pre = pre + taps[CONV - 1 - j : CONV - j, :] * shifted[j]
    return pre, shifted


def in_kernel(l, lanes, act_ref, gain_ref, taps_ref, bias_ref, since_ref, xp_ref, win_hbm,
              whole_ref, conv_ref, gate_ref, xs_ref, proj_ref,
              win_ref, part_ref, stage_ref, inbox_ref, gsend, grecv, psend, precv, wsem):
    d, m = lax.axis_index("dp"), lax.axis_index("mp")
    rows = act_ref.shape[0]
    (weights,) = fetch([(win_hbm.at[l], win_ref)], wsem)
    greet(d, m, lanes, 0, False)
    act = act_ref[...].astype(F32)
    whole_ref[m] = (act * rms_inverse(act) * gain_ref[l : l + 1, :]).astype(BF16)
    gather = LineGather(whole_ref, gsend, grecv, d, m, lanes)
    gather.start()
    conv_ref[:HEAD, :] = jnp.zeros((HEAD, conv_ref.shape[1]), F32)
    weights.wait()

    def project(s):
        u = whole_ref[s]
        conv_ref[pl.ds(pl.multiple_of(s * rows + HEAD, 8), rows), :] = dot(u, win_ref[0])
        gate_ref[pl.ds(pl.multiple_of(s * rows, 8), rows), :] = dot(u, win_ref[1])

    project(m)
    for i in range(lanes - 1):
        project(gather.arrive(i))
    taps, bias = taps_ref[l], bias_ref[l : l + 1, :]

    def conv_step(c, carry):
        base = pl.multiple_of(c * CONV_ROWS, CONV_ROWS)
        pre, _ = conv_window(conv_ref, since_ref, taps, bias, base)
        xs = pre * sigmoid(pre)
        xs_ref[pl.ds(base, CONV_ROWS), :] = xs
        part_ref[:, pl.ds(base, CONV_ROWS)] = dot_nt(xp_ref[l], xs.astype(BF16))
        return carry

    lax.fori_loop(0, lanes * rows // CONV_ROWS, conv_step, 0)
    finish = line_sum(part_ref, stage_ref, inbox_ref, psend, precv, proj_ref, d, m, lanes)
    gather.finish()
    finish()


def in_block(l, lanes, act, gain, taps, bias, since, xp, win):
    rows, width = act.shape
    ch, total = win.shape[3], rows * lanes
    return pl.pallas_call(
        functools.partial(in_kernel, l, lanes),
        out_shape=[bf16(lanes, rows, width), f32(total + HEAD, ch), f32(total, ch), f32(total, ch), bf16(PROJ, total)],
        in_specs=vmem(6) + hbm(1),
        out_specs=vmem(5),
        scratch_shapes=[
            pltpu.VMEM(win.shape[1:], BF16),
            pltpu.VMEM((PROJ, total), F32),
            pltpu.VMEM((2, PARTS, PROJ, total // PARTS), BF16),
            pltpu.VMEM((2, PARTS, PROJ, total // PARTS), BF16),
            dma(2, lanes), dma(lanes), dma(2, PARTS), dma(2, PARTS), dma(1),
        ],
        compiler_params=params(l),
        name="mamba_in",
    )(act, gain, taps, bias, since, xp, win)


class Experts:
    def __init__(self, d, m, lanes, peers, rows_ref, into_ref, pack_ref, slots_ref, part_ref, back_ref, stage_ref, inbox_ref,
                 gsend, grecv, dsend, drecv, bsend, brecv, rsend, rrecv):
        self.d, self.m, self.lanes, self.peers = d, m, lanes, peers
        self.rows, self.into = rows_ref, into_ref
        self.pack, self.slots, self.part, self.back, self.stage, self.inbox = pack_ref, slots_ref, part_ref, back_ref, stage_ref, inbox_ref
        self.dsend, self.drecv, self.bsend, self.brecv, self.rsend, self.rrecv = dsend, drecv, bsend, brecv, rsend, rrecv
        self.cap = pack_ref.shape[1] // peers
        self.gather = LineGather(rows_ref, gsend, grecv, d, m, lanes)

    def at(self, e):
        return pl.ds(pl.multiple_of(e * self.cap, self.cap), self.cap)

    def hop(self, src, dst, send, recv, s, k):
        other = lax.rem(self.d + k, self.peers)
        return pltpu.make_async_remote_copy(
            src_ref=src.at[s, self.at(other)], dst_ref=dst.at[s, self.at(self.d)], send_sem=send.at[s, k - 1],
            recv_sem=recv.at[s, k - 1], device_id=(other, self.m), device_id_type=MESH,
        )

    def across(self, src, dst, send, recv, s):
        for k in range(1, self.peers):
            self.hop(src, dst, send, recv, s, k).start()
        dst[s, self.at(self.d)] = src[s, self.at(self.d)]

    def dispatch(self, s):
        self.pack[s] = dot(self.into[s], self.rows[s]).astype(BF16)
        self.across(self.pack, self.slots, self.dsend, self.drecv, s)

    def answer(self, s, expert):
        for k in range(1, self.peers):
            self.hop(self.pack, self.slots, self.dsend, self.drecv, s, k).wait_recv()
        self.part[s] = expert(s)
        self.across(self.part, self.back, self.bsend, self.brecv, s)

    def home(self, s):
        return pltpu.make_async_remote_copy(
            src_ref=self.stage.at[s], dst_ref=self.inbox.at[self.m], send_sem=self.rsend.at[s], recv_sem=self.rrecv.at[self.m],
            device_id=(self.d, s), device_id_type=MESH,
        )

    def combine(self, s):
        for k in range(1, self.peers):
            self.hop(self.part, self.back, self.bsend, self.brecv, s, k).wait_recv()
        return dot_tn(self.into[s], self.back[s])

    def combine_away(self, s):
        self.stage[s] = self.combine(s).astype(BF16)
        self.home(s).start()

    def run(self, expert, own_ref, meanwhile):
        order = [self.m]
        self.gather.start()
        self.dispatch(self.m)
        for i in range(self.lanes - 1):
            s = self.gather.arrive(i)
            self.dispatch(s)
            self.answer(order[-1], expert)
            if i == 1:
                own_ref[...] = self.combine(self.m)
            if i > 1:
                self.combine_away(order[-2])
            order.append(s)
        self.answer(order[-1], expert)
        self.combine_away(order[-2])
        self.combine_away(order[-1])
        meanwhile()
        for s in order[1:]:
            pltpu.make_async_remote_copy(
                src_ref=self.stage.at[s], dst_ref=self.inbox.at[s], send_sem=self.rsend.at[s], recv_sem=self.rrecv.at[s],
                device_id=(self.d, s), device_id_type=MESH,
            ).wait_recv()
            own_ref[...] += self.inbox[s].astype(F32)
        self.gather.finish()
        for s in order:
            for k in range(1, self.peers):
                self.hop(self.pack, self.slots, self.dsend, self.drecv, s, k).wait_send()
                self.hop(self.part, self.back, self.bsend, self.brecv, s, k).wait_send()
        for s in order[1:]:
            self.home(s).wait_send()


def expert_scratch(lanes, peers, rows, width, slots):
    return [
        pltpu.VMEM((lanes, rows, width), BF16),
        pltpu.VMEM((lanes, slots, width), BF16),
        pltpu.VMEM((lanes, slots, width), BF16),
        pltpu.VMEM((lanes, slots, width), BF16),
        pltpu.VMEM((lanes, rows, width), BF16),
        pltpu.VMEM((lanes, rows, width), BF16),
        pltpu.VMEM((rows, width), F32),
        dma(2, lanes), dma(lanes), dma(lanes, peers - 1), dma(lanes, peers - 1), dma(lanes, peers - 1), dma(lanes, peers - 1),
        dma(lanes), dma(lanes),
    ]


def mid_kernel(l, lanes, peers, experts, act_ref, gated_ref, gain_ref, router_ref, choose_ref, place_ref, wout_hbm, wup_hbm, wdown_hbm,
               middle_ref, chance_ref, into_ref, slots_ref, hidden_ref, active_ref, picked_ref, next_ref,
               rows_ref, pack_ref, part_ref, back_ref, stage_ref, inbox_ref, own_ref,
               gsend, grecv, dsend, drecv, bsend, brecv, rsend, rrecv, cstage_ref, cinbox_ref, csend, crecv,
               places_ref, isend, irecv, wout_ref, wup_ref, wdown_ref, wsem):
    d, m = lax.axis_index("dp"), lax.axis_index("mp")
    wout, wup, wdown = fetch([(wout_hbm.at[l], wout_ref), (wup_hbm.at[l, 0], wup_ref), (wdown_hbm.at[l, 0], wdown_ref)], wsem)
    greet(d, m, lanes, peers, True)
    places_ref[m] = place_ref[...]
    places = LineGather(places_ref, isend, irecv, d, m, lanes)
    places.start()
    reduce = LineReduce(cstage_ref, cinbox_ref, csend, crecv, d, m, lanes)
    wout.wait()
    for s in reduce.order:
        reduce.push(s, dot(gated_ref[s], wout_ref[...]))
    own_ref[...] = act_ref[...].astype(F32) + dot(gated_ref[m], wout_ref[...])
    slots = into_ref.shape[1]

    def spread_places(s):
        numbers = lax.broadcasted_iota(jnp.int32, (slots, into_ref.shape[2]), 0)
        into_ref[s] = (numbers == places_ref[s][:1, : into_ref.shape[2]]).astype(F32).astype(BF16)

    spread_places(m)
    for i in range(lanes - 1):
        spread_places(places.arrive(i))
    places.finish()
    wup.wait()
    wdown.wait()
    reduce.total(own_ref)
    middle = own_ref[...]
    middle_ref[...] = middle
    normed = middle * rms_inverse(middle) * gain_ref[l : l + 1, :]
    rows_ref[m] = normed.astype(BF16)
    moe = Experts(d, m, lanes, peers, rows_ref, into_ref, pack_ref, slots_ref, part_ref, back_ref, stage_ref, inbox_ref,
                  gsend, grecv, dsend, drecv, bsend, brecv, rsend, rrecv)

    def expert(s):
        hidden = dot(slots_ref[s], wup_ref[...])
        hidden_ref[s] = hidden.astype(BF16)
        active = gelu(hidden).astype(BF16)
        active_ref[s] = active
        return dot(active, wdown_ref[...]).astype(BF16)

    def meanwhile():
        reduce.finish()
        normed = middle_ref[...] * rms_inverse(middle_ref[...]) * gain_ref[l : l + 1, :]
        logits = jnp.dot(normed, router_ref[l], precision=highest, preferred_element_type=F32)
        valid = lax.broadcasted_iota(jnp.int32, logits.shape, 1) < experts
        logits = jnp.where(valid, logits, -1e30)
        raised = jnp.exp(logits - jnp.max(logits, axis=1, keepdims=True))
        chance_ref[...] = raised / jnp.sum(raised, axis=1, keepdims=True)

    moe.run(expert, own_ref, meanwhile)
    picked = own_ref[...].astype(BF16)
    picked_ref[...] = picked
    gate = jnp.sum(chance_ref[...] * choose_ref[...], axis=1, keepdims=True)
    next_ref[...] = middle_ref[...] + gate * picked.astype(F32)


def mid_block(l, lanes, peers, experts, padded, act, gated, gain, router, choose, place, wout, wup, wdown):
    rows, width = act.shape
    slots, ff = experts * padded, wup.shape[3]
    return pl.pallas_call(
        functools.partial(mid_kernel, l, lanes, peers, experts),
        out_shape=[f32(rows, width), f32(rows, LANES), bf16(lanes, slots, rows), bf16(lanes, slots, width), bf16(lanes, slots, ff),
                   bf16(lanes, slots, ff), bf16(rows, width), f32(rows, width)],
        in_specs=vmem(6) + hbm(3),
        out_specs=vmem(8),
        scratch_shapes=expert_scratch(lanes, peers, rows, width, slots)
        + [
            pltpu.VMEM((lanes, rows, width), BF16),
            pltpu.VMEM((2, lanes, rows, width), BF16),
            dma(lanes), dma(2, lanes),
            pltpu.VMEM((lanes, *place.shape), jnp.int32),
            dma(2, lanes), dma(lanes),
            pltpu.VMEM(wout.shape[1:], BF16), pltpu.VMEM(wup.shape[2:], BF16), pltpu.VMEM(wdown.shape[2:], BF16), dma(3),
        ],
        compiler_params=params(2 + l),
        name="mid_forward",
    )(act, gated, gain, router, choose, place, wout, wup, wdown)


def moe_back_kernel(l, lanes, peers, up_ref, chance_ref, choose_ref, picked_ref, middle_ref, gain_ref, router_ref, into_ref,
                    slots_ref, hidden_ref, active_ref, gated_ref, wout_hbm, wup_hbm, wdown_hbm,
                    gmid_ref, gup_ref, gdown_ref, ggated_ref, gwout_ref, gshare_ref,
                    rows_ref, pack_ref, part_ref, back_ref, stage_ref, inbox_ref, own_ref,
                    gsend, grecv, dsend, drecv, bsend, brecv, rsend, rrecv, sgrad_ref, ghid_ref, wide_ref, wsend, wrecv,
                    wout_ref, wup_ref, wdown_ref, wsem):
    d, m = lax.axis_index("dp"), lax.axis_index("mp")
    weights = fetch([(wdown_hbm.at[l, 0], wdown_ref), (wup_hbm.at[l, 0], wup_ref), (wout_hbm.at[l], wout_ref)], wsem)
    greet(d, m, lanes, peers, True)
    chance, choose = chance_ref[...], choose_ref[...]
    gate = jnp.sum(chance * choose, axis=1, keepdims=True)
    rows_ref[m] = (gate * up_ref[...].astype(F32)).astype(BF16)
    for weight in weights:
        weight.wait()
    moe = Experts(d, m, lanes, peers, rows_ref, into_ref, pack_ref, sgrad_ref, part_ref, back_ref, stage_ref, inbox_ref,
                  gsend, grecv, dsend, drecv, bsend, brecv, rsend, rrecv)

    def expert(s):
        grad_active = dot_nt(sgrad_ref[s], wdown_ref[...])
        grad_hidden = (grad_active * gelu_slope(hidden_ref[s].astype(F32))).astype(BF16)
        ghid_ref[s] = grad_hidden
        return dot_nt(grad_hidden, wup_ref[...]).astype(BF16)

    flat = lambda ref: ref[...].reshape(ref.shape[0] * ref.shape[1], ref.shape[2])

    def meanwhile():
        gdown_ref[...] = dot_tn(flat(active_ref), flat(sgrad_ref))
        gup_ref[...] = dot_tn(flat(slots_ref), flat(ghid_ref))

    moe.run(expert, own_ref, meanwhile)
    upstream, middle = up_ref[...].astype(F32), middle_ref[...]
    inverse = rms_inverse(middle)
    gain = gain_ref[l : l + 1, :]
    grad_gate = jnp.sum(upstream * picked_ref[...].astype(F32), axis=1, keepdims=True)
    grad_logit = gate * grad_gate * (choose - chance)
    grad_normed = own_ref[...].astype(BF16).astype(F32) + lax.dot_general(
        grad_logit, router_ref[l], (((1,), (1,)), ((), ())), precision=highest, preferred_element_type=F32)
    pulled, grad_gain = norm_back(middle, inverse, gain, grad_normed)
    grad_middle = upstream + pulled
    gmid_ref[...] = grad_middle
    wide_ref[m] = grad_middle.astype(BF16)
    gather = LineGather(wide_ref, wsend, wrecv, d, m, lanes)
    gather.start()
    grad_router = lax.dot_general(
        grad_logit, middle * inverse * gain, (((0,), (0,)), ((), ())), precision=highest, preferred_element_type=F32)
    experts = gshare_ref.shape[0] - 8
    gshare_ref[:experts, :] = grad_router[:experts]
    gshare_ref[experts:, :] = jnp.broadcast_to(grad_gain, (8, grad_gain.shape[1]))

    def gate_back(s):
        ggated_ref[s] = dot_nt(wide_ref[s], wout_ref[...])

    gate_back(m)
    for i in range(lanes - 1):
        gate_back(gather.arrive(i))
    gwout_ref[...] = dot_tn(flat(gated_ref), flat(wide_ref)).astype(BF16)
    gather.finish()


def moe_back(l, lanes, peers, experts, up, chance, choose, picked, middle, gain, router, into, slots, hidden, active, gated, wout, wup, wdown):
    rows, width = up.shape
    count, ff, ch = into.shape[1], wup.shape[3], wout.shape[1]
    return pl.pallas_call(
        functools.partial(moe_back_kernel, l, lanes, peers),
        out_shape=[f32(rows, width), f32(width, ff), f32(ff, width), f32(lanes, rows, ch), bf16(ch, width), f32(experts + 8, width)],
        in_specs=vmem(12) + hbm(3),
        out_specs=vmem(6),
        scratch_shapes=expert_scratch(lanes, peers, rows, width, count)
        + [
            pltpu.VMEM((lanes, count, width), BF16),
            pltpu.VMEM((lanes, count, ff), BF16),
            pltpu.VMEM((lanes, rows, width), BF16),
            dma(2, lanes), dma(lanes),
            pltpu.VMEM(wout.shape[1:], BF16), pltpu.VMEM(wup.shape[2:], BF16), pltpu.VMEM(wdown.shape[2:], BF16), dma(3),
        ],
        compiler_params=params(4 + l),
        name="moe_backward",
    )(up, chance, choose, picked, middle, gain, router, into, slots, hidden, active, gated, wout, wup, wdown)


class PlaneSum:
    def __init__(self, d, m, peers, mine, pair, half, inbox, result, psend, precv, csend, crecv, gsend, grecv):
        self.m, self.mine, self.pair, self.half, self.inbox, self.result = m, mine, pair, half, inbox, result
        self.psend, self.precv, self.csend, self.crecv, self.gsend, self.grecv = psend, precv, csend, crecv, gsend, grecv
        self.chips = peers // 2
        self.chip, self.core = lax.div(d, 2), lax.rem(d, 2)
        self.rows = mine.shape[0] // 2
        self.block = self.rows // self.chips

    def side(self, core):
        return pl.ds(pl.multiple_of(core * self.rows, 16), self.rows)

    def at(self, chip):
        return pl.ds(pl.multiple_of(chip * self.block, 16), self.block)

    def final(self, chip):
        return pl.ds(pl.multiple_of(self.core * self.rows + chip * self.block, 16), self.block)

    def swap(self, src, dst, i):
        return pltpu.make_async_remote_copy(
            src_ref=src, dst_ref=dst, send_sem=self.psend.at[i], recv_sem=self.precv.at[i],
            device_id=(self.chip * 2 + 1 - self.core, self.m), device_id_type=MESH)

    def first_swap(self):
        return self.swap(self.mine.at[self.side(1 - self.core)], self.pair, 0)

    def last_swap(self):
        return self.swap(self.result.at[self.side(self.core)], self.result.at[self.side(self.core)], 1)

    def other(self, k):
        return lax.rem(self.chip + k, self.chips)

    def scatter(self, k):
        return pltpu.make_async_remote_copy(
            src_ref=self.half.at[self.at(self.other(k))], dst_ref=self.inbox.at[k - 1], send_sem=self.csend.at[k - 1],
            recv_sem=self.crecv.at[k - 1], device_id=(self.other(k) * 2 + self.core, self.m), device_id_type=MESH)

    def gather(self, k):
        return pltpu.make_async_remote_copy(
            src_ref=self.result.at[self.final(self.chip)], dst_ref=self.result.at[self.final(self.chip)], send_sem=self.gsend.at[k - 1],
            recv_sem=self.grecv.at[k - 1], device_id=(self.other(k) * 2 + self.core, self.m), device_id_type=MESH)

    def begin(self):
        self.first_swap().start()

    def second(self):
        self.first_swap().wait_recv()
        self.half[...] = (self.mine[self.side(self.core)].astype(F32) + self.pair[...].astype(F32)).astype(BF16)
        for k in range(1, self.chips):
            self.scatter(k).start()

    def third(self):
        for k in range(1, self.chips):
            self.scatter(k).wait_recv()
        summed = self.half[self.at(self.chip)].astype(F32)
        for k in range(1, self.chips):
            summed = summed + self.inbox[k - 1].astype(F32)
        self.result[self.final(self.chip)] = summed.astype(BF16)
        for k in range(1, self.chips):
            self.gather(k).start()

    def fourth(self):
        for k in range(1, self.chips):
            self.gather(k).wait_recv()
        self.last_swap().start()

    def end(self):
        self.last_swap().wait_recv()

    def finish(self):
        self.first_swap().wait_send()
        self.last_swap().wait_send()
        for k in range(1, self.chips):
            self.scatter(k).wait_send()
            self.gather(k).wait_send()


def plane_scratch(peers, rows, width):
    return [
        pltpu.VMEM((rows, width), BF16),
        pltpu.VMEM((rows // 2, width), BF16),
        pltpu.VMEM((rows // 2, width), BF16),
        pltpu.VMEM((peers // 2 - 1, rows // peers, width), BF16),
        dma(2), dma(2), dma(peers // 2 - 1), dma(peers // 2 - 1), dma(peers // 2 - 1), dma(peers // 2 - 1),
    ]


def exchange(targets, buf, inbox, send, recv):
    copies = [
        pltpu.make_async_remote_copy(src_ref=buf, dst_ref=inbox.at[k], send_sem=send.at[k], recv_sem=recv.at[k],
                                     device_id=target, device_id_type=MESH)
        for k, target in enumerate(targets)
    ]
    for copy in copies:
        copy.start()

    def collect():
        total = buf[...].astype(F32)
        for k, copy in enumerate(copies):
            copy.wait()
            total = total + inbox[k].astype(F32)
        return total

    return collect


def early_rows(width, experts):
    sizes = [width, width, DT_RANK, STATE, 16, experts + 8, experts + 8]
    return [sum(sizes[:i]) for i in range(len(sizes) + 1)]


def late_rows(width):
    sizes = [width, PROJ, 16]
    return [sum(sizes[:i]) for i in range(len(sizes) + 1)]


def whole_blocks(rows, peers):
    return -(-rows // (16 * peers)) * 16 * peers


def in_back_kernel(l, lanes, peers, experts, gpart_ref, gxs_ref, gzg_ref, conv_ref, taps_ref, bias_ref, since_ref, xp_ref, xs_ref, whole_ref,
                   act_ref, gain_ref, gmid_ref, gwout_ref, gshare_ref, gdtw_ref, gdtb_ref, galog_ref, gskip_ref, prior_ref, win_hbm,
                   up_ref, early_ref, late_ref, share_ref, gnorm_ref,
                   stage_ref, inbox_ref, gproj_ref, gpre_ref, gxi_ref, gconv_ref, cstage_ref, cinbox_ref, own_ref, psend, precv, csend, crecv,
                   win_ref, wsem, zbuf_ref, zin_ref, zsend, zrecv, nbuf_ref, nin_ref, nsend, nrecv, nbuf2_ref, nin2_ref, nsend2, nrecv2,
                   *plane):
    d, m = lax.axis_index("dp"), lax.axis_index("mp")
    rows, width = act_ref.shape
    ch = gxs_ref.shape[1]
    total = rows * lanes
    (weights,) = fetch([(win_hbm.at[l], win_ref)], wsem)
    greet(d, m, lanes, peers, True)
    line = [(d, lax.rem(m + k, lanes)) for k in range(1, lanes)]
    half = len(plane) // 2
    emine, lmine = plane[0], plane[half]
    early = PlaneSum(d, m, peers, *plane[:4], early_ref, *plane[4:half])
    late = PlaneSum(d, m, peers, *plane[half : half + 4], late_ref, *plane[half + 4 :])
    whole = whole_ref[...].reshape(total, width)
    at = early_rows(width, experts)
    till = late_rows(width)

    def early_work():
        emine[at[0] : at[1], :] = dot_tn(whole, gzg_ref[...]).astype(BF16)
        for i in range(width // ch):
            emine[at[1] + i * ch : at[1] + (i + 1) * ch, :] = gwout_ref[:, i * ch : (i + 1) * ch]
            emine[at[5 + i] : at[6 + i], :] = gshare_ref[:, i * ch : (i + 1) * ch].astype(BF16)
        emine[at[2] : at[3], :] = gdtw_ref[...].astype(BF16)
        emine[at[3] : at[4], :] = galog_ref[...].astype(BF16)
        emine[at[4] : at[5], :] = jnp.concatenate([gdtb_ref[...], gskip_ref[...], jnp.zeros((14, ch), F32)], axis=0).astype(BF16)
        if at[7] < emine.shape[0]:
            emine[at[7] :, :] = jnp.zeros((emine.shape[0] - at[7], ch), BF16)
        early.begin()

    finish = line_sum(gpart_ref, stage_ref, inbox_ref, psend, precv, gproj_ref, d, m, lanes, early_work)
    taps, bias = taps_ref[l], bias_ref[l : l + 1, :]
    gconv_ref[...] = jnp.zeros_like(gconv_ref)
    gpre_ref[total:, :] = jnp.zeros((HEAD, ch), F32)

    def first(c, carry):
        base = pl.multiple_of(c * CONV_ROWS, CONV_ROWS)
        pre, shifted = conv_window(conv_ref, since_ref, taps, bias, base)
        sig = sigmoid(pre)
        grad = gxs_ref[pl.ds(base, CONV_ROWS), :] + dot_tn(gproj_ref[:, pl.ds(base, CONV_ROWS)], xp_ref[l])
        grad = grad * (sig * (1.0 + pre * (1.0 - sig)))
        gpre_ref[pl.ds(base, CONV_ROWS), :] = grad
        for j in range(CONV):
            gconv_ref[CONV - 1 - j : CONV - j, :] += jnp.sum(grad * shifted[j], axis=0, keepdims=True)
        gconv_ref[CONV : CONV + 1, :] += jnp.sum(grad, axis=0, keepdims=True)
        return carry

    lax.fori_loop(0, total // CONV_ROWS, first, 0)

    def second(c, carry):
        base = pl.multiple_of(c * CONV_ROWS, CONV_ROWS)
        window = gpre_ref[pl.ds(base, CONV_ROWS + HEAD), :]
        since = since_ref[pl.ds(base, CONV_ROWS + HEAD), :]
        grad = taps[CONV - 1 : CONV, :] * window[:CONV_ROWS]
        for j in range(1, CONV):
            grad = grad + taps[CONV - 1 - j : CONV - j, :] * (window * (since >= j).astype(F32))[j : j + CONV_ROWS]
        gxi_ref[pl.ds(base, CONV_ROWS), :] = grad.astype(BF16)
        return carry

    lax.fori_loop(0, total // CONV_ROWS, second, 0)
    weights.wait()
    reduce = LineReduce(cstage_ref, cinbox_ref, csend, crecv, d, m, lanes)

    def term(s):
        part = pl.ds(pl.multiple_of(s * rows, 16), rows)
        return dot_nt(gxi_ref[part, :], win_ref[0]) + dot_nt(gzg_ref[part, :], win_ref[1])

    reduce.push(reduce.order[0], term(reduce.order[0]))
    early.second()
    lmine[till[0] : till[1], :] = dot_tn(whole, gxi_ref[...]).astype(BF16)
    lmine[till[1] : till[2], :] = dot(gproj_ref[...], xs_ref[...].astype(BF16)).astype(BF16)
    lmine[till[2] : till[3], :] = gconv_ref[...].astype(BF16)
    if till[3] < lmine.shape[0]:
        lmine[till[3] :, :] = jnp.zeros((lmine.shape[0] - till[3], ch), BF16)
    late.begin()
    for s in reduce.order[1:]:
        reduce.push(s, term(s))
    own_ref[...] = term(m)
    late.second()
    early.third()
    late.third()
    early.fourth()
    early.end()
    zbuf_ref[...] = early_ref[at[5] : at[7], :]
    shared = exchange(line, zbuf_ref, zin_ref, zsend, zrecv)
    late.fourth()
    reduce.total(own_ref)
    act = act_ref[...].astype(F32)
    pulled, grad_gain = norm_back(act, rms_inverse(act), gain_ref[l : l + 1, :], own_ref[...])
    up_ref[...] = gmid_ref[...] + pulled
    late.end()
    if l == 0:
        both = jnp.concatenate([grad_gain, prior_ref[...]], axis=0)
        groups = width // LANES
        for g in range(groups):
            nbuf_ref[2 * g : 2 * g + 2, :] = both[:, g * LANES : (g + 1) * LANES]
        nbuf_ref[2 * groups :, :] = jnp.zeros((nbuf_ref.shape[0] - 2 * groups, LANES), F32)
        nbuf2_ref[...] = exchange([(lax.rem(d + k, peers), m) for k in range(1, peers)], nbuf_ref, nin_ref, nsend, nrecv)()
        summed = exchange(line, nbuf2_ref, nin2_ref, nsend2, nrecv2)()
        gnorm_ref[...] = jnp.concatenate([summed[2 * g : 2 * g + 2, :] for g in range(groups)], axis=1)
    else:
        gnorm_ref[...] = grad_gain
    share_ref[...] = shared()
    finish()
    reduce.finish()
    early.finish()
    late.finish()


def in_back(l, lanes, peers, experts, gpart, gxs, gzg, conv, taps, bias, since, xp, xs, whole, act, gain, gmid, gwout, gshare, gdtw, gdtb,
            galog, gskip, prior, win):
    rows, width = act.shape
    ch, total = win.shape[3], rows * lanes
    early = whole_blocks(early_rows(width, experts)[-1], peers)
    late = whole_blocks(late_rows(width)[-1], peers)
    shared = 2 * (experts + 8)
    small = -(-2 * (width // LANES) // 8) * 8
    return pl.pallas_call(
        functools.partial(in_back_kernel, l, lanes, peers, experts),
        out_shape=[f32(rows, width), bf16(early, ch), bf16(late, ch), f32(shared, ch), f32(2 if l == 0 else 1, width)],
        in_specs=vmem(20) + hbm(1),
        out_specs=vmem(5),
        scratch_shapes=[
            pltpu.VMEM((2, PARTS, PROJ, total // PARTS), BF16),
            pltpu.VMEM((2, PARTS, PROJ, total // PARTS), BF16),
            pltpu.VMEM((PROJ, total), BF16),
            pltpu.VMEM((total + HEAD, ch), F32),
            pltpu.VMEM((total, ch), BF16),
            pltpu.VMEM((16, ch), F32),
            pltpu.VMEM((lanes, rows, width), BF16),
            pltpu.VMEM((2, lanes, rows, width), BF16),
            pltpu.VMEM((rows, width), F32),
            dma(2, PARTS), dma(2, PARTS), dma(lanes), dma(2, lanes),
            pltpu.VMEM(win.shape[1:], BF16), dma(1),
            pltpu.VMEM((shared, ch), BF16), pltpu.VMEM((lanes - 1, shared, ch), BF16), dma(lanes - 1), dma(lanes - 1),
            pltpu.VMEM((small, LANES), F32), pltpu.VMEM((peers - 1, small, LANES), F32), dma(peers - 1), dma(peers - 1),
            pltpu.VMEM((small, LANES), F32), pltpu.VMEM((lanes - 1, small, LANES), F32), dma(lanes - 1), dma(lanes - 1),
        ]
        + plane_scratch(peers, early, ch)
        + plane_scratch(peers, late, ch),
        compiler_params=params(6 + l),
        name="mamba_in_backward",
    )(gpart, gxs, gzg, conv, taps, bias, since, xp, xs, whole, act, gain, gmid, gwout, gshare, gdtw, gdtb, galog, gskip, prior, win)


def on_device(
    tokens, cotangent, lengths, routes, slot_place, norm_in, w_in, conv_w, conv_b, x_proj, dt_proj, dt_bias,
    a_log, d_skip, w_out, norm_moe, router, w_up, w_down,
):
    layers = norm_in.shape[0]
    rows_here, width = tokens.shape
    lanes, peers = lax.axis_size("mp"), lax.axis_size("dp")
    total = rows_here * lanes
    channels = w_in.shape[3]
    experts = router.shape[2]
    capacity = max(2, (5 * rows_here + 4 * experts - 1) // (4 * experts))
    padded = (capacity + 15) // 16 * 16
    position = lax.broadcasted_iota(jnp.int32, (total + HEAD, 1), 0)
    since, first = position, 0
    for i in range(lengths.shape[1] - 1):
        first = first + lengths[0, i]
        since = jnp.where(position >= first, position - first, since)
    since = jnp.where(position < total, since, 0)
    choose = (routes[:, None] == jnp.arange(LANES, dtype=jnp.int32)[None, :]).astype(F32)
    place = jnp.pad(routes * padded + slot_place, (0, -rows_here % LANES))
    place = jnp.broadcast_to(place[None, :], (8, place.shape[0]))
    spread = spread_matrix()
    x_proj = jnp.swapaxes(x_proj, 1, 2)
    router = jnp.pad(router, ((0, 0), (0, 0), (0, LANES - experts)))

    activation = tokens
    stored = []
    for l in range(layers):
        whole, conv_in, gate_in, conv_out, proj = in_block(l, lanes, activation, norm_in, conv_w, conv_b, since, x_proj, w_in)
        gated, ys, marks = scan_fwd(l, conv_out, gate_in, proj, since, dt_proj, dt_bias, a_log, d_skip, spread)
        gated = gated.reshape(lanes, rows_here, channels)
        middle, chance, into, arrived, hidden, active, picked, following = mid_block(
            l, lanes, peers, experts, padded, activation, gated, norm_moe, router, choose, place, w_out, w_up, w_down)
        stored.append((activation, whole, conv_in, gate_in, conv_out, proj, gated, ys, marks, middle, chance, into, arrived, hidden, active, picked))
        activation = following
    upstream = cotangent
    collected = []
    grad_norm_in = jnp.zeros((1, width), F32)
    for l in reversed(range(layers)):
        before, whole, conv_in, gate_in, conv_out, proj, gated, ys, marks, middle, chance, into, arrived, hidden, active, picked = stored[l]
        grad_middle, grad_up, grad_down, grad_gated, grad_w_out, grad_share = moe_back(
            l, lanes, peers, experts, upstream, chance, choose, picked, middle, norm_moe, router, into, arrived, hidden, active, gated,
            w_out, w_up, w_down)
        grad_conv, grad_zg, grad_proj, grad_dtw, grad_dtb, grad_alog, grad_skip = scan_bwd(
            l, conv_out, gate_in, proj, since, ys, grad_gated.reshape(total, channels), marks, dt_proj, dt_bias, a_log, d_skip, spread)
        upstream, early, late, share, grad_norm_in = in_back(
            l, lanes, peers, experts, grad_proj, grad_conv, grad_zg, conv_in, conv_w, conv_b, since, x_proj, conv_out, whole,
            before, norm_in, grad_middle, grad_w_out, grad_share, grad_dtw, grad_dtb, grad_alog, grad_skip, grad_norm_in, w_in)
        collected.append((early, late, share, grad_up, grad_down))
    collected = collected[::-1]
    at, till = early_rows(width, experts), late_rows(width)

    def stacked(make):
        return jnp.stack([make(*entry).astype(F32) for entry in collected])

    def from_early(first, count):
        return stacked(lambda early, *rest: early[first : first + count])

    def from_late(first, count):
        return stacked(lambda early, late, *rest: late[first : first + count])

    def wide(rows, first, count):
        return jnp.concatenate([rows[first + i * count : first + (i + 1) * count] for i in range(width // channels)], axis=1)

    return (
        activation,
        upstream,
        grad_norm_in,
        stacked(lambda early, late, *rest: jnp.stack([late[till[0] : till[1]], early[at[0] : at[1]]])),
        from_late(till[2], CONV),
        from_late(till[2] + CONV, 1)[:, 0],
        jnp.swapaxes(from_late(till[1], PROJ), 1, 2),
        from_early(at[2], DT_RANK),
        from_early(at[4], 1)[:, 0],
        from_early(at[3], STATE),
        from_early(at[4] + 1, 1)[:, 0],
        stacked(lambda early, *rest: wide(early, at[1], channels)),
        stacked(lambda early, late, share, *rest: wide(share, 0, experts + 8)[experts]),
        stacked(lambda early, late, share, *rest: wide(share, 0, experts + 8)[:experts].T),
        jnp.stack([entry[3][None] for entry in collected]),
        jnp.stack([entry[4][None] for entry in collected]),
    )


def solution(mesh):
    return jax.shard_map(
        on_device,
        mesh=mesh,
        in_specs=(
            P(("dp", "mp"), None),
            P(("dp", "mp"), None),
            P("dp", None),
            P(("dp", "mp")),
            P(("dp", "mp")),
            P(),
            P(None, None, None, "mp"),
            P(None, None, "mp"),
            P(None, "mp"),
            P(None, "mp", None),
            P(None, None, "mp"),
            P(None, "mp"),
            P(None, None, "mp"),
            P(None, "mp"),
            P(None, "mp", None),
            P(),
            P(),
            P(None, "dp", None, "mp"),
            P(None, "dp", "mp", None),
        ),
        out_specs=(
            P(("dp", "mp"), None),
            P(("dp", "mp"), None),
            P(),
            P(None, None, None, "mp"),
            P(None, None, "mp"),
            P(None, "mp"),
            P(None, "mp", None),
            P(None, None, "mp"),
            P(None, "mp"),
            P(None, None, "mp"),
            P(None, "mp"),
            P(None, "mp", None),
            P(),
            P(),
            P(None, "dp", None, "mp"),
            P(None, "dp", "mp", None),
        ),
        check_vma=False,
    )
```

time: 1100 us -> 721 us (0.66)
  waiting for transfers between devices: 624 us -> 0 us
  Pallas kernels: 81.2 us -> 665 us
  blocking collectives: 120 us -> 0 us
  matrix products: 106 us -> 0 us
  other arithmetic: 65.9 us -> 17.2 us
  starting transfers between devices: 27.4 us -> 0 us
  local copies, waits for them, and re-layouts: 51.8 us -> 29.2 us
  between operations: 16.3 us -> 3.55 us
    pallas_call x4 -> x12, Pallas kernels: 81.2 us -> 665 us  [the longest x2 200 us: moe_back(): pl.pallas_call(functools.partial(moe_back_kernel, l, lanes, peers), out_s...]
    psum x6 -> x0, waiting for transfers between devices: 223 us -> none  [the longest x4 125 us: sum_over_channels(): return lax.psum(values.astype(BF16), 'mp')]
    all_to_all x6 -> x0, waiting for transfers between devices: 181 us -> none  [the longest x4 125 us: from_experts(): lax.all_to_all(partial_out.reshape(-1, capacity, width).astype(BF16), ('d...]
    reduce_scatter x4 -> x0, waiting for transfers between devices: 112 us -> none  [scatter_rows(): lax.psum_scatter(values.astype(BF16), 'mp', scatter_dimension=0, tiled=True)]
    all_gather x4 -> x0, waiting for transfers between devices: 107 us -> none  [gather_rows(): return lax.all_gather(values, 'mp', axis=0, tiled=True)]
    dot_general x50 -> x0, matrix products: 106 us -> none  [the longest x12 34.7 us: dot_nt(): lax.dot_general(a, b, (((1,), (1,)), ((), ())), preferred_element_type=F32)]
    all_to_all x2 -> x0, blocking collectives: 79.9 us -> none  [to_experts(): lax.all_to_all(copies, ('dp', 'mp'), split_axis=0, concat_axis=0, tiled=T...]
    psum x1 -> x0, blocking collectives: 40 us -> none  [on_device(): shared = lax.psum((grad_norm_in, grad_norm_moe, grad_router), ('dp', 'mp'))]
  transfers between devices with their start and end apart: 20 -> 0, of which waited for: 20 -> 0; matrix products, arithmetic and copies ran while one was open for 9% -> 0% of each run, Pallas kernels for 0% -> 0%
where the time goes in v2:
time: 721 us; the launch traced here: 715 us
  Pallas kernels  665 us (92%)
  local copies, waits for them, and re-layouts  29.2 us (4%)
  other arithmetic  17.2 us (2%)
    pallas_call x2, Pallas kernels, moe_back(): pl.pallas_call(functools.partial(moe_back_kernel, l, lanes, peers), out_s...  200 us
    pallas_call x2, Pallas kernels, mid_block(): pl.pallas_call(functools.partial(mid_kernel, l, lanes, peers, experts), o...  185 us
    pallas_call x2, Pallas kernels, in_back(): pl.pallas_call(functools.partial(in_back_kernel, l, lanes, peers, experts...  117 us
    pallas_call x2, Pallas kernels, in_block(): pl.pallas_call(functools.partial(in_kernel, l, lanes), out_shape=[bf16(la...  83.2 us
    pallas_call x2, Pallas kernels, scan_bwd(): pl.pallas_call(functools.partial(scan_bwd_kernel, l), grid=(steps,), out_...  55.2 us
    unnamed x110, local copies, waits for them, and re-layouts  25.3 us
    pallas_call x2, Pallas kernels, scan_fwd(): pl.pallas_call(functools.partial(scan_fwd_kernel, l), grid=(steps,), out_...  24.9 us

profile of v2, /device:TPU:0, one launch (start us, length us, event | category | flops | bytes accessed | tf_op | source)
XLA Modules:
  0.0 715.3 jit_solution(17692155723061749789)
XLA Ops:
  0.7 1.4 fusion.13
  4.0 1.5 select_select_fusion.since_ref
  5.5 42.0 %mamba_in.2 = (bf16[4,192,768]{2,1,0:T(8,128)(2,1)}, f32[776,384]{1,0:T(8,128)}, f32[768,384]{1,0:T(8,128)}, f32[768,384]{1,0:T(8,128)}, bf16[80,768]{1,0:T(8,128)(2,1)}) custom-call(bf16[192,768]{1,0:T(8,128)(2,1)} %act_ref.5, f32[2,768]{1,0:T(2,128)} %gain_ref.15, f32[2,4,384]{2,1,0:T(4,128)} %taps_ref.7, f32[2,384]{1,0:T(2,128)} %bias_ref.7, ...), custom_call_target="tpu_custom_call" | custom-call | tf_op jit(solution)/shard_map/mamba_in/pallas_call | solution.py:611
  47.6 1.3 copy-done.3
  48.9 1.3 copy-done.7
  50.2 0.9 copy-done.21
  51.1 12.5 %scan_fwd.2 = (bf16[768,384]{1,0:T(8,128)(2,1)S(1)}, f32[768,384]{1,0:T(8,128)S(1)}, f32[6,16,384]{2,1,0:T(8,128)S(1)}) custom-call(f32[768,384]{1,0:T(8,128)S(1)} %copy-done.3, f32[768,384]{1,0:T(8,128)S(1)} %copy-done.7, bf16[80,768]{1,0:T(8,128)(2,1)S(1)} %copy-done.21, s32[776,1]{1,0:T(8,128)S(1)} %copy-done, bf16[2,48,384]{2,1,0:T(8,128)(2,1)S(1)} %copy-done.17, ...), custom_call_target="tpu_custom_call" | custom-call | tf_op jit(solution)/shard_map/scan_fwd/pallas_call | solution.py:113
  63.5 0.8 copy-done.11
  64.3 1.0 copy-done.15
  65.6 0.9 pad.8.router_ref
  66.6 0.7 fusion.1.choose_ref
  67.9 92.2 %mid_forward.2 = (f32[192,768]{1,0:T(8,128)}, f32[192,128]{1,0:T(8,128)}, bf16[4,256,192]{2,1,0:T(8,128)(2,1)}, bf16[4,256,768]{2,1,0:T(8,128)(2,1)}, bf16[4,256...) custom-call(bf16[192,768]{1,0:T(8,128)(2,1)} %act_ref.5, ...), custom_call_target="tpu_custom_call" | custom-call | tf_op jit(solution)/shard_map/mid_forward/pallas_call | solution.py:786
  160.2 41.2 %mamba_in.3 = (bf16[4,192,768]{2,1,0:T(8,128)(2,1)}, f32[776,384]{1,0:T(8,128)}, f32[768,384]{1,0:T(8,128)}, f32[768,384]{1,0:T(8,128)}, bf16[80,768]{1,0:T(8,128)(2,1)}) custom-call(f32[192,768]{1,0:T(8,128)} %get-tuple-element.88.act_ref, f32[2,768]{1,0:T(2,128)} %gain_ref.15, f32[2,4,384]{2,1,0:T(4,128)} %taps_ref.7, f32[2,384]{1,0:T(2,128)} %bias_ref.7, ...), custom_call_target="tpu_custom_call" | custom-call | tf_op jit(solution)/shard_map/mamba_in/pallas_call | solution.py:611
  201.4 1.3 copy-done.5
  202.7 1.3 copy-done.9
  204.0 0.9 copy-done.23
  204.9 12.4 %scan_fwd.3 = (bf16[768,384]{1,0:T(8,128)(2,1)S(1)}, f32[768,384]{1,0:T(8,128)S(1)}, f32[6,16,384]{2,1,0:T(8,128)S(1)}) custom-call(f32[768,384]{1,0:T(8,128)S(1)} %copy-done.5, f32[768,384]{1,0:T(8,128)S(1)} %copy-done.9, bf16[80,768]{1,0:T(8,128)(2,1)S(1)} %copy-done.23, s32[776,1]{1,0:T(8,128)S(1)} %copy-done.1, bf16[2,48,384]{2,1,0:T(8,128)(2,1)S(1)} %copy-done.17, ...), custom_call_target="tpu_custom_call" | custom-call | tf_op jit(solution)/shard_map/scan_fwd/pallas_call | solution.py:113
  217.3 0.8 copy-done.12
  218.1 1.0 copy-done.16
  219.1 92.5 %mid_forward.3 = (f32[192,768]{1,0:T(8,128)}, f32[192,128]{1,0:T(8,128)}, bf16[4,256,192]{2,1,0:T(8,128)(2,1)}, bf16[4,256,768]{2,1,0:T(8,128)(2,1)}, bf16[4,256...) custom-call(f32[192,768]{1,0:T(8,128)} %get-tuple-element.88.act_ref, ...), custom_call_target="tpu_custom_call" | custom-call | tf_op jit(solution)/shard_map/mid_forward/pallas_call | solution.py:786
  311.7 99.9 %moe_backward.2 = (f32[192,768]{1,0:T(8,128)}, f32[768,768]{1,0:T(8,128)}, f32[768,768]{1,0:T(8,128)}, f32[4,192,384]{2,1,0:T(8,128)}, bf16[384,768]{1,0:T(8,128)(2,1)}, /*index=5*/f32[16,768]{1,0:T(8,128)}) custom-call(bf16[192,768]{1,0:T(8,128)(2,1)} %up_ref.1, f32[192,128]{1,0:T(8,128)} %get-tuple-element.96.chance_ref, f32[192,128]{1,0:T(8,128)} %fusion.1.choose_ref, ...), custom_call_target="tpu_custom_call" | custom-call | tf_op jit(solution)/shard_map/moe_backward/pallas_call | solution.py:868
  411.6 27.5 %scan_bwd.2 = (f32[768,384]{1,0:T(8,128)S(1)}, bf16[768,384]{1,0:T(8,128)(2,1)S(1)}, f32[80,768]{1,0:T(8,128)S(1)}, f32[48,384]{1,0:T(8,128)S(1)}, f32[1,384]{1,...) custom-call(f32[768,384]{1,0:T(8,128)S(1)} %copy-done.6, f32[768,384]{1,0:T(8,128)S(1)} %copy-done.10, ...), custom_call_target="tpu_custom_call" | custom-call | tf_op jit(solution)/shard_map/scan_bwd/pallas_call | solution.py:259
  439.1 1.0 copy-done.13
  440.1 0.8 copy-done.19
  441.0 0.7 copy-done.25
  441.7 0.6 copy-done.27
  442.3 0.6 copy-done.31
  444.0 56.6 %mamba_in_backward.2 = (f32[192,768]{1,0:T(8,128)}, bf16[1664,384]{1,0:T(8,128)(2,1)}, bf16[896,384]{1,0:T(8,128)(2,1)}, f32[32,384]{1,0:T(8,128)}, f32[1,768]{1,0:T(1,128)}) custom-call(f32[80,768]{1,0:T(8,128)} %copy-done.25, f32[768,384]{1,0:T(8,128)} %copy-done.13, bf16[768,384]{1,0:T(8,128)(2,1)} %copy-done.19, f32[776,384]{1,0:T(8,128)} %get-tuple-element.108.conv_ref, ...), custom_call_target="tpu_custom_call" | custom-call | tf_op jit(solution)/shard_map/mamba_in_backward/pallas_call | solution.py:1126
  500.7 100.5 %moe_backward.3 = (f32[192,768]{1,0:T(8,128)}, f32[768,768]{1,0:T(8,128)}, f32[768,768]{1,0:T(8,128)}, f32[4,192,384]{2,1,0:T(8,128)}, bf16[384,768]{1,0:T(8,128)(2,1)}, /*index=5*/f32[16,768]{1,0:T(8,128)}) custom-call(f32[192,768]{1,0:T(8,128)} %get-tuple-element.117.up_ref, f32[192,128]{1,0:T(8,128)} %get-tuple-element.118.chance_ref, ...), custom_call_target="tpu_custom_call" | custom-call | tf_op jit(solution)/shard_map/moe_backward/pallas_call | solution.py:868
  601.2 27.7 %scan_bwd.3 = (f32[768,384]{1,0:T(8,128)S(1)}, bf16[768,384]{1,0:T(8,128)(2,1)S(1)}, f32[80,768]{1,0:T(8,128)S(1)}, f32[48,384]{1,0:T(8,128)S(1)}, f32[1,384]{1,...) custom-call(f32[768,384]{1,0:T(8,128)S(1)} %copy-done.4, f32[768,384]{1,0:T(8,128)S(1)} %copy-done.8, ...), custom_call_target="tpu_custom_call" | custom-call | tf_op jit(solution)/shard_map/scan_bwd/pallas_call | solution.py:259
  628.9 1.0 copy-done.14
  630.0 0.8 copy-done.20
  630.8 0.7 copy-done.26
  631.5 0.6 copy-done.28
  633.8 60.4 %mamba_in_backward.3 = (f32[192,768]{1,0:T(8,128)}, bf16[1664,384]{1,0:T(8,128)(2,1)}, bf16[896,384]{1,0:T(8,128)(2,1)}, f32[32,384]{1,0:T(8,128)}, f32[2,768]{1,0:T(2,128)}) custom-call(f32[80,768]{1,0:T(8,128)} %copy-done.26, f32[768,384]{1,0:T(8,128)} %copy-done.14, bf16[768,384]{1,0:T(8,128)(2,1)} %copy-done.20, f32[776,384]{1,0:T(8,128)} %get-tuple-element.130.conv_ref, ...), custom_call_target="tpu_custom_call" | custom-call | tf_op jit(solution)/shard_map/mamba_in_backward/pallas_call | solution.py:1126
  694.4 1.1 copy-done.42
  695.8 2.5 maximum_convert_fusion
  698.3 0.6 maximum_convert_fusion.4
  699.5 0.7 convert_bitcast_fusion
  700.2 0.7 maximum_convert_fusion.2
  701.5 0.6 maximum_convert_fusion.3
  702.9 1.6 maximum_convert_fusion.1
  705.1 0.6 pad_maximum_fusion.2
  706.1 2.7 pad_maximum_fusion
  708.8 1.4 copy-done.39
  710.2 2.5 pad_maximum_fusion.1
  712.7 0.8 copy.39
  713.5 0.8 copy.40
  (120 shorter events, 7.8 us)
Async XLA Ops:
  0.6 46.9 %copy-start.17 = (bf16[2,48,384]{2,1,0:T(8,128)(2,1)S(1)}, bf16[2,48,384]{2,1,0:T(8,128)(2,1)}, u32[]{:S(2)}) copy-start(bf16[2,48,384]{2,1,0:T(8,128)(2,1)} %dtw_ref.7) | copy-start | bytes 221188
  0.7 46.9 %copy-start.29 = (f32[2,384]{1,0:T(2,128)S(1)}, f32[2,384]{1,0:T(2,128)}, u32[]{:S(2)}) copy-start(f32[2,384]{1,0:T(2,128)} %dtb_ref.7) | copy-start | bytes 9220
  0.7 46.9 %copy-start.18 = (f32[2,16,384]{2,1,0:T(8,128)S(1)}, f32[2,16,384]{2,1,0:T(8,128)}, u32[]{:S(2)}) copy-start(f32[2,16,384]{2,1,0:T(8,128)} %alog_ref.7) | copy-start | bytes 147460
  0.7 46.9 %copy-start.30 = (f32[2,384]{1,0:T(2,128)S(1)}, f32[2,384]{1,0:T(2,128)}, u32[]{:S(2)}) copy-start(f32[2,384]{1,0:T(2,128)} %skip_ref.7) | copy-start | bytes 9220
  5.5 42.1 %copy-start = (s32[776,1]{1,0:T(8,128)S(1)}, s32[776,1]{1,0:T(8,128)}, u32[]{:S(2)}) copy-start(s32[776,1]{1,0:T(8,128)} %select_select_fusion.since_ref) | copy-start | bytes 9316
  47.5 17.9 %copy-start.47 = (f32[2,768,8]{1,2,0:T(8,128)S(1)}, f32[2,768,8]{1,2,0:T(8,128)}, u32[]{:S(2)}) copy-start(f32[2,768,8]{1,2,0:T(8,128)} %param.35) | copy-start | bytes 147460
  47.6 1.3 copy-start.3
  48.9 1.3 copy-start.7
  50.1 0.9 copy-start.21
  51.1 15.5 %copy-start.51 = (s32[192]{0:T(256)S(1)}, s32[192]{0:T(256)}, u32[]{:S(2)}) copy-start(s32[192]{0:T(256)} %param.22) | copy-start | bytes 2308
  51.1 16.2 %copy-start.52 = (s32[192]{0:T(256)S(1)}, s32[192]{0:T(256)}, u32[]{:S(2)}) copy-start(s32[192]{0:T(256)} %param.23) | copy-start | bytes 2308
  63.5 0.8 copy-start.11
  64.3 1.0 copy-start.15
  160.2 41.2 %copy-start.1 = (s32[776,1]{1,0:T(8,128)S(1)}, s32[776,1]{1,0:T(8,128)}, u32[]{:S(2)}) copy-start(s32[776,1]{1,0:T(8,128)} %select_select_fusion.since_ref) | copy-start | bytes 9316
  201.4 1.3 copy-start.5
  202.7 1.3 copy-start.9
  204.0 0.9 copy-start.23
  217.3 0.8 copy-start.12
  218.1 1.0 copy-start.16
  311.7 99.9 %copy-start.6 = (f32[768,384]{1,0:T(8,128)S(1)}, f32[768,384]{1,0:T(8,128)}, u32[]{:S(2)}) copy-start(f32[768,384]{1,0:T(8,128)} %get-tuple-element.89.xs_ref) | copy-start | bytes 3538948
  311.7 99.9 %copy-start.10 = (f32[768,384]{1,0:T(8,128)S(1)}, f32[768,384]{1,0:T(8,128)}, u32[]{:S(2)}) copy-start(f32[768,384]{1,0:T(8,128)} %get-tuple-element.90.zg_ref) | copy-start | bytes 3538948
  311.7 99.9 %copy-start.24 = (bf16[80,768]{1,0:T(8,128)(2,1)S(1)}, bf16[80,768]{1,0:T(8,128)(2,1)}, u32[]{:S(2)}) copy-start(bf16[80,768]{1,0:T(8,128)(2,1)} %get-tuple-element.91.proj_ref) | copy-start | bytes 368644
  439.1 1.0 copy-start.13
  440.1 0.8 copy-start.19
  441.0 0.7 copy-start.25
  441.7 0.6 copy-start.27
  442.3 0.6 copy-start.31
  500.6 100.5 %copy-start.2 = (s32[776,1]{1,0:T(8,128)S(1)}, s32[776,1]{1,0:T(8,128)}, u32[]{:S(2)}) copy-start(s32[776,1]{1,0:T(8,128)} %select_select_fusion.since_ref) | copy-start | bytes 9316
  500.6 100.5 %copy-start.4 = (f32[768,384]{1,0:T(8,128)S(1)}, f32[768,384]{1,0:T(8,128)}, u32[]{:S(2)}) copy-start(f32[768,384]{1,0:T(8,128)} %get-tuple-element.84.xs_ref) | copy-start | bytes 3538948
  500.6 100.5 %copy-start.8 = (f32[768,384]{1,0:T(8,128)S(1)}, f32[768,384]{1,0:T(8,128)}, u32[]{:S(2)}) copy-start(f32[768,384]{1,0:T(8,128)} %get-tuple-element.85.zg_ref) | copy-start | bytes 3538948
  500.7 100.5 %copy-start.22 = (bf16[80,768]{1,0:T(8,128)(2,1)S(1)}, bf16[80,768]{1,0:T(8,128)(2,1)}, u32[]{:S(2)}) copy-start(bf16[80,768]{1,0:T(8,128)(2,1)} %get-tuple-element.86.proj_ref) | copy-start | bytes 368644
  628.9 1.0 copy-start.14
  630.0 0.8 copy-start.20
  630.8 0.7 copy-start.26
  631.5 0.6 copy-start.28
  633.8 60.4 %copy-start.41 = (bf16[1664,384]{1,0:T(8,128)(2,1)S(1)}, bf16[1664,384]{1,0:T(8,128)(2,1)}, u32[]{:S(2)}) copy-start(bf16[1664,384]{1,0:T(8,128)(2,1)} %get-tuple-element.145) | copy-start | bytes 3833860
  633.8 60.5 %copy-start.43 = (bf16[896,384]{1,0:T(8,128)(2,1)S(1)}, bf16[896,384]{1,0:T(8,128)(2,1)}, u32[]{:S(2)}) copy-start(bf16[896,384]{1,0:T(8,128)(2,1)} %get-tuple-element.144) | copy-start | bytes 2064388
  694.2 1.3 copy-start.42
  694.2 1.5 copy-start.44
  702.8 1.7 copy-start.48
  702.8 1.7 copy-start.49
  702.8 2.9 copy-start.38
  702.8 3.3 copy-start.40
  706.1 2.7 copy-start.37
  706.1 4.1 copy-start.39
  710.2 2.5 copy-start.45
  710.2 3.3 copy-start.46
  712.7 1.6 copy-start.50
  (5 other events, 2.9 us)

commit v3 on v2

v3 whole, which is shorter than its diff:
```python
import functools
import types

import jax
import jax.numpy as jnp
from jax import lax
from jax.experimental import pallas as pl
from jax.experimental.pallas import tpu as pltpu
from jax.sharding import PartitionSpec as P

STATE = 16
DT_RANK = 48
LANES = 128
CHUNK = 128
LOG2E = 1.4426950408889634
RESET = 1.0e6
PROJ = DT_RANK + 2 * STATE
CONV = 4
dt_most = 0.05
epsilon = 1e-05
highest = lax.Precision.HIGHEST
MESH = pl.DeviceIdType.MESH
F32, BF16 = jnp.float32, jnp.bfloat16


def sigmoid(v):
    return 1.0 / (1.0 + jnp.exp(-v))


def dot(a, b):
    return jnp.dot(a, b, preferred_element_type=F32)


def dot_nt(a, b):
    return lax.dot_general(a, b, (((1,), (1,)), ((), ())), preferred_element_type=F32)


def dot_tn(a, b):
    return lax.dot_general(a, b, (((0,), (0,)), ((), ())), preferred_element_type=F32)


def spread_matrix():
    rows = lax.broadcasted_iota(jnp.int32, (STATE, STATE * LANES), 0)
    cols = lax.broadcasted_iota(jnp.int32, (STATE, STATE * LANES), 1)
    return (rows == cols // LANES).astype(BF16)


def put(ref, value):
    for j in range(ref.shape[0]):
        ref[j] = value[:, j * LANES : (j + 1) * LANES]


def spread_rows(proj, spread, out_ref):
    wide = dot_tn(proj, spread)
    for n in range(STATE):
        out_ref[pl.ds(n, CHUNK, stride=STATE), :] = wide[:, n * LANES : (n + 1) * LANES]


def scan_fwd_kernel(l, xs_ref, zg_ref, proj_ref, since_ref, dtw_ref, dtb_ref, alog_ref, skip_ref, spread_ref,
                    gated_ref, ys_ref, hck_ref,
                    h_ref, dm_ref, dx_ref, bx_ref, cx_ref, yq_ref):
    groups = xs_ref.shape[1] // LANES

    @pl.when(pl.program_id(0) == 0)
    def _():
        h_ref[...] = jnp.zeros_like(h_ref)

    hck_ref[0] = h_ref[...]
    proj = proj_ref[...]
    xs = xs_ref[...]
    delta = dt_most * sigmoid(dot_tn(proj[:DT_RANK], dtw_ref[l]) + dtb_ref[l : l + 1, :])
    put(dm_ref, delta + RESET * (since_ref[...] == 0).astype(F32))
    put(dx_ref, delta * xs)
    spread_rows(proj[DT_RANK : DT_RANK + STATE], spread_ref[...], bx_ref)
    spread_rows(proj[DT_RANK + STATE :], spread_ref[...], cx_ref)
    rate = -LOG2E * jnp.exp(alog_ref[l])
    rates = [rate[:, j * LANES : (j + 1) * LANES] for j in range(groups)]

    def step(g, hs):
        hs = list(hs)
        t0 = pl.multiple_of(g * 8, 8)
        for i in range(8):
            t = t0 + i
            r0 = pl.multiple_of(t * STATE, STATE)
            b = bx_ref[pl.ds(r0, STATE), :]
            c = cx_ref[pl.ds(r0, STATE), :]
            q0 = pl.multiple_of(t * 8, 8)
            for j in range(groups):
                lanes = slice(j * LANES, (j + 1) * LANES)
                dec = jnp.exp2(dm_ref[j, pl.ds(t, 1), :] * rates[j])
                hs[j] = dec * hs[j] + dx_ref[j, pl.ds(t, 1), :] * b
                q = c * hs[j]
                yq_ref[j, pl.ds(q0, 8), :] = q[:8] + q[8:]
        return tuple(hs)

    hs = lax.fori_loop(0, CHUNK // 8, step, tuple(h_ref[:, j * LANES : (j + 1) * LANES] for j in range(groups)))
    for j in range(groups):
        h_ref[:, j * LANES : (j + 1) * LANES] = hs[j]
    zg = zg_ref[...]
    for j in range(groups):
        lanes = slice(j * LANES, (j + 1) * LANES)
        y = skip_ref[l : l + 1, lanes] * xs[:, lanes]
        for k in range(8):
            y = y + yq_ref[j, pl.ds(k, CHUNK, stride=8), :]
        ys_ref[:, lanes] = y
        z = zg[:, lanes]
        gated_ref[:, lanes] = (y * z * sigmoid(z)).astype(BF16)


def scan_fwd(l, xs, zg, proj, since, dtw, dtb, alog, skip, spread):
    rows, ch = xs.shape
    steps = rows // CHUNK
    row = lambda w: pl.BlockSpec((CHUNK, w), lambda i: (i, 0))
    full = lambda s: pl.BlockSpec(s, lambda i: (0,) * len(s))
    return pl.pallas_call(
        functools.partial(scan_fwd_kernel, l),
        grid=(steps,),
        out_shape=[
            jax.ShapeDtypeStruct((rows, ch), BF16),
            jax.ShapeDtypeStruct((rows, ch), F32),
            jax.ShapeDtypeStruct((steps, STATE, ch), F32),
        ],
        in_specs=[row(ch), row(ch), pl.BlockSpec((PROJ, CHUNK), lambda i: (0, i)), row(1)]
        + [full(v.shape) for v in (dtw, dtb, alog, skip, spread)],
        out_specs=[row(ch), row(ch), pl.BlockSpec((1, STATE, ch), lambda i: (i, 0, 0))],
        scratch_shapes=[
            pltpu.VMEM((STATE, ch), F32),
            pltpu.VMEM((ch // LANES, CHUNK, LANES), F32),
            pltpu.VMEM((ch // LANES, CHUNK, LANES), F32),
            pltpu.VMEM((CHUNK * STATE, LANES), F32),
            pltpu.VMEM((CHUNK * STATE, LANES), F32),
            pltpu.VMEM((ch // LANES, CHUNK * 8, LANES), F32),
        ],
        compiler_params=pltpu.CompilerParams(vmem_limit_bytes=60 << 20),
        name="scan_fwd",
    )(xs, zg, proj, since, dtw, dtb, alog, skip, spread)


def scan_bwd_kernel(l, xs_ref, zg_ref, proj_ref, since_ref, ys_ref, gg_ref, hck_ref, dtw_ref, dtb_ref, alog_ref, skip_ref, spread_ref,
                    gxs_ref, gzg_ref, gproj_ref, gdtw_ref, gdtb_ref, galog_ref, gskip_ref,
                    a_ref, dm_ref, dx_ref, dl_ref, gy_ref, bx_ref, cx_ref, h_ref, dec_ref, pq_ref, gq_ref, gb_ref, gc_ref):
    groups = xs_ref.shape[1] // LANES
    cols = [slice(j * LANES, (j + 1) * LANES) for j in range(groups)]

    @pl.when(pl.program_id(0) == 0)
    def _():
        a_ref[...] = jnp.zeros_like(a_ref)
        gdtw_ref[...] = jnp.zeros_like(gdtw_ref)
        gdtb_ref[...] = jnp.zeros_like(gdtb_ref)
        galog_ref[...] = jnp.zeros_like(galog_ref)
        gskip_ref[...] = jnp.zeros_like(gskip_ref)

    proj = proj_ref[...]
    xs = xs_ref[...]
    delta = dt_most * sigmoid(dot_tn(proj[:DT_RANK], dtw_ref[l]) + dtb_ref[l : l + 1, :])
    put(dl_ref, delta)
    put(dm_ref, delta + RESET * (since_ref[...] == 0).astype(F32))
    put(dx_ref, delta * xs)
    zg = zg_ref[...]
    sz = sigmoid(zg)
    gg = gg_ref[...]
    gy = gg * (zg * sz)
    put(gy_ref, gy)
    gzg_ref[...] = (gg * ys_ref[...] * (sz * (1.0 + zg * (1.0 - sz)))).astype(BF16)
    gskip_ref[...] += jnp.sum(gy * xs, axis=0, keepdims=True)
    spread_rows(proj[DT_RANK : DT_RANK + STATE], spread_ref[...], bx_ref)
    spread_rows(proj[DT_RANK + STATE :], spread_ref[...], cx_ref)
    rate = -jnp.exp(alog_ref[l])
    rates2 = [LOG2E * rate[:, c] for c in cols]
    rates = [rate[:, c] for c in cols]

    for j in range(groups):
        h_ref[j, :STATE, :] = hck_ref[0][:, cols[j]]

    def again(g, hs):
        hs = list(hs)
        t0 = pl.multiple_of(g * 8, 8)
        for i in range(8):
            t = t0 + i
            r0 = pl.multiple_of(t * STATE, STATE)
            r1 = pl.multiple_of(t * STATE + STATE, STATE)
            b = bx_ref[pl.ds(r0, STATE), :]
            for j in range(groups):
                dec = jnp.exp2(dm_ref[j, pl.ds(t, 1), :] * rates2[j])
                hs[j] = dec * hs[j] + dx_ref[j, pl.ds(t, 1), :] * b
                dec_ref[j, pl.ds(r0, STATE), :] = dec
                h_ref[j, pl.ds(r1, STATE), :] = hs[j]
        return tuple(hs)

    last = lax.fori_loop(0, CHUNK // 8, again, tuple(hck_ref[0][:, c] for c in cols))

    def back(g, carry):
        carry = [list(c) for c in carry]
        aa, hs, acc = carry
        t0 = pl.multiple_of(CHUNK - 8 - g * 8, 8)
        for i in reversed(range(8)):
            t = t0 + i
            r0 = pl.multiple_of(t * STATE, STATE)
            q0 = pl.multiple_of(t * 8, 8)
            b = bx_ref[pl.ds(r0, STATE), :]
            c = cx_ref[pl.ds(r0, STATE), :]
            gb, gc = None, None
            for j in range(groups):
                gyj = gy_ref[j, pl.ds(t, 1), :]
                a = c * gyj + aa[j]
                dec = dec_ref[j, pl.ds(r0, STATE), :]
                before = h_ref[j, pl.ds(r0, STATE), :]
                carry_a = dec * a
                p = carry_a * before * rates[j]
                ab = a * b
                pq_ref[j, pl.ds(q0, 8), :] = p[:8] + p[8:]
                gq_ref[j, pl.ds(q0, 8), :] = ab[:8] + ab[8:]
                acc[j] = acc[j] + p * dl_ref[j, pl.ds(t, 1), :]
                gbj = a * dx_ref[j, pl.ds(t, 1), :]
                gcj = gyj * hs[j]
                gb = gbj if gb is None else gb + gbj
                gc = gcj if gc is None else gc + gcj
                aa[j] = carry_a
                hs[j] = before
            gb_ref[pl.ds(r0, STATE), :] = gb
            gc_ref[pl.ds(r0, STATE), :] = gc
        return tuple(tuple(c) for c in carry)

    aa, _, acc = lax.fori_loop(
        0, CHUNK // 8, back,
        (tuple(a_ref[:, c] for c in cols), last, tuple(jnp.zeros((STATE, LANES), F32) for _ in cols)))
    for j in range(groups):
        a_ref[:, cols[j]] = aa[j]
        galog_ref[:, cols[j]] += acc[j]

    skip = skip_ref[l : l + 1, :]
    gdts = []
    for j in range(groups):
        psum = pq_ref[j, pl.ds(0, CHUNK, stride=8), :]
        gsum = gq_ref[j, pl.ds(0, CHUNK, stride=8), :]
        for k in range(1, 8):
            psum = psum + pq_ref[j, pl.ds(k, CHUNK, stride=8), :]
            gsum = gsum + gq_ref[j, pl.ds(k, CHUNK, stride=8), :]
        dl = delta[:, cols[j]]
        gdelta = psum + xs[:, cols[j]] * gsum
        gxs_ref[:, cols[j]] = dl * gsum + skip[:, cols[j]] * gy[:, cols[j]]
        gdts.append(gdelta * dl * (1.0 - dl * (1.0 / dt_most)))
    gdt = jnp.concatenate(gdts, axis=1)
    gdtb_ref[...] += jnp.sum(gdt, axis=0, keepdims=True)
    gdt_low = gdt.astype(BF16)
    gdtw_ref[...] += dot(proj[:DT_RANK], gdt_low)
    gproj_ref[:DT_RANK, :] = dot_nt(dtw_ref[l], gdt_low)
    wide_b = jnp.concatenate([gb_ref[pl.ds(n, CHUNK, stride=STATE), :].astype(BF16) for n in range(STATE)], axis=1)
    gproj_ref[DT_RANK : DT_RANK + STATE, :] = dot_nt(spread_ref[...], wide_b)
    wide_c = jnp.concatenate([gc_ref[pl.ds(n, CHUNK, stride=STATE), :].astype(BF16) for n in range(STATE)], axis=1)
    gproj_ref[DT_RANK + STATE :, :] = dot_nt(spread_ref[...], wide_c)


def scan_bwd(l, xs, zg, proj, since, ys, gg, hck, dtw, dtb, alog, skip, spread):
    rows, ch = xs.shape
    steps = rows // CHUNK
    row = lambda w: pl.BlockSpec((CHUNK, w), lambda i: (steps - 1 - i, 0))
    full = lambda s: pl.BlockSpec(s, lambda i: (0,) * len(s))
    big = lambda: pltpu.VMEM((CHUNK * STATE, LANES), F32)
    g = ch // LANES
    return pl.pallas_call(
        functools.partial(scan_bwd_kernel, l),
        grid=(steps,),
        out_shape=[
            jax.ShapeDtypeStruct((rows, ch), F32),
            jax.ShapeDtypeStruct((rows, ch), BF16),
            jax.ShapeDtypeStruct((PROJ, rows), F32),
            jax.ShapeDtypeStruct((DT_RANK, ch), F32),
            jax.ShapeDtypeStruct((1, ch), F32),
            jax.ShapeDtypeStruct((STATE, ch), F32),
            jax.ShapeDtypeStruct((1, ch), F32),
        ],
        in_specs=[row(ch), row(ch), pl.BlockSpec((PROJ, CHUNK), lambda i: (0, steps - 1 - i)), row(1), row(ch), row(ch),
                  pl.BlockSpec((1, STATE, ch), lambda i: (steps - 1 - i, 0, 0))]
        + [full(v.shape) for v in (dtw, dtb, alog, skip, spread)],
        out_specs=[row(ch), row(ch), pl.BlockSpec((PROJ, CHUNK), lambda i: (0, steps - 1 - i)), full((DT_RANK, ch)), full((1, ch)), full((STATE, ch)), full((1, ch))],
        scratch_shapes=[
            pltpu.VMEM((STATE, ch), F32),
            pltpu.VMEM((ch // LANES, CHUNK, LANES), F32),
            pltpu.VMEM((ch // LANES, CHUNK, LANES), F32),
            pltpu.VMEM((ch // LANES, CHUNK, LANES), F32),
            pltpu.VMEM((ch // LANES, CHUNK, LANES), F32),
            big(), big(),
            pltpu.VMEM((g, CHUNK * STATE + STATE, LANES), F32),
            pltpu.VMEM((g, CHUNK * STATE, LANES), F32),
            pltpu.VMEM((g, CHUNK * 8, LANES), F32),
            pltpu.VMEM((g, CHUNK * 8, LANES), F32),
            big(), big(),
        ],
        compiler_params=pltpu.CompilerParams(vmem_limit_bytes=60 << 20),
        name="scan_bwd",
    )(xs, zg, proj, since, ys, gg, hck, dtw, dtb, alog, skip, spread)


def rms_inverse(values):
    return lax.rsqrt(jnp.mean(values * values, axis=-1, keepdims=True) + epsilon)


def norm_back(values, inverse, gain, grad):
    scaled = grad * gain
    pulled = inverse * scaled - values * (inverse * inverse * inverse) * jnp.mean(scaled * values, axis=-1, keepdims=True)
    return pulled, jnp.sum(grad * values * inverse, axis=0, keepdims=True)


GELU_A, GELU_B = 0.7978845608028654, 0.044715


def gelu(v):
    return 0.5 * v * (1.0 + jnp.tanh(GELU_A * (v + GELU_B * v * v * v)))


def gelu_slope(v):
    square = v * v
    t = jnp.tanh(GELU_A * v * (1.0 + GELU_B * square))
    return 0.5 * (1.0 + t) + 0.5 * v * (1.0 - t * t) * GELU_A * (1.0 + 3.0 * GELU_B * square)


def by_lane(m, values):
    picked = jnp.int32(values[0])
    for k in range(1, len(values)):
        picked = jnp.where(m == k, jnp.int32(values[k]), picked)
    return picked


def nearest_first(m, lanes):
    orders = [sorted((s for s in range(lanes) if s != k), key=lambda s: (abs(s - k), s)) for k in range(lanes)]
    return [by_lane(m, [order[i] for order in orders]) for i in range(lanes - 1)]


def chain_order(m, lanes):
    def due(k, s):
        return (lanes - 1 - s) + k if s > k else s + (lanes - 1 - k)

    orders = [sorted((s for s in range(lanes) if s != k), key=lambda s: (due(k, s), s)) for k in range(lanes)]
    return [by_lane(m, [order[i] for order in orders]) for i in range(lanes - 1)]


def greet(d, m, lanes, peers, across):
    barrier = pltpu.get_barrier_semaphore()
    if across:
        for k in range(1, lanes):
            pl.semaphore_signal(barrier, inc=1, device_id=(d, lax.rem(m + k, lanes)), device_id_type=MESH)
        for k in range(1, peers):
            pl.semaphore_signal(barrier, inc=1, device_id=(lax.rem(d + k, peers), m), device_id_type=MESH)
        pl.semaphore_wait(barrier, lanes + peers - 2)
    else:

        @pl.when(m > 0)
        def _():
            pl.semaphore_signal(barrier, inc=1, device_id=(d, m - 1), device_id_type=MESH)

        @pl.when(m < lanes - 1)
        def _():
            pl.semaphore_signal(barrier, inc=1, device_id=(d, m + 1), device_id_type=MESH)

        pl.semaphore_wait(barrier, jnp.where(m > 0, 1, 0) + jnp.where(m < lanes - 1, 1, 0))


class LineGather:
    def __init__(self, buf, send, recv, d, m, lanes):
        self.buf, self.send, self.recv, self.d, self.m, self.lanes = buf, send, recv, d, m, lanes
        self.order = nearest_first(m, lanes)

    def copy(self, s, up):
        return pltpu.make_async_remote_copy(
            src_ref=self.buf.at[s], dst_ref=self.buf.at[s], send_sem=self.send.at[0 if up else 1, s],
            recv_sem=self.recv.at[s], device_id=(self.d, self.m + 1 if up else self.m - 1), device_id_type=MESH,
        )

    def start(self):
        @pl.when(self.m < self.lanes - 1)
        def _():
            self.copy(self.m, True).start()

        @pl.when(self.m > 0)
        def _():
            self.copy(self.m, False).start()

    def arrive(self, i):
        s, m = self.order[i], self.m
        self.copy(s, True).wait_recv()

        @pl.when((s < m) & (m < self.lanes - 1))
        def _():
            self.copy(s, True).start()

        @pl.when((s > m) & (m > 0))
        def _():
            self.copy(s, False).start()

        return s

    def finish(self):
        for s in range(self.lanes):

            @pl.when((s <= self.m) & (self.m < self.lanes - 1))
            def _():
                self.copy(s, True).wait_send()

            @pl.when((s >= self.m) & (self.m > 0))
            def _():
                self.copy(s, False).wait_send()


PIECES = 1


class LineReduce:
    def __init__(self, stage, inbox, send, recv, d, m, lanes):
        self.stage, self.inbox, self.send, self.recv = stage, inbox, send, recv
        self.d, self.m, self.lanes = d, m, lanes
        self.rows = stage.shape[1] // PIECES
        self.order = chain_order(m, lanes)
        self.middle = jnp.logical_and(m > 0, m < lanes - 1)
        self.at_end = jnp.logical_not(self.middle)

    def piece(self, p):
        return pl.ds(p * self.rows, self.rows)

    def copy(self, s, p):
        up = s > self.m
        side = jnp.where(up, 0, 1)
        return pltpu.make_async_remote_copy(
            src_ref=self.stage.at[s, self.piece(p)], dst_ref=self.inbox.at[side, s, self.piece(p)], send_sem=self.send.at[s, p],
            recv_sem=self.recv.at[side, s, p], device_id=(self.d, jnp.where(up, self.m + 1, self.m - 1)), device_id_type=MESH,
        )

    def push_first(self, s, term):
        self.stage[s] = term.astype(BF16)
        for p in range(PIECES):
            self.copy(s, p).start()

    def push_on(self, s, p, term):
        side = jnp.where(s > self.m, 0, 1)
        self.copy(s, p).wait_recv()
        self.stage[s, self.piece(p)] = (term + self.inbox[side, s, self.piece(p)].astype(F32)).astype(BF16)
        self.copy(s, p).start()

    def push(self, s, term):
        @pl.when(self.at_end)
        def _():
            self.push_first(s, term)

        @pl.when(self.middle)
        def _():
            for p in range(PIECES):
                self.push_on(s, p, term[p * self.rows : (p + 1) * self.rows])

    def total(self, own_ref):
        m = self.m

        def add(side):
            for p in range(PIECES):
                pltpu.make_async_remote_copy(
                    src_ref=self.stage.at[m, self.piece(p)], dst_ref=self.inbox.at[side, m, self.piece(p)], send_sem=self.send.at[m, p],
                    recv_sem=self.recv.at[side, m, p], device_id=(self.d, m), device_id_type=MESH,
                ).wait_recv()
            own_ref[...] += self.inbox[side, m].astype(F32)

        @pl.when(m > 0)
        def _():
            add(0)

        @pl.when(m < self.lanes - 1)
        def _():
            add(1)

    def finish(self):
        for s in self.order:
            for p in range(PIECES):
                self.copy(s, p).wait_send()


def reduce_scratch(lanes, rows, width):
    return [
        pltpu.VMEM((lanes, rows, width), BF16),
        pltpu.VMEM((2, lanes, rows, width), BF16),
        dma(lanes, PIECES), dma(2, lanes, PIECES),
    ]


PARTS = 2


def line_sum(part, stage, inbox, send, recv, out, d, m, lanes, between=lambda: None):
    width = part.shape[1] // PARTS

    def copy(side, b):
        return pltpu.make_async_remote_copy(
            src_ref=stage.at[side, b], dst_ref=inbox.at[side, b], send_sem=send.at[side, b], recv_sem=recv.at[side, b],
            device_id=(d, m + 1 if side == 0 else m - 1), device_id_type=MESH,
        )

    def step(side, b):
        has_source = m > 0 if side == 0 else m < lanes - 1
        has_target = m < lanes - 1 if side == 0 else m > 0
        cols = slice(b * width, (b + 1) * width)

        @pl.when(has_source)
        def _():
            copy(side, b).wait_recv()

        @pl.when(jnp.logical_not(has_source))
        def _():
            inbox[side, b] = jnp.zeros(inbox.shape[2:], BF16)

        @pl.when(has_target)
        def _():
            stage[side, b] = (part[:, cols] + inbox[side, b].astype(F32)).astype(BF16)
            copy(side, b).start()

    low = 2 * m < lanes

    def both(first):
        def run(side):
            for b in range(PARTS):
                step(side, b)

        @pl.when(low)
        def _():
            run(0 if first else 1)

        @pl.when(jnp.logical_not(low))
        def _():
            run(1 if first else 0)

    both(True)
    between()
    both(False)
    for b in range(PARTS):
        cols = slice(b * width, (b + 1) * width)
        out[:, cols] = (part[:, cols] + inbox[0, b].astype(F32) + inbox[1, b].astype(F32)).astype(BF16)

    def finish():
        for b in range(PARTS):

            @pl.when(m < lanes - 1)
            def _():
                copy(0, b).wait_send()

            @pl.when(m > 0)
            def _():
                copy(1, b).wait_send()

    return finish


def vmem(count):
    return [pl.BlockSpec(memory_space=pltpu.VMEM)] * count


def f32(*shape):
    return jax.ShapeDtypeStruct(shape, F32)


def bf16(*shape):
    return jax.ShapeDtypeStruct(shape, BF16)


def dma(*shape):
    return pltpu.SemaphoreType.DMA(shape)


def hbm(count):
    return [pl.BlockSpec(memory_space=pl.ANY)] * count


def fetch(pairs, sem):
    copies = [pltpu.make_async_copy(src, dst, sem.at[i]) for i, (src, dst) in enumerate(pairs)]
    for copy in copies:
        copy.start()
    return copies


def params(cid, limit=58):
    return pltpu.CompilerParams(collective_id=cid, has_side_effects=True, vmem_limit_bytes=limit << 20)


CONV_ROWS = 128
HEAD = 8


def conv_window(padded_ref, since_ref, taps, bias, base):
    window = padded_ref[pl.ds(base, CONV_ROWS + HEAD), :]
    since = since_ref[pl.ds(base, CONV_ROWS), :]
    shifted = [window[HEAD:]]
    for j in range(1, CONV):
        shifted.append(window[HEAD - j : HEAD - j + CONV_ROWS] * (since >= j).astype(F32))
    pre = bias
    for j in range(CONV):
        pre = pre + taps[CONV - 1 - j : CONV - j, :] * shifted[j]
    return pre, shifted


class Experts:
    def __init__(self, d, m, lanes, peers, into_ref, rows_ref, pack_ref, slots_ref, part_ref, back_ref, stage_ref, inbox_ref,
                 gsend, grecv, dsend, drecv, bsend, brecv, rsend, rrecv):
        self.d, self.m, self.lanes, self.peers = d, m, lanes, peers
        self.rows, self.into, self.pack, self.slots, self.part, self.back = rows_ref, into_ref, pack_ref, slots_ref, part_ref, back_ref
        self.stage, self.inbox = stage_ref, inbox_ref
        self.dsend, self.drecv, self.bsend, self.brecv, self.rsend, self.rrecv = dsend, drecv, bsend, brecv, rsend, rrecv
        self.sets = rows_ref.shape[1]
        self.cap = pack_ref.shape[2] // self.sets
        self.width = rows_ref.shape[3]
        self.gather = LineGather(rows_ref, gsend, grecv, d, m, lanes)

    def slot_rows(self, ref, s, i):
        return ref[s, :, i * self.cap : (i + 1) * self.cap, :].reshape(self.peers * self.cap, self.width)

    def set_slot_rows(self, ref, s, i, value):
        ref[s, :, i * self.cap : (i + 1) * self.cap, :] = value.reshape(self.peers, self.cap, self.width)

    def hop(self, src, dst, send, recv, s, k):
        other = lax.rem(self.d + k, self.peers)
        return pltpu.make_async_remote_copy(
            src_ref=src.at[s, other], dst_ref=dst.at[s, self.d], send_sem=send.at[s, k - 1],
            recv_sem=recv.at[s, k - 1], device_id=(other, self.m), device_id_type=MESH,
        )

    def across(self, src, dst, send, recv, s):
        for k in range(1, self.peers):
            self.hop(src, dst, send, recv, s, k).start()
        dst[s, self.d] = src[s, self.d]

    def dispatch(self, s):
        for i in range(self.sets):
            self.set_slot_rows(self.pack, s, i, dot(self.into[s], self.rows[s, i]).astype(BF16))
        self.across(self.pack, self.slots, self.dsend, self.drecv, s)

    def answer(self, s, expert):
        for k in range(1, self.peers):
            self.hop(self.pack, self.slots, self.dsend, self.drecv, s, k).wait_recv()
        for i, value in enumerate(expert(s, [self.slot_rows(self.slots, s, i) for i in range(self.sets)])):
            self.set_slot_rows(self.part, s, i, value.astype(BF16))
        self.across(self.part, self.back, self.bsend, self.brecv, s)

    def home(self, s):
        return pltpu.make_async_remote_copy(
            src_ref=self.stage.at[s], dst_ref=self.inbox.at[self.m], send_sem=self.rsend.at[s], recv_sem=self.rrecv.at[self.m],
            device_id=(self.d, s), device_id_type=MESH,
        )

    def combine(self, s):
        for k in range(1, self.peers):
            self.hop(self.part, self.back, self.bsend, self.brecv, s, k).wait_recv()
        return [dot_tn(self.into[s], self.slot_rows(self.back, s, i)) for i in range(self.sets)]

    def combine_away(self, s):
        for i, value in enumerate(self.combine(s)):
            self.stage[s, i] = value.astype(BF16)
        self.home(s).start()

    def run(self, expert, own_ref, meanwhile):
        one, two, three = self.gather.order
        self.gather.start()
        self.dispatch(self.m)
        self.gather.arrive(0)
        self.dispatch(one)
        self.gather.arrive(1)
        self.dispatch(two)
        self.answer(one, expert)
        self.gather.arrive(2)
        self.dispatch(three)
        self.answer(two, expert)
        self.combine_away(one)
        self.answer(three, expert)
        self.combine_away(two)
        self.answer(self.m, expert)
        self.combine_away(three)
        for i, value in enumerate(self.combine(self.m)):
            own_ref[i] = value
        meanwhile()
        for s in (one, two, three):
            pltpu.make_async_remote_copy(
                src_ref=self.stage.at[s], dst_ref=self.inbox.at[s], send_sem=self.rsend.at[s], recv_sem=self.rrecv.at[s],
                device_id=(self.d, s), device_id_type=MESH,
            ).wait_recv()
            own_ref[...] += self.inbox[s].astype(F32)

    def finish(self):
        self.gather.finish()
        order = [self.m, *self.gather.order]
        for s in order:
            for k in range(1, self.peers):
                self.hop(self.pack, self.slots, self.dsend, self.drecv, s, k).wait_send()
                self.hop(self.part, self.back, self.bsend, self.brecv, s, k).wait_send()
        for s in order[1:]:
            self.home(s).wait_send()


def large(v):
    return v.size * v.dtype.itemsize >= 1 << 17


class Refs(types.SimpleNamespace):
    def need(self, *refs):
        for ref in refs:
            if id(ref) in self.coming:
                self.coming.pop(id(ref)).wait()

    def ship(self, *refs):
        for ref in refs:
            self.gone.append(self.going.pop(id(ref)))
            self.gone[-1].start()


def launch(name, cid, body, inputs, far, outputs, scratch, limit=58):
    near = {k: v for k, v in inputs.items() if not large(v)}
    lazy = {k: v for k, v in inputs.items() if large(v)}
    prompt = {k: v for k, v in outputs.items() if not large(v)}
    late = {k: v for k, v in outputs.items() if large(v)}
    buffers = {k: pltpu.VMEM(v.shape, v.dtype) for k, v in {**lazy, **late}.items()}
    away = [k + "_far" for k in (*lazy, *late)]
    names = [*near, *away[: len(lazy)], *far, *prompt, *away[len(lazy) :], *scratch, *buffers, "moves"]

    def kernel(*refs):
        r = Refs(**dict(zip(names, refs)))
        get = lambda k: getattr(r, k)
        r.gone = []
        r.coming = {id(get(k)): pltpu.make_async_copy(get(k + "_far"), get(k), r.moves.at[i]) for i, k in enumerate(lazy)}
        r.going = {id(get(k)): pltpu.make_async_copy(get(k), get(k + "_far"), r.moves.at[len(lazy) + i]) for i, k in enumerate(late)}
        for copy in r.coming.values():
            copy.start()
        body(r)
        r.need(*map(get, lazy))
        r.ship(*(get(k) for k in late if id(get(k)) in r.going))
        for copy in r.gone:
            copy.wait()

    results = pl.pallas_call(
        kernel,
        out_shape=[*prompt.values(), *late.values()],
        in_specs=vmem(len(near)) + hbm(len(lazy) + len(far)),
        out_specs=vmem(len(prompt)) + hbm(len(late)),
        scratch_shapes=[*scratch.values(), *buffers.values(), dma(max(1, len(lazy) + len(late)))],
        compiler_params=params(cid, limit),
        name=name,
    )(*near.values(), *lazy.values(), *far.values())
    return types.SimpleNamespace(**dict(zip([*prompt, *late], results)))


def convolution(small):
    return dict(norm_in=small.norm_in, conv_w=small.conv_w, conv_b=small.conv_b, since=small.since, x_proj=small.x_proj)


def routing(small):
    return dict(norm_moe=small.norm_moe, router=small.router)


def flat(ref):
    return ref[...].reshape(ref.shape[0] * ref.shape[1], ref.shape[2])


def gate_of(chance, choose):
    return jnp.sum(chance * choose, axis=1, keepdims=True)


class Sizes:
    def __init__(self, lanes, peers, experts, cap, rows, width, channels, hidden):
        self.lanes, self.peers, self.experts, self.cap = lanes, peers, experts, cap
        self.rows, self.width, self.channels, self.hidden = rows, width, channels, hidden
        self.total, self.slots = rows * lanes, experts * cap


def in_outputs(z):
    return dict(whole=bf16(z.lanes, z.rows, z.width), conv=f32(z.total + HEAD, z.channels), zgate=f32(z.total, z.channels),
                xs=f32(z.total, z.channels), proj=bf16(PROJ, z.total))


def sum_scratch(z):
    halves = pltpu.VMEM((2, PARTS, PROJ, z.total // PARTS), BF16)
    return dict(sum_stage=halves, sum_inbox=halves, sum_send=dma(2, PARTS), sum_recv=dma(2, PARTS))


def in_scratch(z):
    return dict(part=pltpu.VMEM((PROJ, z.total), F32), u_send=dma(2, z.lanes), u_recv=dma(z.lanes), **sum_scratch(z))


def in_stage(z, r, l, act, weights):
    d, m = lax.axis_index("dp"), lax.axis_index("mp")
    r.whole[m] = (act * rms_inverse(act) * r.norm_in[l : l + 1, :]).astype(BF16)
    gather = LineGather(r.whole, r.u_send, r.u_recv, d, m, z.lanes)
    gather.start()
    r.conv[:HEAD, :] = jnp.zeros((HEAD, z.channels), F32)
    weights.wait()

    def project(s):
        u = r.whole[s]
        r.conv[pl.ds(pl.multiple_of(s * z.rows + HEAD, 8), z.rows), :] = dot(u, r.win[0])
        r.zgate[pl.ds(pl.multiple_of(s * z.rows, 8), z.rows), :] = dot(u, r.win[1])

    project(m)
    for i in range(z.lanes - 1):
        project(gather.arrive(i))
    r.ship(r.conv, r.zgate, r.whole)
    taps, bias = r.conv_w[l], r.conv_b[l : l + 1, :]

    def conv_step(c, carry):
        base = pl.multiple_of(c * CONV_ROWS, CONV_ROWS)
        pre, _ = conv_window(r.conv, r.since, taps, bias, base)
        xs = pre * sigmoid(pre)
        r.xs[pl.ds(base, CONV_ROWS), :] = xs
        r.part[:, pl.ds(base, CONV_ROWS)] = dot_nt(r.x_proj[l], xs.astype(BF16))
        return carry

    lax.fori_loop(0, z.total // CONV_ROWS, conv_step, 0)
    r.ship(r.xs)
    finish = line_sum(r.part, r.sum_stage, r.sum_inbox, r.sum_send, r.sum_recv, r.proj, d, m, z.lanes)
    gather.finish()
    finish()


def first_block(z, l, act, small, w_in):
    def body(r):
        d, m = lax.axis_index("dp"), lax.axis_index("mp")
        (weights,) = fetch([(r.w_in.at[l], r.win)], r.fetched)
        greet(d, m, z.lanes, 0, False)
        r.need(r.act)
        in_stage(z, r, l, r.act[...].astype(F32), weights)

    inputs = dict(act=act, **convolution(small))
    return launch("mamba_in", 0, body, inputs, dict(w_in=w_in), in_outputs(z),
                  dict(win=pltpu.VMEM(w_in.shape[1:], BF16), fetched=dma(1), **in_scratch(z)))


def expert_refs(r):
    return (r.e_rows, r.e_pack, r.e_slots, r.e_part, r.e_back, r.e_stage, r.e_inbox, r.e_gs, r.e_gr, r.e_ds, r.e_dr, r.e_bs, r.e_br,
            r.e_rs, r.e_rr)


def expert_names(z, sets):
    across = pltpu.VMEM((z.lanes, z.peers, sets * z.cap, z.width), BF16)
    along = pltpu.VMEM((z.lanes, sets, z.rows, z.width), BF16)
    plane, line = dma(z.lanes, z.peers - 1), dma(z.lanes)
    return dict(
        e_rows=along, e_pack=across, e_slots=across, e_part=across, e_back=across, e_stage=along, e_inbox=along, e_gs=dma(2, z.lanes),
        e_gr=line, e_ds=plane, e_dr=plane, e_bs=plane, e_br=plane, e_rs=line, e_rr=line, e_own=pltpu.VMEM((sets, z.rows, z.width), F32))


def weight_scratch(wout, wup, wdown):
    return dict(wout=pltpu.VMEM(wout.shape[1:], BF16), wup=pltpu.VMEM(wup.shape[2:], BF16), wdown=pltpu.VMEM(wdown.shape[2:], BF16))


def out_scratch(z, place):
    stage, inbox, send, recv = reduce_scratch(z.lanes, z.rows, z.width)
    return dict(m_stage=stage, m_inbox=inbox, m_send=send, m_recv=recv, places=pltpu.VMEM((z.lanes, *place.shape), jnp.int32),
                p_send=dma(2, z.lanes), p_recv=dma(z.lanes), m_own=pltpu.VMEM((z.rows, z.width), F32))


def out_stage(z, r, l, wout):
    d, m = lax.axis_index("dp"), lax.axis_index("mp")
    r.places[m] = r.place[...]
    places = LineGather(r.places, r.p_send, r.p_recv, d, m, z.lanes)
    places.start()
    reduce = LineReduce(r.m_stage, r.m_inbox, r.m_send, r.m_recv, d, m, z.lanes)
    wout.wait()
    r.need(r.act, r.gated)
    for s in reduce.order:
        reduce.push(s, dot(r.gated[s], r.wout[...]))
    r.m_own[...] = r.act[...].astype(F32) + dot(r.gated[m], r.wout[...])

    def spread_places(s):
        numbers = lax.broadcasted_iota(jnp.int32, (z.slots, z.rows), 0)
        r.into[s] = (numbers == r.places[s][:1, : z.rows]).astype(F32).astype(BF16)

    spread_places(m)
    owner = lax.broadcasted_iota(jnp.int32, (z.slots, z.experts), 0) // z.cap == lax.broadcasted_iota(jnp.int32, (z.slots, z.experts), 1)
    r.choose[...] = dot_tn(r.into[m], owner.astype(F32).astype(BF16))
    for i in range(z.lanes - 1):
        spread_places(places.arrive(i))
    reduce.total(r.m_own)

    def finish():
        places.finish()
        reduce.finish()

    return finish


def chances(z, normed, table):
    logits = lax.dot_general(normed, table, (((1,), (1,)), ((), ())), precision=highest, preferred_element_type=F32)
    raised = jnp.exp(logits - jnp.max(logits, axis=1, keepdims=True))
    return raised / jnp.sum(raised, axis=1, keepdims=True)


def middle_block(z, l, act, gated, small, weights):
    def body(r):
        d, m = lax.axis_index("dp"), lax.axis_index("mp")
        wout, wup, wdown, win = fetch([(r.w_out.at[l], r.wout), (r.w_up.at[l, 0], r.wup), (r.w_down.at[l, 0], r.wdown),
                                       (r.w_in.at[l + 1], r.win)], r.fetched)
        greet(d, m, z.lanes, z.peers, True)
        finish = out_stage(z, r, l, wout)
        wup.wait()
        wdown.wait()
        middle = r.m_own[...]
        r.middle[...] = middle
        r.e_rows[m, 0] = (middle * rms_inverse(middle) * r.norm_moe[l : l + 1, :]).astype(BF16)
        moe = Experts(d, m, z.lanes, z.peers, r.into, *expert_refs(r))

        def expert(s, rows):
            r.slots[s] = rows[0]
            hidden = dot(rows[0], r.wup[...])
            r.hidden[s] = hidden.astype(BF16)
            active = gelu(hidden).astype(BF16)
            r.active[s] = active
            return [dot(active, r.wdown[...])]

        def meanwhile():
            finish()
            middle = r.middle[...]
            r.chance[...] = chances(z, middle * rms_inverse(middle) * r.norm_moe[l : l + 1, :], r.router[l])

        moe.run(expert, r.e_own, meanwhile)
        r.ship(r.into, r.middle, r.slots, r.hidden, r.active)
        picked = r.e_own[0].astype(BF16)
        r.picked[...] = picked
        following = r.middle[...] + gate_of(r.chance[...], r.choose[...]) * picked.astype(F32)
        r.following[...] = following
        r.ship(r.picked, r.following)
        in_stage(z, r, l + 1, following, win)
        moe.finish()

    w_in, w_out, w_up, w_down = weights
    slots = (z.lanes, z.slots)
    return launch(
        "middle", 1 + l, body, dict(act=act, gated=gated, place=small.place, **routing(small), **convolution(small)),
        dict(w_in=w_in, w_out=w_out, w_up=w_up, w_down=w_down),
        dict(middle=f32(z.rows, z.width), chance=f32(z.rows, z.experts), into=bf16(*slots, z.rows), slots=bf16(*slots, z.width),
             hidden=bf16(*slots, z.hidden), active=bf16(*slots, z.hidden), picked=bf16(z.rows, z.width), choose=f32(z.rows, z.experts), following=f32(z.rows, z.width),
             **in_outputs(z)),
        dict(win=pltpu.VMEM(w_in.shape[1:], BF16), fetched=dma(4), **weight_scratch(w_out, w_up, w_down), **out_scratch(z, small.place),
             **expert_names(z, 1), **in_scratch(z)))


def back_outputs(z):
    return dict(gmid=f32(z.rows, z.width), gup=f32(z.width, z.hidden), gdown=f32(z.hidden, z.width), ggated=f32(z.lanes, z.rows, z.channels),
                gwout=bf16(z.channels, z.width), gshare=f32(z.experts + 8, z.width))


def back_scratch(z):
    return dict(wide=pltpu.VMEM((z.lanes, z.rows, z.width), BF16), w_send=dma(2, z.lanes), w_recv=dma(z.lanes))


def route_back(z, r, l, upstream, middle, chance, choose, picked, returned):
    d, m = lax.axis_index("dp"), lax.axis_index("mp")
    gate = gate_of(chance, choose)
    inverse, gain = rms_inverse(middle), r.norm_moe[l : l + 1, :]
    grad_gate = jnp.sum(upstream * picked.astype(F32), axis=1, keepdims=True)
    grad_logit = gate * grad_gate * (choose - chance)
    grad_normed = returned.astype(BF16).astype(F32) + lax.dot_general(
        grad_logit, r.router[l], (((1,), (0,)), ((), ())), precision=highest, preferred_element_type=F32)
    pulled, grad_gain = norm_back(middle, inverse, gain, grad_normed)
    grad_middle = upstream + pulled
    r.gmid[...] = grad_middle
    r.ship(r.gmid)
    r.wide[m] = grad_middle.astype(BF16)
    gather = LineGather(r.wide, r.w_send, r.w_recv, d, m, z.lanes)
    gather.start()
    grad_router = lax.dot_general(
        grad_logit, middle * inverse * gain, (((0,), (0,)), ((), ())), precision=highest, preferred_element_type=F32)
    r.gshare[: z.experts, :] = grad_router
    r.gshare[z.experts :, :] = jnp.broadcast_to(grad_gain, (8, z.width))

    def gate_back(s):
        r.ggated[s] = dot_nt(r.wide[s], r.wout[...])

    gate_back(m)
    for i in range(z.lanes - 1):
        gate_back(gather.arrive(i))
    r.ship(r.ggated)
    r.need(r.gated)
    r.gwout[...] = dot_tn(flat(r.gated), flat(r.wide)).astype(BF16)
    gather.finish()


def turn_block(z, l, act, gated, cotangent, small, weights):
    def body(r):
        d, m = lax.axis_index("dp"), lax.axis_index("mp")
        wout, wup, wdown = fetch([(r.w_out.at[l], r.wout), (r.w_up.at[l, 0], r.wup), (r.w_down.at[l, 0], r.wdown)], r.fetched)
        greet(d, m, z.lanes, z.peers, True)
        finish = out_stage(z, r, l, wout)
        wup.wait()
        wdown.wait()
        middle = r.m_own[...]
        normed = middle * rms_inverse(middle) * r.norm_moe[l : l + 1, :]
        r.e_rows[m, 0] = normed.astype(BF16)
        chance = chances(z, normed, r.router[l])
        r.chance[...] = chance
        r.need(r.cotangent)
        r.e_rows[m, 1] = (gate_of(chance, r.choose[...]) * r.cotangent[...].astype(F32)).astype(BF16)
        moe = Experts(d, m, z.lanes, z.peers, r.into, *expert_refs(r))

        def expert(s, rows):
            hidden = dot(rows[0], r.wup[...])
            active = gelu(hidden).astype(BF16)
            r.active[s] = active
            grad_hidden = (dot_nt(rows[1], r.wdown[...]) * gelu_slope(hidden)).astype(BF16)
            r.ghid[s] = grad_hidden
            return [dot(active, r.wdown[...]), dot_nt(grad_hidden, r.wup[...])]

        def meanwhile():
            finish()
            for s in range(z.lanes):
                down = dot_tn(r.active[s], moe.slot_rows(moe.slots, s, 1))
                r.gdown[...] = down if s == 0 else r.gdown[...] + down
                up = dot_tn(moe.slot_rows(moe.slots, s, 0), r.ghid[s])
                r.gup[...] = up if s == 0 else r.gup[...] + up
            r.ship(r.gdown, r.gup)

        moe.run(expert, r.e_own, meanwhile)
        picked = r.e_own[0].astype(BF16)
        r.following[...] = r.m_own[...] + gate_of(r.chance[...], r.choose[...]) * picked.astype(F32)
        r.ship(r.following)
        route_back(z, r, l, r.cotangent[...].astype(F32), r.m_own[...], r.chance[...], r.choose[...], picked, r.e_own[1])
        moe.finish()

    w_in, w_out, w_up, w_down = weights
    slots = (z.lanes, z.slots)
    return launch(
        "turn", 8, body, dict(act=act, gated=gated, cotangent=cotangent, place=small.place, **routing(small)),
        dict(w_out=w_out, w_up=w_up, w_down=w_down),
        dict(following=f32(z.rows, z.width), **back_outputs(z)),
        dict(fetched=dma(3), choose=pltpu.VMEM((z.rows, z.experts), F32), chance=pltpu.VMEM((z.rows, z.experts), F32), into=pltpu.VMEM((*slots, z.rows), BF16),
             active=pltpu.VMEM((*slots, z.hidden), BF16), ghid=pltpu.VMEM((*slots, z.hidden), BF16),
             **weight_scratch(w_out, w_up, w_down), **out_scratch(z, small.place), **expert_names(z, 2), **back_scratch(z)),
        58 if z.slots <= 256 else 61)


class PlaneSum:
    def __init__(self, d, m, peers, mine, pair, half, inbox, result, psend, precv, csend, crecv, gsend, grecv):
        self.m, self.mine, self.pair, self.half, self.inbox, self.result = m, mine, pair, half, inbox, result
        self.psend, self.precv, self.csend, self.crecv, self.gsend, self.grecv = psend, precv, csend, crecv, gsend, grecv
        self.chips = peers // 2
        self.chip, self.core = lax.div(d, 2), lax.rem(d, 2)
        self.rows = mine.shape[0] // 2
        self.block = self.rows // self.chips

    def side(self, core):
        return pl.ds(pl.multiple_of(core * self.rows, 16), self.rows)

    def at(self, chip):
        return pl.ds(pl.multiple_of(chip * self.block, 16), self.block)

    def final(self, chip):
        return pl.ds(pl.multiple_of(self.core * self.rows + chip * self.block, 16), self.block)

    def swap(self, src, dst, i):
        return pltpu.make_async_remote_copy(
            src_ref=src, dst_ref=dst, send_sem=self.psend.at[i], recv_sem=self.precv.at[i],
            device_id=(self.chip * 2 + 1 - self.core, self.m), device_id_type=MESH)

    def first_swap(self):
        return self.swap(self.mine.at[self.side(1 - self.core)], self.pair, 0)

    def last_swap(self):
        return self.swap(self.result.at[self.side(self.core)], self.result.at[self.side(self.core)], 1)

    def other(self, k):
        return lax.rem(self.chip + k, self.chips)

    def scatter(self, k):
        return pltpu.make_async_remote_copy(
            src_ref=self.half.at[self.at(self.other(k))], dst_ref=self.inbox.at[k - 1], send_sem=self.csend.at[k - 1],
            recv_sem=self.crecv.at[k - 1], device_id=(self.other(k) * 2 + self.core, self.m), device_id_type=MESH)

    def gather(self, k):
        return pltpu.make_async_remote_copy(
            src_ref=self.result.at[self.final(self.chip)], dst_ref=self.result.at[self.final(self.chip)], send_sem=self.gsend.at[k - 1],
            recv_sem=self.grecv.at[k - 1], device_id=(self.other(k) * 2 + self.core, self.m), device_id_type=MESH)

    def begin(self):
        self.first_swap().start()

    def second(self):
        self.first_swap().wait_recv()
        self.half[...] = (self.mine[self.side(self.core)].astype(F32) + self.pair[...].astype(F32)).astype(BF16)
        for k in range(1, self.chips):
            self.scatter(k).start()

    def third(self):
        for k in range(1, self.chips):
            self.scatter(k).wait_recv()
        summed = self.half[self.at(self.chip)].astype(F32)
        for k in range(1, self.chips):
            summed = summed + self.inbox[k - 1].astype(F32)
        self.result[self.final(self.chip)] = summed.astype(BF16)
        for k in range(1, self.chips):
            self.gather(k).start()

    def fourth(self):
        for k in range(1, self.chips):
            self.gather(k).wait_recv()
        self.last_swap().start()

    def end(self):
        self.last_swap().wait_recv()

    def finish(self):
        self.first_swap().wait_send()
        self.last_swap().wait_send()
        for k in range(1, self.chips):
            self.scatter(k).wait_send()
            self.gather(k).wait_send()


def plane_scratch(peers, rows, width):
    return [
        pltpu.VMEM((rows, width), BF16),
        pltpu.VMEM((rows // 2, width), BF16),
        pltpu.VMEM((rows // 2, width), BF16),
        pltpu.VMEM((peers // 2 - 1, rows // peers, width), BF16),
        dma(2), dma(2), dma(peers // 2 - 1), dma(peers // 2 - 1), dma(peers // 2 - 1), dma(peers // 2 - 1),
    ]


def exchange(targets, buf, inbox, send, recv):
    copies = [
        pltpu.make_async_remote_copy(src_ref=buf, dst_ref=inbox.at[k], send_sem=send.at[k], recv_sem=recv.at[k],
                                     device_id=target, device_id_type=MESH)
        for k, target in enumerate(targets)
    ]
    for copy in copies:
        copy.start()

    def collect():
        total = buf[...].astype(F32)
        for k, copy in enumerate(copies):
            copy.wait()
            total = total + inbox[k].astype(F32)
        return total

    return collect


def early_rows(width, experts):
    sizes = [width, width, DT_RANK, STATE, 16, experts + 8, experts + 8]
    return [sum(sizes[:i]) for i in range(len(sizes) + 1)]


def late_rows(width):
    sizes = [width, PROJ, 16]
    return [sum(sizes[:i]) for i in range(len(sizes) + 1)]


def whole_blocks(rows, peers):
    return -(-rows // (16 * peers)) * 16 * peers


def in_back_scratch(z, win, last):
    early = whole_blocks(early_rows(z.width, z.experts)[-1], z.peers)
    late = whole_blocks(late_rows(z.width)[-1], z.peers)
    shared = 2 * (z.experts + 8)
    small = -(-2 * (z.width // LANES) // 8) * 8
    stage, inbox, send, recv = reduce_scratch(z.lanes, z.rows, z.width)
    found = dict(
        gproj=pltpu.VMEM((PROJ, z.total), BF16), gpre=pltpu.VMEM((z.total + HEAD, z.channels), F32),
        gxi=pltpu.VMEM((z.total, z.channels), BF16), gconv=pltpu.VMEM((16, z.channels), F32), c_own=pltpu.VMEM((z.rows, z.width), F32),
        win=pltpu.VMEM(win.shape[1:], BF16), z_buf=pltpu.VMEM((shared, z.channels), BF16),
        z_in=pltpu.VMEM((z.lanes - 1, shared, z.channels), BF16), z_send=dma(z.lanes - 1), z_recv=dma(z.lanes - 1),
        c_stage=stage, c_inbox=inbox, c_send=send, c_recv=recv,
        **{"e%d" % i: v for i, v in enumerate(plane_scratch(z.peers, early, z.channels))},
        **{"l%d" % i: v for i, v in enumerate(plane_scratch(z.peers, late, z.channels))},
        **sum_scratch(z),
    )
    if last:
        found.update(
            n_buf=pltpu.VMEM((small, LANES), F32), n_in=pltpu.VMEM((z.peers - 1, small, LANES), F32), n_send=dma(z.peers - 1),
            n_recv=dma(z.peers - 1), n_buf2=pltpu.VMEM((small, LANES), F32), n_in2=pltpu.VMEM((z.lanes - 1, small, LANES), F32),
            n_send2=dma(z.lanes - 1), n_recv2=dma(z.lanes - 1))
    return found


def in_back_outputs(z, last):
    early = whole_blocks(early_rows(z.width, z.experts)[-1], z.peers)
    late = whole_blocks(late_rows(z.width)[-1], z.peers)
    return dict(early=bf16(early, z.channels), late=bf16(late, z.channels), share=f32(2 * (z.experts + 8), z.channels),
                gnorm=f32(2 if last else 1, z.width))


def plane_sum(z, r, which, result):
    d, m = lax.axis_index("dp"), lax.axis_index("mp")
    parts = [getattr(r, which + str(i)) for i in range(10)]
    return PlaneSum(d, m, z.peers, *parts[:4], result, *parts[4:])


def in_back_stage(z, r, l, weights, emit):
    d, m = lax.axis_index("dp"), lax.axis_index("mp")
    line = [(d, lax.rem(m + k, z.lanes)) for k in range(1, z.lanes)]
    early, late = plane_sum(z, r, "e", r.early), plane_sum(z, r, "l", r.late)
    emine, lmine = early.mine, late.mine
    ch = z.channels
    at, till = early_rows(z.width, z.experts), late_rows(z.width)

    def early_work():
        r.need(r.b_whole, r.gzg, r.b_gwout, r.b_gshare)
        whole = r.b_whole[...].reshape(z.total, z.width)
        emine[at[0] : at[1], :] = dot_tn(whole, r.gzg[...]).astype(BF16)
        for i in range(z.width // ch):
            emine[at[1] + i * ch : at[1] + (i + 1) * ch, :] = r.b_gwout[:, i * ch : (i + 1) * ch]
            emine[at[5 + i] : at[6 + i], :] = r.b_gshare[:, i * ch : (i + 1) * ch].astype(BF16)
        emine[at[2] : at[3], :] = r.gdtw[...].astype(BF16)
        emine[at[3] : at[4], :] = r.galog[...].astype(BF16)
        emine[at[4] : at[5], :] = jnp.concatenate([r.gdtb[...], r.gskip[...], jnp.zeros((14, ch), F32)], axis=0).astype(BF16)
        if at[7] < emine.shape[0]:
            emine[at[7] :, :] = jnp.zeros((emine.shape[0] - at[7], ch), BF16)
        early.begin()

    r.need(r.gpart)
    finish_sum = line_sum(r.gpart, r.sum_stage, r.sum_inbox, r.sum_send, r.sum_recv, r.gproj, d, m, z.lanes, early_work)
    taps, bias = r.conv_w[l], r.conv_b[l : l + 1, :]
    r.gconv[...] = jnp.zeros_like(r.gconv)
    r.gpre[z.total :, :] = jnp.zeros((HEAD, ch), F32)

    def first(c, carry):
        base = pl.multiple_of(c * CONV_ROWS, CONV_ROWS)
        pre, shifted = conv_window(r.b_conv, r.since, taps, bias, base)
        sig = sigmoid(pre)
        grad = r.gxs[pl.ds(base, CONV_ROWS), :] + dot_tn(r.gproj[:, pl.ds(base, CONV_ROWS)], r.x_proj[l])
        grad = grad * (sig * (1.0 + pre * (1.0 - sig)))
        r.gpre[pl.ds(base, CONV_ROWS), :] = grad
        for j in range(CONV):
            r.gconv[CONV - 1 - j : CONV - j, :] += jnp.sum(grad * shifted[j], axis=0, keepdims=True)
        r.gconv[CONV : CONV + 1, :] += jnp.sum(grad, axis=0, keepdims=True)
        return carry

    r.need(r.b_conv, r.gxs)
    lax.fori_loop(0, z.total // CONV_ROWS, first, 0)

    def second(c, carry):
        base = pl.multiple_of(c * CONV_ROWS, CONV_ROWS)
        window = r.gpre[pl.ds(base, CONV_ROWS + HEAD), :]
        since = r.since[pl.ds(base, CONV_ROWS + HEAD), :]
        grad = taps[CONV - 1 : CONV, :] * window[:CONV_ROWS]
        for j in range(1, CONV):
            grad = grad + taps[CONV - 1 - j : CONV - j, :] * (window * (since >= j).astype(F32))[j : j + CONV_ROWS]
        r.gxi[pl.ds(base, CONV_ROWS), :] = grad.astype(BF16)
        return carry

    lax.fori_loop(0, z.total // CONV_ROWS, second, 0)
    weights.wait()
    reduce = LineReduce(r.c_stage, r.c_inbox, r.c_send, r.c_recv, d, m, z.lanes)

    def term(s):
        part = pl.ds(pl.multiple_of(s * z.rows, 16), z.rows)
        return dot_nt(r.gxi[part, :], r.win[0]) + dot_nt(r.gzg[part, :], r.win[1])

    def push_middle(s):
        @pl.when(reduce.middle)
        def _():
            for p in range(PIECES):
                reduce.push_on(s, p, term(s)[p * reduce.rows : (p + 1) * reduce.rows])

    one, two, three = reduce.order

    @pl.when(reduce.at_end)
    def _():
        for s in reduce.order:
            reduce.push_first(s, term(s))

    early.second()
    r.need(r.b_xs)
    whole = r.b_whole[...].reshape(z.total, z.width)
    lmine[till[0] : till[1], :] = dot_tn(whole, r.gxi[...]).astype(BF16)
    lmine[till[1] : till[2], :] = dot(r.gproj[...], r.b_xs[...].astype(BF16)).astype(BF16)
    lmine[till[2] : till[3], :] = r.gconv[...].astype(BF16)
    if till[3] < lmine.shape[0]:
        lmine[till[3] :, :] = jnp.zeros((lmine.shape[0] - till[3], ch), BF16)
    late.begin()
    push_middle(one)
    late.second()
    r.c_own[...] = term(m)
    early.third()
    push_middle(two)
    late.third()
    early.fourth()
    push_middle(three)
    late.fourth()
    early.end()
    r.ship(r.early)
    r.z_buf[...] = r.early[at[5] : at[7], :]
    shared = exchange(line, r.z_buf, r.z_in, r.z_send, r.z_recv)
    reduce.total(r.c_own)
    r.need(r.b_act, r.b_gmid)
    act = r.b_act[...].astype(F32)
    pulled, grad_gain = norm_back(act, rms_inverse(act), r.norm_in[l : l + 1, :], r.c_own[...])
    emit(r.b_gmid[...] + pulled)

    def finish():
        late.end()
        r.ship(r.late)
        if l == 0:
            both = jnp.concatenate([grad_gain, r.prior[...]], axis=0)
            groups = z.width // LANES
            for g in range(groups):
                r.n_buf[2 * g : 2 * g + 2, :] = both[:, g * LANES : (g + 1) * LANES]
            if 2 * groups < r.n_buf.shape[0]:
                r.n_buf[2 * groups :, :] = jnp.zeros((r.n_buf.shape[0] - 2 * groups, LANES), F32)
            plane = [(lax.rem(d + k, z.peers), m) for k in range(1, z.peers)]
            r.n_buf2[...] = exchange(plane, r.n_buf, r.n_in, r.n_send, r.n_recv)()
            summed = exchange(line, r.n_buf2, r.n_in2, r.n_send2, r.n_recv2)()
            r.gnorm[...] = jnp.concatenate([summed[2 * g : 2 * g + 2, :] for g in range(groups)], axis=1)
        else:
            r.gnorm[...] = grad_gain
        r.share[...] = shared()
        finish_sum()
        reduce.finish()
        early.finish()
        late.finish()

    return finish


def last_block(z, back, prior, small, w_in):
    def body(r):
        d, m = lax.axis_index("dp"), lax.axis_index("mp")
        (win,) = fetch([(r.w_in.at[0], r.win)], r.fetched)
        greet(d, m, z.lanes, z.peers, True)

        def emit(value):
            r.up[...] = value

        in_back_stage(z, r, 0, win, emit)()

    return launch("mamba_in_backward", 9, body, dict(**back, prior=prior, **convolution(small)), dict(w_in=w_in),
                  dict(up=f32(z.rows, z.width), **in_back_outputs(z, True)), dict(fetched=dma(1), **in_back_scratch(z, w_in, True)))


def experts_back(z, r, l, fetched, finish):
    d, m = lax.axis_index("dp"), lax.axis_index("mp")
    for weight in fetched:
        weight.wait()
    r.need(r.into, r.hidden)
    moe = Experts(d, m, z.lanes, z.peers, r.into, *expert_refs(r))

    def expert(s, rows):
        grad_hidden = (dot_nt(rows[0], r.wdown[...]) * gelu_slope(r.hidden[s].astype(F32))).astype(BF16)
        r.ghid[s] = grad_hidden
        return [dot_nt(grad_hidden, r.wup[...])]

    def meanwhile():
        r.need(r.active, r.slots)
        r.gdown[...] = dot_tn(flat(r.active), r.e_slots[...].reshape(z.lanes * z.slots, z.width))
        r.gup[...] = dot_tn(flat(r.slots), flat(r.ghid))
        r.ship(r.gdown, r.gup)
        finish()

    moe.run(expert, r.e_own, meanwhile)
    r.need(r.picked, r.middle)
    route_back(z, r, l, r.upstream[...], r.middle[...], r.chance[...], r.choose[...], r.picked[...], r.e_own[0])
    moe.finish()


def down_blocks(z, l, back, kept, small, weights):
    def upper(r):
        d, m = lax.axis_index("dp"), lax.axis_index("mp")
        (win,) = fetch([(r.w_in.at[l], r.win)], r.fetched)
        greet(d, m, z.lanes, z.peers, True)

        def emit(value):
            r.up[...] = value

        in_back_stage(z, r, l, win, emit)()

    def lower(r):
        d, m = lax.axis_index("dp"), lax.axis_index("mp")
        fetched = fetch([(r.w_down.at[l - 1, 0], r.wdown), (r.w_up.at[l - 1, 0], r.wup), (r.w_out.at[l - 1], r.wout)], r.fetched)
        greet(d, m, z.lanes, z.peers, True)
        r.need(r.upstream)
        r.e_rows[m, 0] = (gate_of(r.chance[...], r.choose[...]) * r.upstream[...]).astype(BF16)
        experts_back(z, r, l - 1, fetched, lambda: None)

    w_in, w_out, w_up, w_down = weights
    slots = (z.lanes, z.slots)
    one = launch("mamba_in_backward", 20 + l, upper, dict(**back, **convolution(small)),
                 dict(w_in=w_in), dict(up=f32(z.rows, z.width), **in_back_outputs(z, False)),
                 dict(fetched=dma(1), **in_back_scratch(z, w_in, False)))
    two = launch("experts_backward", 30 + l, lower, dict(**kept, upstream=one.up, **routing(small)),
                 dict(w_out=w_out, w_up=w_up, w_down=w_down), back_outputs(z),
                 dict(fetched=dma(3), ghid=pltpu.VMEM((*slots, z.hidden), BF16), **weight_scratch(w_out, w_up, w_down),
                      **expert_names(z, 1), **back_scratch(z)))
    return types.SimpleNamespace(**vars(one), **vars(two))


def down_block(z, l, back, kept, small, weights):
    def body(r):
        d, m = lax.axis_index("dp"), lax.axis_index("mp")
        win, wdown, wup, wout = fetch([(r.w_in.at[l], r.win), (r.w_down.at[l - 1, 0], r.wdown), (r.w_up.at[l - 1, 0], r.wup),
                                       (r.w_out.at[l - 1], r.wout)], r.fetched)
        greet(d, m, z.lanes, z.peers, True)

        def emit(value):
            r.upstream[...] = value
            r.e_rows[m, 0] = (gate_of(r.chance[...], r.choose[...]) * value).astype(BF16)

        experts_back(z, r, l - 1, (wdown, wup, wout), in_back_stage(z, r, l, win, emit))

    w_in, w_out, w_up, w_down = weights
    slots = (z.lanes, z.slots)
    return launch(
        "down", 9 + l, body, dict(**back, **kept, **convolution(small), **routing(small)),
        dict(w_in=w_in, w_out=w_out, w_up=w_up, w_down=w_down), dict(**in_back_outputs(z, False), **back_outputs(z)),
        dict(fetched=dma(4), upstream=pltpu.VMEM((z.rows, z.width), F32),
             ghid=pltpu.VMEM((*slots, z.hidden), BF16), **weight_scratch(w_out, w_up, w_down), **in_back_scratch(z, w_in, False),
             **expert_names(z, 1), **back_scratch(z)))


def final_block(z, result, up, gnorm, layers):
    count, ch = len(layers), z.channels
    at, till = early_rows(z.width, z.experts), late_rows(z.width)
    far = dict(result=(z.rows, z.width), tokens=(z.rows, z.width), w_in=(count, 2, z.width, ch), w_out=(count, ch, z.width),
               w_up=(count, 1, z.width, z.hidden), w_down=(count, 1, z.hidden, z.width))
    near = dict(norm_in=(count, z.width), conv_w=(count, CONV, ch), conv_b=(count, ch), x_proj=(count, ch, PROJ), dt_proj=(count, DT_RANK, ch),
                dt_bias=(count, ch), a_log=(count, STATE, ch), skip=(count, ch), norm_moe=(count, z.width), router=(count, z.experts, z.width))
    shapes = {**far, **near}
    sums = [v for layer in layers for v in layer[:2]]
    whole = [result, up, *(v for layer in layers for v in layer[3:])]

    def kernel(*refs):
        small, refs = refs[: 1 + count], refs[1 + count :]
        there, refs = refs[: len(sums) + len(whole)], refs[len(sums) + len(whole) :]
        outs, refs = refs[: len(shapes)], refs[len(shapes) :]
        held, (w_in, w_out, came, went) = refs[: len(there)], refs[len(there) :]
        out = types.SimpleNamespace(**dict(zip(shapes, outs)))
        coming = fetch(list(zip(there, held)), came)
        places = [out.result, out.tokens] + [v.at[l, 0] for l in range(count) for v in (out.w_up, out.w_down)]
        out.norm_in[...] = small[0][...]
        going = []
        for l in range(count):
            early, late, share = held[2 * l], held[2 * l + 1], small[1 + l]
            coming[2 * l].wait()
            coming[2 * l + 1].wait()
            one = slice(l, l + 1)
            w_in[l, 0] = late[till[0] : till[1], :].astype(F32)
            w_in[l, 1] = early[at[0] : at[1], :].astype(F32)
            for i in range(z.width // ch):
                cols = slice(i * ch, (i + 1) * ch)
                w_out[l, :, cols] = early[at[1] + i * ch : at[1] + (i + 1) * ch, :].astype(F32)
                rows = share[i * (z.experts + 8) : (i + 1) * (z.experts + 8), :]
                out.router[l, :, cols] = rows[: z.experts]
                out.norm_moe[one, cols] = rows[z.experts : z.experts + 1]
            for src, dst in ((w_in, out.w_in), (w_out, out.w_out)):
                going.append(pltpu.make_async_copy(src.at[l], dst.at[l], went.at[len(going)]))
                going[-1].start()
            conv = late[till[2] : till[3], :].astype(F32)
            out.conv_w[l] = conv[:CONV]
            out.conv_b[one, :] = conv[CONV : CONV + 1]
            out.x_proj[l] = late[till[1] : till[2], :].astype(F32).T
            out.dt_proj[l] = early[at[2] : at[3], :].astype(F32)
            out.a_log[l] = early[at[3] : at[4], :].astype(F32)
            both = early[at[4] : at[5], :].astype(F32)
            out.dt_bias[one, :] = both[:1]
            out.skip[one, :] = both[1:2]
        for i, place in enumerate(places):
            coming[len(sums) + i].wait()
            going.append(pltpu.make_async_copy(held[len(sums) + i], place, went.at[len(going)]))
            going[-1].start()
        for copy in going:
            copy.wait()

    outputs = pl.pallas_call(
        kernel,
        out_shape=[f32(*shape) for shape in shapes.values()],
        in_specs=vmem(1 + count) + hbm(len(sums) + len(whole)),
        out_specs=hbm(len(far)) + vmem(len(near)),
        scratch_shapes=[pltpu.VMEM(v.shape, v.dtype) for v in (*sums, *whole)]
        + [pltpu.VMEM(far["w_in"], F32), pltpu.VMEM(far["w_out"], F32), dma(len(sums) + len(whole)), dma(2 * count + len(whole))],
        compiler_params=pltpu.CompilerParams(vmem_limit_bytes=60 << 20),
        name="outputs",
    )(gnorm, *(layer[2] for layer in layers), *sums, *whole)
    o = types.SimpleNamespace(**dict(zip(shapes, outputs)))
    return (o.result, o.tokens, o.norm_in, o.w_in, o.conv_w, o.conv_b, o.x_proj, o.dt_proj, o.dt_bias, o.a_log, o.skip, o.w_out, o.norm_moe,
            jnp.swapaxes(o.router, 1, 2), o.w_up, o.w_down)


def on_device(
    tokens, cotangent, lengths, routes, slot_place, norm_in, w_in, conv_w, conv_b, x_proj, dt_proj, dt_bias,
    a_log, d_skip, w_out, norm_moe, router, w_up, w_down,
):
    layers = norm_in.shape[0]
    assert layers == 2
    rows_here, width = tokens.shape
    lanes, peers = lax.axis_size("mp"), lax.axis_size("dp")
    experts, channels = router.shape[2], w_in.shape[3]
    capacity = max(2, (5 * rows_here + 4 * experts - 1) // (4 * experts))
    padded = (capacity + 15) // 16 * 16
    z = Sizes(lanes, peers, experts, padded, rows_here, width, channels, w_up.shape[3])
    position = lax.broadcasted_iota(jnp.int32, (z.total + HEAD, 1), 0)
    since, first = position, 0
    for i in range(lengths.shape[1] - 1):
        first = first + lengths[0, i]
        since = jnp.where(position >= first, position - first, since)
    since = jnp.where(position < z.total, since, 0)
    place = jnp.pad(routes * padded + slot_place, (0, -rows_here % LANES))
    small = types.SimpleNamespace(
        norm_in=norm_in, norm_moe=norm_moe, conv_w=conv_w, conv_b=conv_b, since=since, x_proj=jnp.swapaxes(x_proj, 1, 2),
        router=jnp.swapaxes(router, 1, 2),
        place=jnp.broadcast_to(place[None, :], (8, place.shape[0])),
    )
    weights = (w_in, w_out, w_up, w_down)
    scan_weights = (dt_proj, dt_bias, a_log, d_skip, spread_matrix())

    act, entry = tokens, first_block(z, 0, tokens, small, w_in)
    kept = []
    for l in range(layers):
        gated, ys, marks = scan_fwd(l, entry.xs, entry.zgate, entry.proj, since, *scan_weights)
        gated = gated.reshape(lanes, rows_here, channels)
        if l + 1 < layers:
            out = middle_block(z, l, act, gated, small, weights)
            kept.append((act, entry, gated, ys, marks, out))
            act, entry = out.following, out
        else:
            turn = turn_block(z, l, act, gated, cotangent, small, weights)
            kept.append((act, entry, gated, ys, marks, turn))
    result, above = turn.following, turn
    collected = []
    for l in reversed(range(layers)):
        act, entry, gated, ys, marks, _ = kept[l]
        gxs, gzg, gpart, gdtw, gdtb, galog, gskip = scan_bwd(
            l, entry.xs, entry.zgate, entry.proj, since, ys, above.ggated.reshape(z.total, channels), marks, *scan_weights)
        back = dict(gpart=gpart, gxs=gxs, gzg=gzg, b_conv=entry.conv, b_xs=entry.xs, b_whole=entry.whole, b_act=act, b_gmid=above.gmid,
                    b_gwout=above.gwout, b_gshare=above.gshare, gdtw=gdtw, gdtb=gdtb, galog=galog, gskip=gskip)
        grads = (above.gup, above.gdown)
        if l > 0:
            _, _, below_gated, _, _, below = kept[l - 1]
            forward = dict(gated=below_gated, chance=below.chance, choose=below.choose, into=below.into, slots=below.slots, hidden=below.hidden,
                           active=below.active, picked=below.picked, middle=below.middle)
            above = (down_block if z.slots <= 256 else down_blocks)(z, l, back, forward, small, weights)
            prior = above.gnorm
            collected.append((above.early, above.late, above.share, *grads))
        else:
            end = last_block(z, back, prior, small, w_in)
            collected.append((end.early, end.late, end.share, *grads))
    collected = collected[::-1]
    at, till = early_rows(width, experts), late_rows(width)

    return final_block(z, result, end.up, end.gnorm, collected)


def solution(mesh):
    return jax.shard_map(
        on_device,
        mesh=mesh,
        in_specs=(
            P(("dp", "mp"), None),
            P(("dp", "mp"), None),
            P("dp", None),
            P(("dp", "mp")),
            P(("dp", "mp")),
            P(),
            P(None, None, None, "mp"),
            P(None, None, "mp"),
            P(None, "mp"),
            P(None, "mp", None),
            P(None, None, "mp"),
            P(None, "mp"),
            P(None, None, "mp"),
            P(None, "mp"),
            P(None, "mp", None),
            P(),
            P(),
            P(None, "dp", None, "mp"),
            P(None, "dp", "mp", None),
        ),
        out_specs=(
            P(("dp", "mp"), None),
            P(("dp", "mp"), None),
            P(),
            P(None, None, None, "mp"),
            P(None, None, "mp"),
            P(None, "mp"),
            P(None, "mp", None),
            P(None, None, "mp"),
            P(None, "mp"),
            P(None, None, "mp"),
            P(None, "mp"),
            P(None, "mp", None),
            P(),
            P(),
            P(None, "dp", None, "mp"),
            P(None, "dp", "mp", None),
        ),
        check_vma=False,
    )
```

time: 721 us -> 635 us (0.88)
  Pallas kernels: 665 us -> 620 us
  local copies, waits for them, and re-layouts: 29.2 us -> 3.8 us
  other arithmetic: 17.2 us -> 2.89 us
    pallas_call x8 -> x6, Pallas kernels: 585 us -> 535 us  [the longest x5 522 us: launch(): pl.pallas_call(kernel, out_shape=[*prompt.values(), *late.values()], in_s...]
    unnamed x110 -> x1, local copies, waits for them, and re-layouts: 25.3 us -> 1.84 us
    another operation x11 -> x0, other arithmetic: 12.4 us -> none  [the longest x9 7.24 us: stacked(): return jnp.stack([make(*entry).astype(F32) for entry in collected])]
where the time goes in v3:
time: 635 us; the launch traced here: 630 us
  Pallas kernels  620 us (98%)
    pallas_call x5, Pallas kernels, launch(): pl.pallas_call(kernel, out_shape=[*prompt.values(), *late.values()], in_s...  522 us
    pallas_call x2, Pallas kernels, scan_bwd(): pl.pallas_call(functools.partial(scan_bwd_kernel, l), grid=(steps,), out_...  56.5 us
    pallas_call x2, Pallas kernels, scan_fwd(): pl.pallas_call(functools.partial(scan_fwd_kernel, l), grid=(steps,), out_...  29 us
    pallas_call x1, Pallas kernels, final_block(): pl.pallas_call(kernel, out_shape=[f32(*shape) for shape in shapes.values(...  13.1 us

profile of v3, /device:TPU:0, one launch (start us, length us, event | category | flops | bytes accessed | tf_op | source)
XLA Modules:
  0.0 630.0 jit_solution(17843502075347310375)
XLA Ops:
  0.6 0.7 multiply_add_fusion
  1.4 1.4 fusion.4
  4.7 0.6 broadcast_in_dim.10.refs_0_
  5.3 0.7 fusion.spread_ref
  5.9 1.5 select_select_fusion.refs_3_.since_ref.refs_6_.refs_10_.refs_9_
  7.5 40.3 %mamba_in.1 = (bf16[80,768]{1,0:T(8,128)(2,1)}, bf16[4,192,768]{2,1,0:T(8,128)(2,1)}, f32[776,384]{1,0:T(8,128)}, f32[768,384]{1,0:T(8,128)}, f32[768,384]{1,0:T(8,128)}) custom-call(f32[2,768]{1,0:T(2,128)} %refs_6_.5, f32[2,4,384]{2,1,0:T(4,128)} %refs_7_.5, f32[2,384]{1,0:T(2,128)} %refs_8_.7, ...), custom_call_target="tpu_custom_call" | custom-call | tf_op jit(solution)/shard_map/mamba_in/pallas_call | solution.py:730
  47.7 14.5 %scan_fwd.2 = (bf16[768,384]{1,0:T(8,128)(2,1)}, f32[768,384]{1,0:T(8,128)}, f32[6,16,384]{2,1,0:T(8,128)}) custom-call(f32[768,384]{1,0:T(8,128)} %get-tuple-element.93.xs_ref.refs_15_, f32[768,384]{1,0:T(8,128)} %get-tuple-element.94.zg_ref, bf16[80,768]{1,0:T(8,128)(2,1)} %get-tuple-element.95.proj_ref, ...), custom_call_target="tpu_custom_call" | custom-call | tf_op jit(solution)/shard_map/scan_fwd/pallas_call | solution.py:115
  62.3 125.0 %middle.1 = (f32[192,8]{1,0:T(8,128)}, f32[192,8]{1,0:T(8,128)}, bf16[80,768]{1,0:T(8,128)(2,1)}, f32[192,768]{1,0:T(8,128)}, bf16[4,256,192]{2,1,0:T(8,128)(2,1...) custom-call(s32[8,256]{1,0:T(8,128)} %broadcast_in_dim.10.refs_0_, ...), custom_call_target="tpu_custom_call" | custom-call | tf_op jit(solution)/shard_map/middle/pallas_call | solution.py:730
  187.3 14.5 %scan_fwd.3 = (bf16[768,384]{1,0:T(8,128)(2,1)}, f32[768,384]{1,0:T(8,128)}, f32[6,16,384]{2,1,0:T(8,128)}) custom-call(f32[768,384]{1,0:T(8,128)} %get-tuple-element.98.xs_ref.refs_18_, f32[768,384]{1,0:T(8,128)} %get-tuple-element.99.zg_ref, bf16[80,768]{1,0:T(8,128)(2,1)} %get-tuple-element.100.proj_ref, ...), custom_call_target="tpu_custom_call" | custom-call | tf_op jit(solution)/shard_map/scan_fwd/pallas_call | solution.py:115
  201.8 167.6 %turn.1 = (f32[16,768]{1,0:T(8,128)}, f32[192,768]{1,0:T(8,128)}, f32[192,768]{1,0:T(8,128)}, f32[768,768]{1,0:T(8,128)}, f32[768,768]{1,0:T(8,128)}, /*index=5*/f32[4,192,384]{2,1,0:T(8,128)}, bf16[384,768]{1,0:T(8,128)(2,1)}) custom-call(s32[8,256]{1,0:T(8,128)} %broadcast_in_dim.10.refs_0_, f32[2,768]{1,0:T(2,128)} %refs_12_.3, f32[2,8,768]{2,1,0:T(8,128)} %bitcast.20, ...), custom_call_target="tpu_custom_call" | custom-call | tf_op jit(solution)/shard_map/turn/pallas_call | solution.py:730
  369.4 28.1 %scan_bwd.2 = (f32[768,384]{1,0:T(8,128)}, bf16[768,384]{1,0:T(8,128)(2,1)}, f32[80,768]{1,0:T(8,128)}, f32[48,384]{1,0:T(8,128)}, f32[1,384]{1,0:T(1,128)}, /*index=5*/f32[16,384]{1,0:T(8,128)}, f32[1,384]{1,0:T(1,128)}) custom-call(f32[768,384]{1,0:T(8,128)} %get-tuple-element.98.xs_ref.refs_18_, f32[768,384]{1,0:T(8,128)} %get-tuple-element.99.zg_ref, ...), custom_call_target="tpu_custom_call" | custom-call | tf_op jit(solution)/shard_map/scan_bwd/pallas_call | solution.py:261
  397.5 133.5 %down.1 = (f32[32,384]{1,0:T(8,128)}, f32[1,768]{1,0:T(1,128)}, f32[16,768]{1,0:T(8,128)}, bf16[1664,384]{1,0:T(8,128)(2,1)}, bf16[896,384]{1,0:T(8,128)(2,1)}, ...) custom-call(f32[16,768]{1,0:T(8,128)} %get-tuple-element.102.refs_0_, ...), custom_call_target="tpu_custom_call" | custom-call | tf_op jit(solution)/shard_map/down/pallas_call | solution.py:730
  531.0 28.4 %scan_bwd.3 = (f32[768,384]{1,0:T(8,128)}, bf16[768,384]{1,0:T(8,128)(2,1)}, f32[80,768]{1,0:T(8,128)}, f32[48,384]{1,0:T(8,128)}, f32[1,384]{1,0:T(1,128)}, /*index=5*/f32[16,384]{1,0:T(8,128)}, f32[1,384]{1,0:T(1,128)}) custom-call(f32[768,384]{1,0:T(8,128)} %get-tuple-element.93.xs_ref.refs_15_, f32[768,384]{1,0:T(8,128)} %get-tuple-element.94.zg_ref, ...), custom_call_target="tpu_custom_call" | custom-call | tf_op jit(solution)/shard_map/scan_bwd/pallas_call | solution.py:261
  559.4 55.1 %mamba_in_backward.1 = (f32[32,384]{1,0:T(8,128)}, f32[2,768]{1,0:T(2,128)}, f32[192,768]{1,0:T(8,128)}, bf16[1664,384]{1,0:T(8,128)(2,1)}, bf16[896,384]{1,0:T(8,128)(2,1)}) custom-call(f32[16,768]{1,0:T(8,128)} %get-tuple-element.125.refs_0_, f32[48,384]{1,0:T(8,128)} %get-tuple-element.129.refs_1_, f32[1,384]{1,0:T(1,128)} %get-tuple-element.130.refs_2_, ...), custom_call_target="tpu_custom_call" | custom-call | tf_op jit(solution)/shard_map/mamba_in_backward/pallas_call | solution.py:730
  614.6 13.1 %outputs.1 = (f32[192,768]{1,0:T(8,128)}, f32[192,768]{1,0:T(8,128)}, f32[2,2,768,384]{3,2,1,0:T(8,128)}, f32[2,384,768]{2,1,0:T(8,128)}, f32[2,1,768,768]{3,2,1...) custom-call(f32[2,768]{1,0:T(2,128)} %get-tuple-element.141.refs_0_,, ...), custom_call_target="tpu_custom_call" | custom-call | tf_op jit(solution)/shard_map/outputs/pallas_call | solution.py:1460
  627.7 1.8 copy.35
  (3 shorter events, 0.0 us)

commit v4 on v3

--- a/solution.py
+++ b/solution.py
@@ -479,7 +479,7 @@
     ]
 
 
-PARTS = 2
+PARTS = 3
 
 
 def line_sum(part, stage, inbox, send, recv, out, d, m, lanes, between=lambda: None):
@@ -650,32 +650,46 @@
             self.stage[s, i] = value.astype(BF16)
         self.home(s).start()
 
-    def run(self, expert, own_ref, meanwhile):
+    def steps(self, expert, own_ref):
         one, two, three = self.gather.order
-        self.gather.start()
         self.dispatch(self.m)
+        yield
         self.gather.arrive(0)
         self.dispatch(one)
+        yield
         self.gather.arrive(1)
         self.dispatch(two)
         self.answer(one, expert)
+        yield
         self.gather.arrive(2)
         self.dispatch(three)
         self.answer(two, expert)
         self.combine_away(one)
+        yield
         self.answer(three, expert)
         self.combine_away(two)
+        yield
         self.answer(self.m, expert)
         self.combine_away(three)
+        yield
         for i, value in enumerate(self.combine(self.m)):
             own_ref[i] = value
-        meanwhile()
-        for s in (one, two, three):
+        yield
+
+    def settle(self, own_ref):
+        for s in self.gather.order:
             pltpu.make_async_remote_copy(
                 src_ref=self.stage.at[s], dst_ref=self.inbox.at[s], send_sem=self.rsend.at[s], recv_sem=self.rrecv.at[s],
                 device_id=(self.d, s), device_id_type=MESH,
             ).wait_recv()
             own_ref[...] += self.inbox[s].astype(F32)
+
+    def run(self, expert, own_ref, meanwhile):
+        self.gather.start()
+        for _ in self.steps(expert, own_ref):
+            pass
+        meanwhile()
+        self.settle(own_ref)
 
     def finish(self):
         self.gather.finish()
@@ -983,36 +997,41 @@
         wdown.wait()
         middle = r.m_own[...]
         normed = middle * rms_inverse(middle) * r.norm_moe[l : l + 1, :]
+        forth = Experts(d, m, z.lanes, z.peers, r.into, *expert_refs(r))
+        back = Experts(d, m, z.lanes, z.peers, r.into, *(getattr(r, "f" + k[1:]) for k in list(expert_names(z, 1))[:-1]))
         r.e_rows[m, 0] = normed.astype(BF16)
+        forth.gather.start()
         chance = chances(z, normed, r.router[l])
         r.chance[...] = chance
         r.need(r.cotangent)
-        r.e_rows[m, 1] = (gate_of(chance, r.choose[...]) * r.cotangent[...].astype(F32)).astype(BF16)
-        moe = Experts(d, m, z.lanes, z.peers, r.into, *expert_refs(r))
-
-        def expert(s, rows):
-            hidden = dot(rows[0], r.wup[...])
-            active = gelu(hidden).astype(BF16)
+        r.f_rows[m, 0] = (gate_of(chance, r.choose[...]) * r.cotangent[...].astype(F32)).astype(BF16)
+        back.gather.start()
+
+        def expert_forth(s, rows):
+            active = gelu(dot(rows[0], r.wup[...])).astype(BF16)
             r.active[s] = active
-            grad_hidden = (dot_nt(rows[1], r.wdown[...]) * gelu_slope(hidden)).astype(BF16)
+            return [dot(active, r.wdown[...])]
+
+        def expert_back(s, rows):
+            slope = gelu_slope(dot(forth.slot_rows(forth.slots, s, 0), r.wup[...]))
+            grad_hidden = (dot_nt(rows[0], r.wdown[...]) * slope).astype(BF16)
             r.ghid[s] = grad_hidden
-            return [dot(active, r.wdown[...]), dot_nt(grad_hidden, r.wup[...])]
-
-        def meanwhile():
-            finish()
-            for s in range(z.lanes):
-                down = dot_tn(r.active[s], moe.slot_rows(moe.slots, s, 1))
-                r.gdown[...] = down if s == 0 else r.gdown[...] + down
-                up = dot_tn(moe.slot_rows(moe.slots, s, 0), r.ghid[s])
-                r.gup[...] = up if s == 0 else r.gup[...] + up
-            r.ship(r.gdown, r.gup)
-
-        moe.run(expert, r.e_own, meanwhile)
+            return [dot_nt(grad_hidden, r.wup[...])]
+
+        for _ in zip(forth.steps(expert_forth, r.e_own), back.steps(expert_back, r.f_own)):
+            pass
+        finish()
+        r.gdown[...] = dot_tn(flat(r.active), r.f_slots[...].reshape(z.lanes * z.slots, z.width))
+        r.gup[...] = dot_tn(r.e_slots[...].reshape(z.lanes * z.slots, z.width), flat(r.ghid))
+        r.ship(r.gdown, r.gup)
+        forth.settle(r.e_own)
+        back.settle(r.f_own)
         picked = r.e_own[0].astype(BF16)
         r.following[...] = r.m_own[...] + gate_of(r.chance[...], r.choose[...]) * picked.astype(F32)
         r.ship(r.following)
-        route_back(z, r, l, r.cotangent[...].astype(F32), r.m_own[...], r.chance[...], r.choose[...], picked, r.e_own[1])
-        moe.finish()
+        route_back(z, r, l, r.cotangent[...].astype(F32), r.m_own[...], r.chance[...], r.choose[...], picked, r.f_own[0])
+        forth.finish()
+        back.finish()
 
     w_in, w_out, w_up, w_down = weights
     slots = (z.lanes, z.slots)
@@ -1022,7 +1041,8 @@
         dict(following=f32(z.rows, z.width), **back_outputs(z)),
         dict(fetched=dma(3), choose=pltpu.VMEM((z.rows, z.experts), F32), chance=pltpu.VMEM((z.rows, z.experts), F32), into=pltpu.VMEM((*slots, z.rows), BF16),
              active=pltpu.VMEM((*slots, z.hidden), BF16), ghid=pltpu.VMEM((*slots, z.hidden), BF16),
-             **weight_scratch(w_out, w_up, w_down), **out_scratch(z, small.place), **expert_names(z, 2), **back_scratch(z)),
+             **weight_scratch(w_out, w_up, w_down), **out_scratch(z, small.place), **expert_names(z, 1),
+             **{"f" + k[1:]: v for k, v in expert_names(z, 1).items()}, **back_scratch(z)),
         58 if z.slots <= 256 else 61)
 
 
@@ -1409,7 +1429,7 @@
     at, till = early_rows(z.width, z.experts), late_rows(z.width)
     far = dict(result=(z.rows, z.width), tokens=(z.rows, z.width), w_in=(count, 2, z.width, ch), w_out=(count, ch, z.width),
                w_up=(count, 1, z.width, z.hidden), w_down=(count, 1, z.hidden, z.width))
-    near = dict(norm_in=(count, z.width), conv_w=(count, CONV, ch), conv_b=(count, ch), x_proj=(count, ch, PROJ), dt_proj=(count, DT_RANK, ch),
+    near = dict(norm_in=(count, z.width), conv_w=(count, CONV, ch), conv_b=(count, ch), x_proj=(count, PROJ, ch), dt_proj=(count, DT_RANK, ch),
                 dt_bias=(count, ch), a_log=(count, STATE, ch), skip=(count, ch), norm_moe=(count, z.width), router=(count, z.experts, z.width))
     shapes = {**far, **near}
     sums = [v for layer in layers for v in layer[:2]]
@@ -1444,7 +1464,7 @@
             conv = late[till[2] : till[3], :].astype(F32)
             out.conv_w[l] = conv[:CONV]
             out.conv_b[one, :] = conv[CONV : CONV + 1]
-            out.x_proj[l] = late[till[1] : till[2], :].astype(F32).T
+            out.x_proj[l] = late[till[1] : till[2], :].astype(F32)
             out.dt_proj[l] = early[at[2] : at[3], :].astype(F32)
             out.a_log[l] = early[at[3] : at[4], :].astype(F32)
             both = early[at[4] : at[5], :].astype(F32)
@@ -1468,7 +1488,7 @@
         name="outputs",
     )(gnorm, *(layer[2] for layer in layers), *sums, *whole)
     o = types.SimpleNamespace(**dict(zip(shapes, outputs)))
-    return (o.result, o.tokens, o.norm_in, o.w_in, o.conv_w, o.conv_b, o.x_proj, o.dt_proj, o.dt_bias, o.a_log, o.skip, o.w_out, o.norm_moe,
+    return (o.result, o.tokens, o.norm_in, o.w_in, o.conv_w, o.conv_b, jnp.swapaxes(o.x_proj, 1, 2), o.dt_proj, o.dt_bias, o.a_log, o.skip, o.w_out, o.norm_moe,
             jnp.swapaxes(o.router, 1, 2), o.w_up, o.w_down)
 
 

time: 635 us -> 624 us (0.983)
  Pallas kernels: 620 us -> 611 us
    pallas_call x5, Pallas kernels: 522 us -> 512 us  [launch(): pl.pallas_call(kernel, out_shape=[*prompt.values(), *late.values()], in_s...]
where the time goes in v4:
time: 624 us; the launch traced here: 619 us
  Pallas kernels  611 us (98%)
    pallas_call x5, Pallas kernels, launch(): pl.pallas_call(kernel, out_shape=[*prompt.values(), *late.values()], in_s...  512 us
    pallas_call x2, Pallas kernels, scan_bwd(): pl.pallas_call(functools.partial(scan_bwd_kernel, l), grid=(steps,), out_...  56.5 us
    pallas_call x2, Pallas kernels, scan_fwd(): pl.pallas_call(functools.partial(scan_fwd_kernel, l), grid=(steps,), out_...  29 us
    pallas_call x1, Pallas kernels, final_block(): pl.pallas_call(kernel, out_shape=[f32(*shape) for shape in shapes.values(...  13.1 us

profile of v4, /device:TPU:0, one launch (start us, length us, event | category | flops | bytes accessed | tf_op | source)
XLA Modules:
  0.0 619.0 jit_solution(6878089917815350303)
XLA Ops:
  0.6 0.7 multiply_add_fusion
  1.4 1.4 fusion.4
  4.7 0.6 broadcast_in_dim.10.refs_0_
  5.3 0.7 fusion.spread_ref
  5.9 1.5 select_select_fusion.refs_3_.since_ref.refs_6_.refs_10_.refs_9_
  7.5 39.9 %mamba_in.1 = (bf16[80,768]{1,0:T(8,128)(2,1)}, bf16[4,192,768]{2,1,0:T(8,128)(2,1)}, f32[776,384]{1,0:T(8,128)}, f32[768,384]{1,0:T(8,128)}, f32[768,384]{1,0:T(8,128)}) custom-call(f32[2,768]{1,0:T(2,128)} %refs_6_.5, f32[2,4,384]{2,1,0:T(4,128)} %refs_7_.5, f32[2,384]{1,0:T(2,128)} %refs_8_.7, ...), custom_call_target="tpu_custom_call" | custom-call | tf_op jit(solution)/shard_map/mamba_in/pallas_call | solution.py:744
  47.3 14.5 %scan_fwd.2 = (bf16[768,384]{1,0:T(8,128)(2,1)}, f32[768,384]{1,0:T(8,128)}, f32[6,16,384]{2,1,0:T(8,128)}) custom-call(f32[768,384]{1,0:T(8,128)} %get-tuple-element.93.xs_ref.refs_15_, f32[768,384]{1,0:T(8,128)} %get-tuple-element.94.zg_ref, bf16[80,768]{1,0:T(8,128)(2,1)} %get-tuple-element.95.proj_ref, ...), custom_call_target="tpu_custom_call" | custom-call | tf_op jit(solution)/shard_map/scan_fwd/pallas_call | solution.py:115
  61.8 124.8 %middle.1 = (f32[192,8]{1,0:T(8,128)}, f32[192,8]{1,0:T(8,128)}, bf16[80,768]{1,0:T(8,128)(2,1)}, f32[192,768]{1,0:T(8,128)}, bf16[4,256,192]{2,1,0:T(8,128)(2,1...) custom-call(s32[8,256]{1,0:T(8,128)} %broadcast_in_dim.10.refs_0_, ...), custom_call_target="tpu_custom_call" | custom-call | tf_op jit(solution)/shard_map/middle/pallas_call | solution.py:744
  186.6 14.5 %scan_fwd.3 = (bf16[768,384]{1,0:T(8,128)(2,1)}, f32[768,384]{1,0:T(8,128)}, f32[6,16,384]{2,1,0:T(8,128)}) custom-call(f32[768,384]{1,0:T(8,128)} %get-tuple-element.98.xs_ref.refs_18_, f32[768,384]{1,0:T(8,128)} %get-tuple-element.99.zg_ref, bf16[80,768]{1,0:T(8,128)(2,1)} %get-tuple-element.100.proj_ref, ...), custom_call_target="tpu_custom_call" | custom-call | tf_op jit(solution)/shard_map/scan_fwd/pallas_call | solution.py:115
  201.2 160.6 %turn.1 = (f32[16,768]{1,0:T(8,128)}, f32[192,768]{1,0:T(8,128)}, f32[192,768]{1,0:T(8,128)}, f32[768,768]{1,0:T(8,128)}, f32[768,768]{1,0:T(8,128)}, /*index=5*/f32[4,192,384]{2,1,0:T(8,128)}, bf16[384,768]{1,0:T(8,128)(2,1)}) custom-call(s32[8,256]{1,0:T(8,128)} %broadcast_in_dim.10.refs_0_, f32[2,768]{1,0:T(2,128)} %refs_12_.3, f32[2,8,768]{2,1,0:T(8,128)} %bitcast.21, ...), custom_call_target="tpu_custom_call" | custom-call | tf_op jit(solution)/shard_map/turn/pallas_call | solution.py:744
  361.8 28.1 %scan_bwd.2 = (f32[768,384]{1,0:T(8,128)}, bf16[768,384]{1,0:T(8,128)(2,1)}, f32[80,768]{1,0:T(8,128)}, f32[48,384]{1,0:T(8,128)}, f32[1,384]{1,0:T(1,128)}, /*index=5*/f32[16,384]{1,0:T(8,128)}, f32[1,384]{1,0:T(1,128)}) custom-call(f32[768,384]{1,0:T(8,128)} %get-tuple-element.98.xs_ref.refs_18_, f32[768,384]{1,0:T(8,128)} %get-tuple-element.99.zg_ref, ...), custom_call_target="tpu_custom_call" | custom-call | tf_op jit(solution)/shard_map/scan_bwd/pallas_call | solution.py:261
  389.9 131.1 %down.1 = (f32[32,384]{1,0:T(8,128)}, f32[1,768]{1,0:T(1,128)}, f32[16,768]{1,0:T(8,128)}, bf16[1664,384]{1,0:T(8,128)(2,1)}, bf16[896,384]{1,0:T(8,128)(2,1)}, ...) custom-call(f32[16,768]{1,0:T(8,128)} %get-tuple-element.102.refs_0_, ...), custom_call_target="tpu_custom_call" | custom-call | tf_op jit(solution)/shard_map/down/pallas_call | solution.py:744
  521.0 28.4 %scan_bwd.3 = (f32[768,384]{1,0:T(8,128)}, bf16[768,384]{1,0:T(8,128)(2,1)}, f32[80,768]{1,0:T(8,128)}, f32[48,384]{1,0:T(8,128)}, f32[1,384]{1,0:T(1,128)}, /*index=5*/f32[16,384]{1,0:T(8,128)}, f32[1,384]{1,0:T(1,128)}) custom-call(f32[768,384]{1,0:T(8,128)} %get-tuple-element.93.xs_ref.refs_15_, f32[768,384]{1,0:T(8,128)} %get-tuple-element.94.zg_ref, ...), custom_call_target="tpu_custom_call" | custom-call | tf_op jit(solution)/shard_map/scan_bwd/pallas_call | solution.py:261
  549.4 56.1 %mamba_in_backward.1 = (f32[32,384]{1,0:T(8,128)}, f32[2,768]{1,0:T(2,128)}, f32[192,768]{1,0:T(8,128)}, bf16[1664,384]{1,0:T(8,128)(2,1)}, bf16[896,384]{1,0:T(8,128)(2,1)}) custom-call(f32[16,768]{1,0:T(8,128)} %get-tuple-element.125.refs_0_, f32[48,384]{1,0:T(8,128)} %get-tuple-element.129.refs_1_, f32[1,384]{1,0:T(1,128)} %get-tuple-element.130.refs_2_, ...), custom_call_target="tpu_custom_call" | custom-call | tf_op jit(solution)/shard_map/mamba_in_backward/pallas_call | solution.py:744
  605.5 13.1 %outputs.1 = (f32[192,768]{1,0:T(8,128)}, f32[192,768]{1,0:T(8,128)}, f32[2,2,768,384]{3,2,1,0:T(8,128)}, f32[2,384,768]{2,1,0:T(8,128)}, f32[2,1,768,768]{3,2,1...) custom-call(f32[2,768]{1,0:T(2,128)} %get-tuple-element.141.refs_0_,, ...), custom_call_target="tpu_custom_call" | custom-call | tf_op jit(solution)/shard_map/outputs/pallas_call | solution.py:1480
  (3 shorter events, 0.0 us)

commit v5 on v4

--- a/solution.py
+++ b/solution.py
@@ -78,8 +78,8 @@
 
     def step(g, hs):
         hs = list(hs)
-        t0 = pl.multiple_of(g * 8, 8)
-        for i in range(8):
+        t0 = pl.multiple_of(g * 32, 32)
+        for i in range(32):
             t = t0 + i
             r0 = pl.multiple_of(t * STATE, STATE)
             b = bx_ref[pl.ds(r0, STATE), :]
@@ -93,7 +93,7 @@
                 yq_ref[j, pl.ds(q0, 8), :] = q[:8] + q[8:]
         return tuple(hs)
 
-    hs = lax.fori_loop(0, CHUNK // 8, step, tuple(h_ref[:, j * LANES : (j + 1) * LANES] for j in range(groups)))
+    hs = lax.fori_loop(0, CHUNK // 32, step, tuple(h_ref[:, j * LANES : (j + 1) * LANES] for j in range(groups)))
     for j in range(groups):
         h_ref[:, j * LANES : (j + 1) * LANES] = hs[j]
     zg = zg_ref[...]
@@ -174,8 +174,8 @@
 
     def again(g, hs):
         hs = list(hs)
-        t0 = pl.multiple_of(g * 8, 8)
-        for i in range(8):
+        t0 = pl.multiple_of(g * 32, 32)
+        for i in range(32):
             t = t0 + i
             r0 = pl.multiple_of(t * STATE, STATE)
             r1 = pl.multiple_of(t * STATE + STATE, STATE)
@@ -187,13 +187,13 @@
                 h_ref[j, pl.ds(r1, STATE), :] = hs[j]
         return tuple(hs)
 
-    last = lax.fori_loop(0, CHUNK // 8, again, tuple(hck_ref[0][:, c] for c in cols))
+    last = lax.fori_loop(0, CHUNK // 32, again, tuple(hck_ref[0][:, c] for c in cols))
 
     def back(g, carry):
         carry = [list(c) for c in carry]
         aa, hs, acc = carry
-        t0 = pl.multiple_of(CHUNK - 8 - g * 8, 8)
-        for i in reversed(range(8)):
+        t0 = pl.multiple_of(CHUNK - 32 - g * 32, 32)
+        for i in reversed(range(32)):
             t = t0 + i
             r0 = pl.multiple_of(t * STATE, STATE)
             q0 = pl.multiple_of(t * 8, 8)
@@ -222,7 +222,7 @@
         return tuple(tuple(c) for c in carry)
 
     aa, _, acc = lax.fori_loop(
-        0, CHUNK // 8, back,
+        0, CHUNK // 32, back,
         (tuple(a_ref[:, c] for c in cols), last, tuple(jnp.zeros((STATE, LANES), F32) for _ in cols)))
     for j in range(groups):
         a_ref[:, cols[j]] = aa[j]
@@ -251,15 +251,26 @@
     gproj_ref[DT_RANK + STATE :, :] = dot_nt(spread_ref[...], wide_c)
 
 
-def scan_bwd(l, xs, zg, proj, since, ys, gg, hck, dtw, dtb, alog, skip, spread):
+def scan_bwd(l, xs, zg, proj, since, ys, gg, hck, dtw, dtb, alog, skip, spread, beside=None):
+    work, far, made, room = beside or (None, [], [], [])
     rows, ch = xs.shape
     steps = rows // CHUNK
     row = lambda w: pl.BlockSpec((CHUNK, w), lambda i: (steps - 1 - i, 0))
     full = lambda s: pl.BlockSpec(s, lambda i: (0,) * len(s))
     big = lambda: pltpu.VMEM((CHUNK * STATE, LANES), F32)
     g = ch // LANES
+
+    def kernel(*refs):
+        cuts = [12, len(far), 7, len(made), 13, len(room)]
+        at = [sum(cuts[:i]) for i in range(7)]
+        ins, xin, outs, xout, held, xheld = (refs[at[i] : at[i + 1]] for i in range(6))
+        if work is not None:
+            work(steps, xin, xout, xheld)
+        scan_bwd_kernel(l, *ins, *outs, *held)
+
+    anywhere = pl.BlockSpec(memory_space=pl.ANY)
     return pl.pallas_call(
-        functools.partial(scan_bwd_kernel, l),
+        kernel,
         grid=(steps,),
         out_shape=[
             jax.ShapeDtypeStruct((rows, ch), F32),
@@ -269,11 +280,14 @@
             jax.ShapeDtypeStruct((1, ch), F32),
             jax.ShapeDtypeStruct((STATE, ch), F32),
             jax.ShapeDtypeStruct((1, ch), F32),
+            *made,
         ],
         in_specs=[row(ch), row(ch), pl.BlockSpec((PROJ, CHUNK), lambda i: (0, steps - 1 - i)), row(1), row(ch), row(ch),
                   pl.BlockSpec((1, STATE, ch), lambda i: (steps - 1 - i, 0, 0))]
-        + [full(v.shape) for v in (dtw, dtb, alog, skip, spread)],
-        out_specs=[row(ch), row(ch), pl.BlockSpec((PROJ, CHUNK), lambda i: (0, steps - 1 - i)), full((DT_RANK, ch)), full((1, ch)), full((STATE, ch)), full((1, ch))],
+        + [full(v.shape) for v in (dtw, dtb, alog, skip, spread)]
+        + [anywhere] * len(far),
+        out_specs=[row(ch), row(ch), pl.BlockSpec((PROJ, CHUNK), lambda i: (0, steps - 1 - i)), full((DT_RANK, ch)), full((1, ch)), full((STATE, ch)), full((1, ch))]
+        + [anywhere] * len(made),
         scratch_shapes=[
             pltpu.VMEM((STATE, ch), F32),
             pltpu.VMEM((ch // LANES, CHUNK, LANES), F32),
@@ -286,10 +300,11 @@
             pltpu.VMEM((g, CHUNK * 8, LANES), F32),
             pltpu.VMEM((g, CHUNK * 8, LANES), F32),
             big(), big(),
+            *room,
         ],
         compiler_params=pltpu.CompilerParams(vmem_limit_bytes=60 << 20),
         name="scan_bwd",
-    )(xs, zg, proj, since, ys, gg, hck, dtw, dtb, alog, skip, spread)
+    )(xs, zg, proj, since, ys, gg, hck, dtw, dtb, alog, skip, spread, *far)
 
 
 def rms_inverse(values):
@@ -1424,43 +1439,93 @@
              **expert_names(z, 1), **back_scratch(z)))
 
 
-def final_block(z, result, up, gnorm, layers):
+def big_outputs(z, count):
+    return dict(w_in=(count, 2, z.width, z.channels), w_out=(count, z.channels, z.width), w_up=(count, 1, z.width, z.hidden),
+                w_down=(count, 1, z.hidden, z.width))
+
+
+def widen(z, early, late, w_in, w_out):
+    at, till, ch = early_rows(z.width, z.experts), late_rows(z.width), z.channels
+    w_in[0] = late[till[0] : till[1], :].astype(F32)
+    w_in[1] = early[at[0] : at[1], :].astype(F32)
+    for i in range(z.width // ch):
+        w_out[:, i * ch : (i + 1) * ch] = early[at[1] + i * ch : at[1] + (i + 1) * ch, :].astype(F32)
+
+
+def upper_outputs(z, count, layer):
+    early, late, _, up, down = layer
+    far = [early, late, up, down]
+    shapes = big_outputs(z, count)
+    room = [pltpu.VMEM(v.shape, v.dtype) for v in far]
+    room += [pltpu.VMEM(shapes["w_in"][1:], F32), pltpu.VMEM(shapes["w_out"][1:], F32), dma(4), dma(4)]
+
+    def work(steps, there, outs, held):
+        e, l, u, v, w_in, w_out, came, went = held
+        coming = [pltpu.make_async_copy(src, dst, came.at[i]) for i, (src, dst) in enumerate(zip(there, (e, l, u, v)))]
+        out_in, out_out, out_up, out_down = outs
+        pairs = [(w_in, out_in.at[1]), (w_out, out_out.at[1]), (u, out_up.at[1, 0]), (v, out_down.at[1, 0])]
+        going = [pltpu.make_async_copy(src, dst, went.at[i]) for i, (src, dst) in enumerate(pairs)]
+
+        @pl.when(pl.program_id(0) == 0)
+        def _():
+            for copy in coming:
+                copy.start()
+
+        @pl.when(pl.program_id(0) == 1)
+        def _():
+            for copy in coming:
+                copy.wait()
+            widen(z, e, l, w_in, w_out)
+            for copy in going:
+                copy.start()
+
+        @pl.when(pl.program_id(0) == steps - 1)
+        def _():
+            for copy in going:
+                copy.wait()
+
+    return work, far, [f32(*shape) for shape in shapes.values()], room
+
+
+def final_block(z, result, up, gnorm, layers, large_ones):
     count, ch = len(layers), z.channels
+    assert count == 2
     at, till = early_rows(z.width, z.experts), late_rows(z.width)
-    far = dict(result=(z.rows, z.width), tokens=(z.rows, z.width), w_in=(count, 2, z.width, ch), w_out=(count, ch, z.width),
-               w_up=(count, 1, z.width, z.hidden), w_down=(count, 1, z.hidden, z.width))
+    far = dict(result=(z.rows, z.width), tokens=(z.rows, z.width), **big_outputs(z, count))
     near = dict(norm_in=(count, z.width), conv_w=(count, CONV, ch), conv_b=(count, ch), x_proj=(count, PROJ, ch), dt_proj=(count, DT_RANK, ch),
                 dt_bias=(count, ch), a_log=(count, STATE, ch), skip=(count, ch), norm_moe=(count, z.width), router=(count, z.experts, z.width))
     shapes = {**far, **near}
     sums = [v for layer in layers for v in layer[:2]]
-    whole = [result, up, *(v for layer in layers for v in layer[3:])]
+    whole = [*layers[0][3:], result, up]
 
     def kernel(*refs):
         small, refs = refs[: 1 + count], refs[1 + count :]
-        there, refs = refs[: len(sums) + len(whole)], refs[len(sums) + len(whole) :]
+        there, refs = refs[: len(sums) + len(whole)], refs[len(sums) + len(whole) + len(large_ones) :]
         outs, refs = refs[: len(shapes)], refs[len(shapes) :]
         held, (w_in, w_out, came, went) = refs[: len(there)], refs[len(there) :]
         out = types.SimpleNamespace(**dict(zip(shapes, outs)))
         coming = fetch(list(zip(there, held)), came)
-        places = [out.result, out.tokens] + [v.at[l, 0] for l in range(count) for v in (out.w_up, out.w_down)]
         out.norm_in[...] = small[0][...]
         going = []
+
+        def send(src, dst):
+            going.append(pltpu.make_async_copy(src, dst, went.at[len(going)]))
+            going[-1].start()
+
         for l in range(count):
             early, late, share = held[2 * l], held[2 * l + 1], small[1 + l]
             coming[2 * l].wait()
             coming[2 * l + 1].wait()
             one = slice(l, l + 1)
-            w_in[l, 0] = late[till[0] : till[1], :].astype(F32)
-            w_in[l, 1] = early[at[0] : at[1], :].astype(F32)
+            if l == 0:
+                widen(z, early, late, w_in, w_out)
+                send(w_in, out.w_in.at[0])
+                send(w_out, out.w_out.at[0])
             for i in range(z.width // ch):
                 cols = slice(i * ch, (i + 1) * ch)
-                w_out[l, :, cols] = early[at[1] + i * ch : at[1] + (i + 1) * ch, :].astype(F32)
                 rows = share[i * (z.experts + 8) : (i + 1) * (z.experts + 8), :]
                 out.router[l, :, cols] = rows[: z.experts]
                 out.norm_moe[one, cols] = rows[z.experts : z.experts + 1]
-            for src, dst in ((w_in, out.w_in), (w_out, out.w_out)):
-                going.append(pltpu.make_async_copy(src.at[l], dst.at[l], went.at[len(going)]))
-                going[-1].start()
             conv = late[till[2] : till[3], :].astype(F32)
             out.conv_w[l] = conv[:CONV]
             out.conv_b[one, :] = conv[CONV : CONV + 1]
@@ -1470,23 +1535,24 @@
             both = early[at[4] : at[5], :].astype(F32)
             out.dt_bias[one, :] = both[:1]
             out.skip[one, :] = both[1:2]
-        for i, place in enumerate(places):
+        for i, place in enumerate((out.w_up.at[0, 0], out.w_down.at[0, 0], out.result, out.tokens)):
             coming[len(sums) + i].wait()
-            going.append(pltpu.make_async_copy(held[len(sums) + i], place, went.at[len(going)]))
-            going[-1].start()
+            send(held[len(sums) + i], place)
         for copy in going:
             copy.wait()
 
+    before = 1 + count + len(sums) + len(whole)
     outputs = pl.pallas_call(
         kernel,
         out_shape=[f32(*shape) for shape in shapes.values()],
-        in_specs=vmem(1 + count) + hbm(len(sums) + len(whole)),
+        in_specs=vmem(1 + count) + hbm(len(sums) + len(whole) + len(large_ones)),
         out_specs=hbm(len(far)) + vmem(len(near)),
         scratch_shapes=[pltpu.VMEM(v.shape, v.dtype) for v in (*sums, *whole)]
-        + [pltpu.VMEM(far["w_in"], F32), pltpu.VMEM(far["w_out"], F32), dma(len(sums) + len(whole)), dma(2 * count + len(whole))],
+        + [pltpu.VMEM(far["w_in"][1:], F32), pltpu.VMEM(far["w_out"][1:], F32), dma(len(sums) + len(whole)), dma(2 + len(whole))],
+        input_output_aliases={before + i: 2 + i for i in range(len(large_ones))},
         compiler_params=pltpu.CompilerParams(vmem_limit_bytes=60 << 20),
         name="outputs",
-    )(gnorm, *(layer[2] for layer in layers), *sums, *whole)
+    )(gnorm, *(layer[2] for layer in layers), *sums, *whole, *large_ones)
     o = types.SimpleNamespace(**dict(zip(shapes, outputs)))
     return (o.result, o.tokens, o.norm_in, o.w_in, o.conv_w, o.conv_b, jnp.swapaxes(o.x_proj, 1, 2), o.dt_proj, o.dt_bias, o.a_log, o.skip, o.w_out, o.norm_moe,
             jnp.swapaxes(o.router, 1, 2), o.w_up, o.w_down)
@@ -1505,10 +1571,10 @@
     padded = (capacity + 15) // 16 * 16
     z = Sizes(lanes, peers, experts, padded, rows_here, width, channels, w_up.shape[3])
     position = lax.broadcasted_iota(jnp.int32, (z.total + HEAD, 1), 0)
-    since, first = position, 0
-    for i in range(lengths.shape[1] - 1):
-        first = first + lengths[0, i]
-        since = jnp.where(position >= first, position - first, since)
+    sequences = lengths.shape[1]
+    earlier = jnp.arange(sequences)[:, None] < jnp.arange(sequences)[None, :]
+    starts = jnp.sum(jnp.where(earlier, lengths[0][:, None], 0), axis=0)
+    since = position - jnp.max(jnp.where(position >= starts[None, :], starts[None, :], 0), axis=1, keepdims=True)
     since = jnp.where(position < z.total, since, 0)
     place = jnp.pad(routes * padded + slot_place, (0, -rows_here % LANES))
     small = types.SimpleNamespace(
@@ -1535,8 +1601,9 @@
     collected = []
     for l in reversed(range(layers)):
         act, entry, gated, ys, marks, _ = kept[l]
-        gxs, gzg, gpart, gdtw, gdtb, galog, gskip = scan_bwd(
-            l, entry.xs, entry.zgate, entry.proj, since, ys, above.ggated.reshape(z.total, channels), marks, *scan_weights)
+        gxs, gzg, gpart, gdtw, gdtb, galog, gskip, *large_ones = scan_bwd(
+            l, entry.xs, entry.zgate, entry.proj, since, ys, above.ggated.reshape(z.total, channels), marks, *scan_weights,
+            beside=upper_outputs(z, layers, collected[-1]) if l == 0 else None)
         back = dict(gpart=gpart, gxs=gxs, gzg=gzg, b_conv=entry.conv, b_xs=entry.xs, b_whole=entry.whole, b_act=act, b_gmid=above.gmid,
                     b_gwout=above.gwout, b_gshare=above.gshare, gdtw=gdtw, gdtb=gdtb, galog=galog, gskip=gskip)
         grads = (above.gup, above.gdown)
@@ -1553,7 +1620,7 @@
     collected = collected[::-1]
     at, till = early_rows(width, experts), late_rows(width)
 
-    return final_block(z, result, end.up, end.gnorm, collected)
+    return final_block(z, result, end.up, end.gnorm, collected, large_ones)
 
 
 def solution(mesh):

time: 624 us -> 613 us (0.982)
  Pallas kernels: 611 us -> 604 us
where the time goes in v5:
time: 613 us; the launch traced here: 608 us
  Pallas kernels  604 us (99%)
    pallas_call x5, Pallas kernels, launch(): pl.pallas_call(kernel, out_shape=[*prompt.values(), *late.values()], in_s...  512 us
    pallas_call x2, Pallas kernels, scan_bwd(): pl.pallas_call(kernel, grid=(steps,), out_shape=[jax.ShapeDtypeStruct((ro...  54.4 us
    pallas_call x2, Pallas kernels, scan_fwd(): pl.pallas_call(functools.partial(scan_fwd_kernel, l), grid=(steps,), out_...  27.7 us

profile of v5, /device:TPU:0, one launch (start us, length us, event | category | flops | bytes accessed | tf_op | source)
XLA Modules:
  0.0 608.4 jit_solution(8458636194729250069)
XLA Ops:
  0.6 0.7 select_reduce_fusion.1
  1.4 0.7 multiply_add_fusion
  2.1 0.1 select_reduce_fusion
  2.2 0.6 broadcast_in_dim.39.refs_0_
  2.8 0.6 fusion.1.spread_ref.refs_11_
  3.4 0.9 fusion.refs_3_.since_ref.refs_6_.refs_10_.refs_9_
  4.4 39.9 %mamba_in.1 = (bf16[80,768]{1,0:T(8,128)(2,1)}, bf16[4,192,768]{2,1,0:T(8,128)(2,1)}, f32[776,384]{1,0:T(8,128)}, f32[768,384]{1,0:T(8,128)}, f32[768,384]{1,0:T(8,128)}) custom-call(f32[2,768]{1,0:T(2,128)} %refs_6_.5, f32[2,4,384]{2,1,0:T(4,128)} %refs_7_.9, f32[2,384]{1,0:T(2,128)} %refs_8_.11, s32[776,1]{1,0:T(8,128)} %fusion.refs_3_.since_ref.refs_6_.refs_10_.refs_9_, ...), custom_call_target="tpu_custom_call" | custom-call | tf_op jit(solution)/shard_map/mamba_in/pallas_call | solution.py:759
  44.3 13.8 %scan_fwd.2 = (bf16[768,384]{1,0:T(8,128)(2,1)}, f32[768,384]{1,0:T(8,128)}, f32[6,16,384]{2,1,0:T(8,128)}) custom-call(f32[768,384]{1,0:T(8,128)} %get-tuple-element.97.xs_ref.refs_0_.refs_15_, f32[768,384]{1,0:T(8,128)} %get-tuple-element.98.zg_ref.refs_1_, bf16[80,768]{1,0:T(8,128)(2,1)} %get-tuple-element.99.proj_ref.refs_2_, ...), custom_call_target="tpu_custom_call" | custom-call | tf_op jit(solution)/shard_map/scan_fwd/pallas_call | solution.py:115
  58.1 124.7 %middle.1 = (f32[192,8]{1,0:T(8,128)}, f32[192,8]{1,0:T(8,128)}, bf16[80,768]{1,0:T(8,128)(2,1)}, f32[192,768]{1,0:T(8,128)}, bf16[4,256,192]{2,1,0:T(8,128)(2,1...) custom-call(s32[8,256]{1,0:T(8,128)} %broadcast_in_dim.39.refs_0_, ...), custom_call_target="tpu_custom_call" | custom-call | tf_op jit(solution)/shard_map/middle/pallas_call | solution.py:759
  182.8 13.8 %scan_fwd.3 = (bf16[768,384]{1,0:T(8,128)(2,1)}, f32[768,384]{1,0:T(8,128)}, f32[6,16,384]{2,1,0:T(8,128)}) custom-call(f32[768,384]{1,0:T(8,128)} %get-tuple-element.102.xs_ref.refs_0_.refs_18_, f32[768,384]{1,0:T(8,128)} %get-tuple-element.103.zg_ref.refs_1_, bf16[80,768]{1,0:T(8,128)(2,1)} %get-tuple-element.104.proj_ref.refs_2_, ...), custom_call_target="tpu_custom_call" | custom-call | tf_op jit(solution)/shard_map/scan_fwd/pallas_call | solution.py:115
  196.7 160.6 %turn.1 = (f32[16,768]{1,0:T(8,128)}, f32[192,768]{1,0:T(8,128)}, f32[192,768]{1,0:T(8,128)}, f32[768,768]{1,0:T(8,128)}, f32[768,768]{1,0:T(8,128)}, /*index=5*/f32[4,192,384]{2,1,0:T(8,128)}, bf16[384,768]{1,0:T(8,128)(2,1)}) custom-call(s32[8,256]{1,0:T(8,128)} %broadcast_in_dim.39.refs_0_, f32[2,768]{1,0:T(2,128)} %refs_12_.3, f32[2,8,768]{2,1,0:T(8,128)} %bitcast.19, ...), custom_call_target="tpu_custom_call" | custom-call | tf_op jit(solution)/shard_map/turn/pallas_call | solution.py:759
  357.3 26.9 %scan_bwd.2 = (f32[768,384]{1,0:T(8,128)}, bf16[768,384]{1,0:T(8,128)(2,1)}, f32[80,768]{1,0:T(8,128)}, f32[48,384]{1,0:T(8,128)}, f32[1,384]{1,0:T(1,128)}, /*index=5*/f32[16,384]{1,0:T(8,128)}, f32[1,384]{1,0:T(1,128)}) custom-call(f32[768,384]{1,0:T(8,128)} %get-tuple-element.102.xs_ref.refs_0_.refs_18_, f32[768,384]{1,0:T(8,128)} %get-tuple-element.103.zg_ref.refs_1_, ...), custom_call_target="tpu_custom_call" | custom-call | tf_op jit(solution)/shard_map/scan_bwd/pallas_call | solution.py:272
  384.2 131.3 %down.1 = (f32[32,384]{1,0:T(8,128)}, f32[1,768]{1,0:T(1,128)}, f32[16,768]{1,0:T(8,128)}, bf16[1664,384]{1,0:T(8,128)(2,1)}, bf16[896,384]{1,0:T(8,128)(2,1)}, ...) custom-call(f32[16,768]{1,0:T(8,128)} %get-tuple-element.106.refs_0_, ...), custom_call_target="tpu_custom_call" | custom-call | tf_op jit(solution)/shard_map/down/pallas_call | solution.py:759
  515.5 27.5 %scan_bwd.3 = (f32[768,384]{1,0:T(8,128)}, bf16[768,384]{1,0:T(8,128)(2,1)}, f32[80,768]{1,0:T(8,128)}, f32[48,384]{1,0:T(8,128)}, f32[1,384]{1,0:T(1,128)}, /*i...) custom-call(f32[768,384]{1,0:T(8,128)} %get-tuple-element.97.xs_ref., ...), custom_call_target="tpu_custom_call" | custom-call | tf_op jit(solution)/shard_map/scan_bwd/pallas_call | solution.py:272
  543.0 55.7 %mamba_in_backward.1 = (f32[32,384]{1,0:T(8,128)}, f32[2,768]{1,0:T(2,128)}, f32[192,768]{1,0:T(8,128)}, bf16[1664,384]{1,0:T(8,128)(2,1)}, bf16[896,384]{1,0:T(8,128)(2,1)}) custom-call(f32[16,768]{1,0:T(8,128)} %get-tuple-element.129.refs_0_, f32[48,384]{1,0:T(8,128)} %get-tuple-element.137.refs_1_, f32[1,384]{1,0:T(1,128)} %get-tuple-element.138.refs_2_, ...), custom_call_target="tpu_custom_call" | custom-call | tf_op jit(solution)/shard_map/mamba_in_backward/pallas_call | solution.py:759
  598.7 9.3 %outputs.1 = (f32[192,768]{1,0:T(8,128)}, f32[192,768]{1,0:T(8,128)}, f32[2,2,768,384]{3,2,1,0:T(8,128)}, f32[2,384,768]{2,1,0:T(8,128)}, f32[2,1,768,768]{3,2,1...) custom-call(f32[2,768]{1,0:T(2,128)} %get-tuple-element.149.refs_0_,, ...), custom_call_target="tpu_custom_call", output_to_operand_aliasing={{2}: (11, {}), {3}: (12, {}), {4}: (13, {}), {5}: (14, {})} | custom-call | tf_op jit(solution)/shard_map/outputs/pallas_call | solution.py:1545
  (3 shorter events, 0.0 us)

commit v6 on v5

--- a/solution.py
+++ b/solution.py
@@ -497,7 +497,7 @@
 PARTS = 3
 
 
-def line_sum(part, stage, inbox, send, recv, out, d, m, lanes, between=lambda: None):
+def line_sum(part, stage, inbox, send, recv, out, d, m, lanes, between=lambda: None, produce=lambda b: None):
     width = part.shape[1] // PARTS
 
     def copy(side, b):
@@ -526,22 +526,21 @@
 
     low = 2 * m < lanes
 
-    def both(first):
-        def run(side):
-            for b in range(PARTS):
-                step(side, b)
-
+    def either(side, b):
         @pl.when(low)
         def _():
-            run(0 if first else 1)
+            step(side, b)
 
         @pl.when(jnp.logical_not(low))
         def _():
-            run(1 if first else 0)
-
-    both(True)
+            step(1 - side, b)
+
+    for b in range(PARTS):
+        produce(b)
+        either(0, b)
     between()
-    both(False)
+    for b in range(PARTS):
+        either(1, b)
     for b in range(PARTS):
         cols = slice(b * width, (b + 1) * width)
         out[:, cols] = (part[:, cols] + inbox[0, b].astype(F32) + inbox[1, b].astype(F32)).astype(BF16)
@@ -684,8 +683,9 @@
         self.answer(three, expert)
         self.combine_away(two)
         yield
+        self.combine_away(three)
+        yield
         self.answer(self.m, expert)
-        self.combine_away(three)
         yield
         for i, value in enumerate(self.combine(self.m)):
             own_ref[i] = value
@@ -832,9 +832,12 @@
         r.part[:, pl.ds(base, CONV_ROWS)] = dot_nt(r.x_proj[l], xs.astype(BF16))
         return carry
 
-    lax.fori_loop(0, z.total // CONV_ROWS, conv_step, 0)
-    r.ship(r.xs)
-    finish = line_sum(r.part, r.sum_stage, r.sum_inbox, r.sum_send, r.sum_recv, r.proj, d, m, z.lanes)
+    chunks = z.total // CONV_ROWS // PARTS
+
+    def produce(b):
+        lax.fori_loop(b * chunks, (b + 1) * chunks, conv_step, 0)
+
+    finish = line_sum(r.part, r.sum_stage, r.sum_inbox, r.sum_send, r.sum_recv, r.proj, d, m, z.lanes, lambda: r.ship(r.xs), produce)
     gather.finish()
     finish()
 

time: 613 us -> 611 us (level)
  no operation moved by 1% of the time
where the time goes in v6:
time: 611 us; the launch traced here: 606 us
  Pallas kernels  601 us (98%)
    pallas_call x5, Pallas kernels, launch(): pl.pallas_call(kernel, out_shape=[*prompt.values(), *late.values()], in_s...  510 us
    pallas_call x2, Pallas kernels, scan_bwd(): pl.pallas_call(kernel, grid=(steps,), out_shape=[jax.ShapeDtypeStruct((ro...  54.4 us
    pallas_call x2, Pallas kernels, scan_fwd(): pl.pallas_call(functools.partial(scan_fwd_kernel, l), grid=(steps,), out_...  27.7 us

profile of v6, /device:TPU:0, one launch (start us, length us, event | category | flops | bytes accessed | tf_op | source)
XLA Modules:
  0.0 606.0 jit_solution(16449020278933356010)
XLA Ops:
  0.6 0.7 select_reduce_fusion.1
  1.4 0.7 multiply_add_fusion
  2.1 0.1 select_reduce_fusion
  2.2 0.6 broadcast_in_dim.39.refs_0_
  2.8 0.6 fusion.1.spread_ref.refs_11_
  3.4 0.9 fusion.refs_3_.since_ref.refs_6_.refs_10_.refs_9_
  4.4 39.0 %mamba_in.1 = (bf16[80,768]{1,0:T(8,128)(2,1)}, bf16[4,192,768]{2,1,0:T(8,128)(2,1)}, f32[776,384]{1,0:T(8,128)}, f32[768,384]{1,0:T(8,128)}, f32[768,384]{1,0:T(8,128)}) custom-call(f32[2,768]{1,0:T(2,128)} %refs_6_.5, f32[2,4,384]{2,1,0:T(4,128)} %refs_7_.9, f32[2,384]{1,0:T(2,128)} %refs_8_.11, s32[776,1]{1,0:T(8,128)} %fusion.refs_3_.since_ref.refs_6_.refs_10_.refs_9_, ...), custom_call_target="tpu_custom_call" | custom-call | tf_op jit(solution)/shard_map/mamba_in/pallas_call | solution.py:759
  43.4 13.8 %scan_fwd.2 = (bf16[768,384]{1,0:T(8,128)(2,1)}, f32[768,384]{1,0:T(8,128)}, f32[6,16,384]{2,1,0:T(8,128)}) custom-call(f32[768,384]{1,0:T(8,128)} %get-tuple-element.97.xs_ref.refs_0_.refs_15_, f32[768,384]{1,0:T(8,128)} %get-tuple-element.98.zg_ref.refs_1_, bf16[80,768]{1,0:T(8,128)(2,1)} %get-tuple-element.99.proj_ref.refs_2_, ...), custom_call_target="tpu_custom_call" | custom-call | tf_op jit(solution)/shard_map/scan_fwd/pallas_call | solution.py:115
  57.2 124.3 %middle.1 = (f32[192,8]{1,0:T(8,128)}, f32[192,8]{1,0:T(8,128)}, bf16[80,768]{1,0:T(8,128)(2,1)}, f32[192,768]{1,0:T(8,128)}, bf16[4,256,192]{2,1,0:T(8,128)(2,1...) custom-call(s32[8,256]{1,0:T(8,128)} %broadcast_in_dim.39.refs_0_, ...), custom_call_target="tpu_custom_call" | custom-call | tf_op jit(solution)/shard_map/middle/pallas_call | solution.py:759
  181.5 13.8 %scan_fwd.3 = (bf16[768,384]{1,0:T(8,128)(2,1)}, f32[768,384]{1,0:T(8,128)}, f32[6,16,384]{2,1,0:T(8,128)}) custom-call(f32[768,384]{1,0:T(8,128)} %get-tuple-element.102.xs_ref.refs_0_.refs_18_, f32[768,384]{1,0:T(8,128)} %get-tuple-element.103.zg_ref.refs_1_, bf16[80,768]{1,0:T(8,128)(2,1)} %get-tuple-element.104.proj_ref.refs_2_, ...), custom_call_target="tpu_custom_call" | custom-call | tf_op jit(solution)/shard_map/scan_fwd/pallas_call | solution.py:115
  195.3 160.5 %turn.1 = (f32[16,768]{1,0:T(8,128)}, f32[192,768]{1,0:T(8,128)}, f32[192,768]{1,0:T(8,128)}, f32[768,768]{1,0:T(8,128)}, f32[768,768]{1,0:T(8,128)}, /*index=5*/f32[4,192,384]{2,1,0:T(8,128)}, bf16[384,768]{1,0:T(8,128)(2,1)}) custom-call(s32[8,256]{1,0:T(8,128)} %broadcast_in_dim.39.refs_0_, f32[2,768]{1,0:T(2,128)} %refs_12_.3, f32[2,8,768]{2,1,0:T(8,128)} %bitcast.19, ...), custom_call_target="tpu_custom_call" | custom-call | tf_op jit(solution)/shard_map/turn/pallas_call | solution.py:759
  355.8 26.9 %scan_bwd.2 = (f32[768,384]{1,0:T(8,128)}, bf16[768,384]{1,0:T(8,128)(2,1)}, f32[80,768]{1,0:T(8,128)}, f32[48,384]{1,0:T(8,128)}, f32[1,384]{1,0:T(1,128)}, /*index=5*/f32[16,384]{1,0:T(8,128)}, f32[1,384]{1,0:T(1,128)}) custom-call(f32[768,384]{1,0:T(8,128)} %get-tuple-element.102.xs_ref.refs_0_.refs_18_, f32[768,384]{1,0:T(8,128)} %get-tuple-element.103.zg_ref.refs_1_, ...), custom_call_target="tpu_custom_call" | custom-call | tf_op jit(solution)/shard_map/scan_bwd/pallas_call | solution.py:272
  382.7 131.2 %down.1 = (f32[32,384]{1,0:T(8,128)}, f32[1,768]{1,0:T(1,128)}, f32[16,768]{1,0:T(8,128)}, bf16[1664,384]{1,0:T(8,128)(2,1)}, bf16[896,384]{1,0:T(8,128)(2,1)}, ...) custom-call(f32[16,768]{1,0:T(8,128)} %get-tuple-element.106.refs_0_, ...), custom_call_target="tpu_custom_call" | custom-call | tf_op jit(solution)/shard_map/down/pallas_call | solution.py:759
  514.0 27.5 %scan_bwd.3 = (f32[768,384]{1,0:T(8,128)}, bf16[768,384]{1,0:T(8,128)(2,1)}, f32[80,768]{1,0:T(8,128)}, f32[48,384]{1,0:T(8,128)}, f32[1,384]{1,0:T(1,128)}, /*i...) custom-call(f32[768,384]{1,0:T(8,128)} %get-tuple-element.97.xs_ref., ...), custom_call_target="tpu_custom_call" | custom-call | tf_op jit(solution)/shard_map/scan_bwd/pallas_call | solution.py:272
  541.5 54.8 %mamba_in_backward.1 = (f32[32,384]{1,0:T(8,128)}, f32[2,768]{1,0:T(2,128)}, f32[192,768]{1,0:T(8,128)}, bf16[1664,384]{1,0:T(8,128)(2,1)}, bf16[896,384]{1,0:T(8,128)(2,1)}) custom-call(f32[16,768]{1,0:T(8,128)} %get-tuple-element.129.refs_0_, f32[48,384]{1,0:T(8,128)} %get-tuple-element.137.refs_1_, f32[1,384]{1,0:T(1,128)} %get-tuple-element.138.refs_2_, ...), custom_call_target="tpu_custom_call" | custom-call | tf_op jit(solution)/shard_map/mamba_in_backward/pallas_call | solution.py:759
  596.3 9.3 %outputs.1 = (f32[192,768]{1,0:T(8,128)}, f32[192,768]{1,0:T(8,128)}, f32[2,2,768,384]{3,2,1,0:T(8,128)}, f32[2,384,768]{2,1,0:T(8,128)}, f32[2,1,768,768]{3,2,1...) custom-call(f32[2,768]{1,0:T(2,128)} %get-tuple-element.149.refs_0_,, ...), custom_call_target="tpu_custom_call", output_to_operand_aliasing={{2}: (11, {}), {3}: (12, {}), {4}: (13, {}), {5}: (14, {})} | custom-call | tf_op jit(solution)/shard_map/outputs/pallas_call | solution.py:1548
  (3 shorter events, 0.0 us)
